TPU v7x, 32 devices: a whole 2x2x4 slice. The times are simulated.
32 devices in a mesh: dp: 16 (over z, x, core), tensor: 2 (over y).
Axes of the slice: x: 2, y: 2, z: 4, core: 2. Of those that a mesh axis runs over, the one named last changes fastest.
Arguments:
- layer_in: bfloat16 [16, 2, 1024, 768], P(None, 'tensor', 'dp'), may hold values from -6 to 6
- out_grad: bfloat16 [16, 2, 1024, 768], P(None, 'tensor', 'dp'), may hold values from -6 to 6
- seq_lengths: int32 [16], replicated, may hold values from 1 to 2048, 20480 in all
- slot_perm: int32 [16], replicated, may hold values from 0 to 15, each once
- norm_gain: float32 [768], replicated, may hold values from 0.1 to 1.9
- w_gate: bfloat16 [768, 1536], P('dp', 'tensor'), may hold values from -0.21875 to 0.21875
- w_inner: bfloat16 [768, 1536], P('dp', 'tensor'), may hold values from -0.21875 to 0.21875
- w_bc: bfloat16 [768, 128], P('dp'), may hold values from -0.21875 to 0.21875
- w_dt: bfloat16 [768, 48], P('dp', 'tensor'), may hold values from -0.21875 to 0.21875
- conv_x: float32 [4, 1536], P(None, 'tensor'), may hold values from -3 to 3
- conv_bc: float32 [4, 128], replicated, may hold values from -2 to 2
- dt_bias: float32 [48], P('tensor'), may hold values from -4 to -2
- a_log: float32 [24], P('tensor'), may hold values from -4.5 to 0.5
- dskip: float32 [24], P('tensor'), may hold values from 1 to 3
- inner_gain: float32 [1536], P('tensor'), may hold values from 0.1 to 1.9
- w_out: bfloat16 [1536, 768], P('tensor', 'dp'), may hold values from -0.15625 to 0.15625
Outputs:
- output: bfloat16 [16, 2, 1024, 768], P(None, 'tensor', 'dp')
- input_grad: bfloat16 [16, 2, 1024, 768], P(None, 'tensor', 'dp')
- grad_norm_gain: float32 [768], replicated
- grad_w_gate: float32 [768, 1536], P('dp', 'tensor')
- grad_w_inner: float32 [768, 1536], P('dp', 'tensor')
- grad_w_bc: float32 [768, 128], P('dp')
- grad_w_dt: float32 [768, 48], P('dp', 'tensor')
- grad_conv_x: float32 [4, 1536], P(None, 'tensor')
- grad_conv_bc: float32 [4, 128], replicated
- grad_dt_bias: float32 [48], P('tensor')
- grad_a_log: float32 [24], P('tensor')
- grad_dskip: float32 [24], P('tensor')
- grad_inner_gain: float32 [1536], P('tensor')
- grad_w_out: float32 [1536, 768], P('tensor', 'dp')
Inputs may be any that keep to these rules, and one draw needn't show every extreme that they name: Sequence s is computed in slot slot_perm[s]; slot i belongs to index i of dp; out_grad, output and input_grad are indexed by slot. `seq_lengths`: some sequence has exactly 2048 valid positions.
All inputs are finite; a program needn't handle non-finite values.
Results may differ from a plain program's by a relative error of at most 0.011.
Values may be sent and summed in bfloat16 or wider, within the bound.
No kernel may reach another device: no remote copies, remote signals or barrier semaphores. Data moves between devices by JAX's collectives and lax.ppermute only.
A program may use at most 320 MiB of HBM per device.

v0:
```python
import jax
import jax.numpy as jnp
from jax import lax
from jax.sharding import PartitionSpec as P

BLOCK = 128


exact_prec = lax.Precision.HIGHEST


def causal_conv(values, kernel):
    taps_count = kernel.shape[0]
    length = values.shape[0]
    padded = jnp.pad(values, ((taps_count - 1, 0), (0, 0)))
    summed = jnp.zeros(values.shape, jnp.float32)
    for offset in range(taps_count):
        summed = summed + kernel[offset] * padded[offset : offset + length]
    return summed


def strict_scan(values, state_in, state_out, log_decay):
    length, head_count, head_width = values.shape
    blocks = length // BLOCK
    blocked = values.reshape(blocks, BLOCK, head_count, head_width)
    in_maps = state_in.reshape(blocks, BLOCK, -1)
    out_maps = state_out.reshape(blocks, BLOCK, -1)
    partial_sums = jnp.cumsum(log_decay.reshape(blocks, BLOCK, head_count), axis=1)
    scores = jnp.einsum("kin,kjn->kij", out_maps, in_maps, precision=exact_prec)
    row_ids = lax.broadcasted_iota(jnp.int32, (BLOCK, BLOCK), 0)
    col_ids = lax.broadcasted_iota(jnp.int32, (BLOCK, BLOCK), 1)
    lower = (row_ids > col_ids)[None, :, :, None]
    spread = partial_sums[:, :, None, :] - partial_sums[:, None, :, :]
    decay = jnp.where(lower, jnp.exp(jnp.where(lower, spread, 0.0)), 0.0)
    weights_in = scores[..., None] * decay
    inside = jnp.einsum("kijh,kjhp->kihp", weights_in, blocked, precision=exact_prec)
    to_end = jnp.exp(partial_sums[:, -1:, :] - partial_sums)
    block_states = jnp.einsum(
        "kjn,kjhp->khnp", in_maps, blocked * to_end[..., None], precision=exact_prec
    )
    block_decay = jnp.exp(partial_sums[:, -1, :])

    def carry_step(carried, item):
        decay_now, state_now = item
        return (carried * decay_now[:, None, None] + state_now, carried)

    start_state = jnp.zeros(block_states.shape[1:], jnp.float32)
    _, entering = lax.scan(carry_step, start_state, (block_decay, block_states))
    outside = jnp.einsum("kin,khnp->kihp", out_maps, entering, precision=exact_prec)
    outside = outside * jnp.exp(partial_sums)[..., None]
    return (inside + outside).reshape(length, head_count, head_width)


def mixer(
    inner_in, bc_raw, step_raw, gate, conv_x, conv_bc, dt_bias, a_log, dskip, inner_gain, mask
):
    length = inner_in.shape[0]
    head_count = a_log.shape[0]
    head_width = inner_in.shape[1] // head_count
    conv_out = jax.nn.silu(causal_conv(inner_in, conv_x))
    bc_conv = jax.nn.silu(causal_conv(bc_raw, conv_bc))
    state_width = bc_conv.shape[1] // 2
    state_in = bc_conv[:, :state_width]
    state_out = bc_conv[:, state_width:]
    step_size = jax.nn.softplus(step_raw + dt_bias).reshape(length, head_count, 2)
    log_decay = -step_size * jnp.exp(a_log)[None, :, None]
    heads_x = conv_out.reshape(length, head_count, head_width)
    forward_v = (mask[:, None] * step_size[:, :, 0])[:, :, None] * heads_x
    backward_v = (mask[:, None] * step_size[:, :, 1])[:, :, None] * heads_x
    forward_out = strict_scan(forward_v, state_in, state_out, log_decay[:, :, 0])
    backward_out = jnp.flip(
        strict_scan(
            jnp.flip(backward_v, 0),
            jnp.flip(state_in, 0),
            jnp.flip(state_out, 0),
            jnp.flip(log_decay[:, :, 1], 0),
        ),
        0,
    )
    mixture = forward_out + backward_out + dskip[None, :, None] * heads_x
    gated_out = mixture * jax.nn.silu(gate.reshape(length, head_count, head_width))
    scaled = gated_out * lax.rsqrt(jnp.mean(gated_out * gated_out, axis=-1, keepdims=True) + 1e-05)
    return (scaled * inner_gain.reshape(head_count, head_width)).reshape(
        length, head_count * head_width
    )


def project(left_operand, right_operand):
    return jnp.einsum(
        "web,bz->wez", left_operand, right_operand, preferred_element_type=jnp.float32
    )


def back_project(left_operand, right_operand):
    return jnp.einsum(
        "hkq,nq->hkn", left_operand, right_operand, preferred_element_type=jnp.float32
    )


def weight_grad(left_operand, right_operand):
    return jnp.einsum(
        "rno,rnm->om", left_operand, right_operand, preferred_element_type=jnp.float32
    )


def shards(
    layer_in,
    out_grad,
    seq_lengths,
    slot_perm,
    norm_gain,
    w_gate,
    w_inner,
    w_bc,
    w_dt,
    conv_x,
    conv_bc,
    dt_bias,
    a_log,
    dskip,
    inner_gain,
    w_out,
):
    dp_count = lax.axis_size("dp")
    rank_dp = lax.axis_index("dp")
    rank_tensor = lax.axis_index("tensor")
    seq_total = slot_perm.shape[0]
    seq_dev = seq_total // dp_count
    sender = jnp.argsort(slot_perm)
    placed_in = jnp.take(layer_in, sender, axis=0)
    local_in, local_grad = (
        lax.all_to_all(placed_in, "dp", split_axis=0, concat_axis=2, tiled=True),
        lax.all_to_all(out_grad, "dp", split_axis=0, concat_axis=2, tiled=True),
    )
    rows_half = local_in[:, 0].astype(jnp.float32)
    cot_half = local_grad[:, 0].astype(jnp.float32)
    half_len = rows_half.shape[1]
    full_len = half_len * lax.axis_size("tensor")
    mine = lax.dynamic_slice_in_dim(sender, rank_dp * seq_dev, seq_dev)
    my_lengths = jnp.take(seq_lengths, mine)
    positions = jnp.arange(full_len, dtype=jnp.int32)
    mask_full = (positions[None, :] < my_lengths[:, None]).astype(jnp.float32)
    mask_half = lax.dynamic_slice_in_dim(mask_full, rank_tensor * half_len, half_len, 1)
    inv_rms = lax.rsqrt(jnp.mean(rows_half * rows_half, axis=-1, keepdims=True) + 1e-05)
    unit_rows = rows_half * inv_rms
    normed_half = (unit_rows * norm_gain).astype(jnp.bfloat16)
    normed = lax.all_gather(normed_half, "tensor", axis=1, tiled=True)
    gate_w, inner_w, bc_w, dt_w, output_weight = (
        lax.all_gather(w_gate, "dp", axis=0, tiled=True),
        lax.all_gather(w_inner, "dp", axis=0, tiled=True),
        lax.all_gather(w_bc, "dp", axis=0, tiled=True),
        lax.all_gather(w_dt, "dp", axis=0, tiled=True),
        lax.all_gather(w_out, "dp", axis=1, tiled=True),
    )
    gate = project(normed, gate_w)
    inner_in = project(normed, inner_w)
    bc_raw = project(normed, bc_w)
    step_raw = project(normed, dt_w)

    def local_mixer(
        inner_val,
        bc_val,
        step_val,
        gate_val,
        convx_val,
        convbc_val,
        bias_val,
        alog_val,
        skip_val,
        gain_val,
    ):
        return jax.vmap(mixer, in_axes=(0, 0, 0, 0, None, None, None, None, None, None, 0))(
            inner_val,
            bc_val,
            step_val,
            gate_val,
            convx_val,
            convbc_val,
            bias_val,
            alog_val,
            skip_val,
            gain_val,
            mask_full,
        )

    mixed_out, pull_mixer = jax.vjp(
        local_mixer,
        inner_in,
        bc_raw,
        step_raw,
        gate,
        conv_x,
        conv_bc,
        dt_bias,
        a_log,
        dskip,
        inner_gain,
    )
    mixed_reduced = mixed_out.astype(jnp.bfloat16)
    cot_masked = (cot_half * mask_half[..., None]).astype(jnp.bfloat16)
    cotangent_whole = lax.all_gather(cot_masked, "tensor", axis=1, tiled=True)
    partial_row_block = jnp.einsum(
        "mtu,ur->mtr", mixed_reduced, output_weight, preferred_element_type=jnp.float32
    )
    mixed_half = lax.psum_scatter(partial_row_block, "tensor", scatter_dimension=1, tiled=True)
    gradient_whole = jnp.einsum(
        "mbn,pn->mbp", cotangent_whole, output_weight, preferred_element_type=jnp.float32
    )
    grad_mixed = lax.optimization_barrier(gradient_whole.astype(jnp.bfloat16)).astype(jnp.float32)
    output_local = jnp.einsum(
        "thw,thz->wz", mixed_reduced, cotangent_whole, preferred_element_type=jnp.float32
    )
    (
        grad_inner,
        grad_bc_part,
        grad_step,
        grad_gate,
        grad_convx,
        grad_convbc,
        grad_bias,
        grad_alog,
        grad_skip,
        grad_gain,
    ) = pull_mixer(grad_mixed)
    gate_low = grad_gate.astype(jnp.bfloat16)
    inner_low = grad_inner.astype(jnp.bfloat16)
    step_low = grad_step.astype(jnp.bfloat16)
    normed_part = back_project(gate_low, gate_w) + back_project(inner_low, inner_w)
    normed_part = normed_part + back_project(step_low, dt_w)
    normed_grad, bc_grad = (
        lax.psum_scatter(normed_part, "tensor", scatter_dimension=1, tiled=True),
        lax.psum_scatter(grad_bc_part, "tensor", scatter_dimension=1, tiled=True),
    )
    bc_low = bc_grad.astype(jnp.bfloat16)
    normed_grad = normed_grad + back_project(bc_low, bc_w)
    gate_wgrad = weight_grad(normed, gate_low)
    inner_wgrad = weight_grad(normed, inner_low)
    step_wgrad = weight_grad(normed, step_low)
    bc_wgrad = weight_grad(normed_half, bc_low)
    scaled_grad = normed_grad * norm_gain
    norm_part = jnp.sum(normed_grad * unit_rows, axis=(0, 1))
    rows_grad = cot_half + inv_rms * (
        scaled_grad - unit_rows * jnp.mean(scaled_grad * unit_rows, axis=-1, keepdims=True)
    )
    gate_sum, inner_sum, step_sum, out_sum = (
        lax.psum_scatter(gate_wgrad, "dp", scatter_dimension=0, tiled=True),
        lax.psum_scatter(inner_wgrad, "dp", scatter_dimension=0, tiled=True),
        lax.psum_scatter(step_wgrad, "dp", scatter_dimension=0, tiled=True),
        lax.psum_scatter(output_local, "dp", scatter_dimension=1, tiled=True),
    )
    bc_all, norm_all, convbc_all = lax.psum((bc_wgrad, norm_part, grad_convbc), ("dp", "tensor"))
    bc_rows = w_bc.shape[0]
    bc_sum = lax.dynamic_slice_in_dim(bc_all, rank_dp * bc_rows, bc_rows, 0)
    convx_sum, bias_sum, alog_sum, skip_sum, gain_sum = lax.psum(
        (grad_convx, grad_bias, grad_alog, grad_skip, grad_gain), "dp"
    )
    out_half = rows_half + mask_half[..., None] * mixed_half
    output, input_grad = (
        lax.all_to_all(
            out_half.astype(jnp.bfloat16)[:, None], "dp", split_axis=2, concat_axis=0, tiled=True
        ),
        lax.all_to_all(
            rows_grad.astype(jnp.bfloat16)[:, None], "dp", split_axis=2, concat_axis=0, tiled=True
        ),
    )
    return (
        output,
        input_grad,
        norm_all,
        gate_sum,
        inner_sum,
        bc_sum,
        step_sum,
        convx_sum,
        convbc_all,
        bias_sum,
        alog_sum,
        skip_sum,
        gain_sum,
        out_sum,
    )


def solution(mesh):
    return jax.shard_map(
        shards,
        mesh=mesh,
        in_specs=(
            P(None, "tensor", "dp", None),
            P(None, "tensor", "dp", None),
            P(),
            P(),
            P(),
            P("dp", "tensor"),
            P("dp", "tensor"),
            P("dp", None),
            P("dp", "tensor"),
            P(None, "tensor"),
            P(),
            P("tensor"),
            P("tensor"),
            P("tensor"),
            P("tensor"),
            P("tensor", "dp"),
        ),
        out_specs=(
            P(None, "tensor", "dp", None),
            P(None, "tensor", "dp", None),
            P(),
            P("dp", "tensor"),
            P("dp", "tensor"),
            P("dp", None),
            P("dp", "tensor"),
            P(None, "tensor"),
            P(),
            P("tensor"),
            P("tensor"),
            P("tensor"),
            P("tensor"),
            P("tensor", "dp"),
        ),
        check_vma=False,
    )
```

profile of v0, /device:TPU:9, one launch (start us, length us, event | category | flops | bytes accessed | tf_op | source)
XLA Modules:
  0.0 1659.0 jit_solution(1774268298412946500)
XLA Ops:
  10.7 43.0 %all_to_all.42 = bf16[16,1,64,768]{3,2,1,0:T(8,128)(2,1)S(1)} all-to-all(bf16[16,1,64,768]{3,2,1,0:T(8,128)(2,1)S(1)} %bitcast_select_fusion), channel_id=1, replica_groups=mesh['dp'=16,'tensor'=2] {'dp'}, dimensions={0} | all-to-all | bytes 3145728 | tf_op jit(solution)/shard_map/all_to_all | solution.py:132
  66.7 43.0 %all-gather = bf16[16,48,24]{1,2,0:T(8,128)(2,1)S(1)} all-gather(bf16[1,48,24]{1,2,0:T(8,128)(2,1)} %bitcast.685), channel_id=1, replica_groups=mesh['dp'=16,'tensor'=2] {'dp'}, dimensions={0}, use_global_device_ids=true | all-gather | bytes 39168 | tf_op jit(solution)/shard_map/all_gather | solution.py:152
  113.1 18.8 %all_gather.24 = bf16[768,128]{1,0:T(8,128)(2,1)} all-gather(bf16[48,128]{1,0:T(8,128)(2,1)S(1)} %copy-done.93), channel_id=1, replica_groups=mesh['dp'=16,'tensor'=2] {'dp'}, dimensions={0}, use_global_device_ids=true | all-gather | bytes 208896 | tf_op jit(solution)/shard_map/all_gather | solution.py:151
  200.0 9.5 fusion.111
  212.9 34.2 %while.69 = (s32[]{:T(128)}, f32[1,12,64,64]{3,2,1,0:T(8,128)S(1)}, f32[16,1,12,64,64]{4,3,2,1,0:T(8,128)}, f32[16,1,12,1,1]{2,4,3,1,0:T(1,128)S(1)}, f32[16,1,1...) while((s32[]{:T(128)}, f32[1,12,64,64]{3,2,1,0:T(8,128)S(1)}, ...), condition=%wide.region_4.5_spmd.clone, body=%wide.region_3.4_spmd.clone.sunk | while | flops 196611 | bytes 1967868 | solution.py:48
  258.9 9.2 fusion.216
  279.8 12.3 rev.36
  302.7 9.4 fusion.114
  315.5 54.7 %while.70 = (s32[]{:T(128)}, f32[1,12,64,64]{3,2,1,0:T(8,128)S(1)}, f32[16,1,12,64,64]{4,3,2,1,0:T(8,128)}, f32[16,1,12,1,1]{2,4,3,1,0:T(1,128)S(1)}, f32[16,1,1...) while((s32[]{:T(128)}, f32[1,12,64,64]{3,2,1,0:T(8,128)S(1)}, ...), condition=%wide.region_7.8_spmd.clone, body=%wide.region_6.7_spmd.clone.sunk | while | flops 196611 | bytes 1967404 | solution.py:48
  376.8 9.2 fusion.218
  391.0 30.4 %bitcast_add_fusion.6 = f32[1,16,128,12,64]{2,4,3,1,0:T(8,128)} fusion(f32[16,128,12,64]{1,3,2,0:T(8,128)} %bitcast.637, f32[16,128,12]{1,2,0:T(8,128)S(1)} %copy.646, f32[16,128,12]{1,2,0:T(8,128)S(1)} %copy.636, f32[16,128,128]{2,1,0:T(8,128)} %fusion.217, pred[128,128]{1,0:T(8,128)(4,1)S(1)} %copy-done.91, f32[16,128,12,64]{1,0,3,2:T(8,128)} %bitcast.604), kind=kOutput, calls=%fused_computation.67 | convolution fusion | flops 2431647744 | bytes 20135936 | tf_op jit(solution)/shard_map/jvp(vmap(kijh,kjhp->kihp))/dot_general | solution.py:36
  421.4 29.2 %bitcast_add_fusion.7 = f32[1,16,128,12,64]{2,4,3,1,0:T(8,128)} fusion(f32[16,128,12,64]{1,3,2,0:T(8,128)S(1)} %bitcast.635, f32[16,128,12]{1,2,0:T(8,128)S(1)} %copy.628, f32[16,128,12]{1,2,0:T(8,128)S(1)} %copy.618, f32[16,128,128]{2,1,0:T(8,128)S(1)} %copy-done.46, pred[128,128]{1,0:T(8,128)(4,1)S(1)} %copy-done.91, ...), kind=kOutput, calls=%fused_computation.68 | convolution fusion | flops 2431647744 | bytes 20135936 | tf_op jit(solution)/shard_map/jvp(vmap(kijh,kjhp->kihp))/dot_general | solution.py:36
  451.3 16.1 copy.672
  468.8 9.8 copy.629
  491.6 12.1 rev.40
  508.9 13.8 multiply_reduce_fusion.11
  542.9 12.9 fusion.144
  555.8 12.5 rev.41
  576.7 9.5 fusion.110
  589.6 51.8 %while.71 = (s32[]{:T(128)}, f32[1,12,64,64]{3,2,1,0:T(8,128)S(1)}, f32[16,1,12]{2,1,0:T(1,128)S(1)}, f32[16,1,12,64,64]{4,3,2,1,0:T(8,128)}, f32[16,1,12,64,64]...) while((s32[]{:T(128)}, f32[1,12,64,64]{3,2,1,0:T(8,128)S(1)}, ...), condition=%wide.region_13.14_spmd.clone, body=%wide.region_11.13_spmd.clone.sunk | while | flops 294904 | bytes 2164048 | solution.py:48
  641.4 15.9 fusion.37
  667.9 9.6 fusion.109
  681.1 61.6 %while.72 = (s32[]{:T(128)}, f32[1,12,64,64]{3,2,1,0:T(8,128)S(1)}, f32[16,1,12]{2,1,0:T(1,128)S(1)}, f32[16,1,12,64,64]{4,3,2,1,0:T(8,128)}, f32[16,1,12,64,64]...) while((s32[]{:T(128)}, f32[1,12,64,64]{3,2,1,0:T(8,128)S(1)}, ...), condition=%wide.region_16.17_spmd.clone, body=%wide.region_14.16_spmd.clone.sunk | while | flops 294904 | bytes 2164048 | solution.py:48
  742.7 12.4 fusion.30
  755.2 27.0 %fusion.62 = f32[16,12,128,128]{3,2,1,0:T(8,128)} fusion(f32[16,12,64,128]{3,0,2,1:T(8,128)S(1)} %bitcast.583, f32[16,128,12,64]{1,0,3,2:T(8,128)} %get-tuple-element.851), kind=kOutput, calls=%fused_computation.126 | convolution fusion | flops 2415919104 | bytes 25165824 | tf_op jit(solution)/shard_map/transpose(jvp(vmap(kijh,kjhp->kihp)))/dot_general | solution.py:36
  782.2 19.3 %fusion.36 = (f32[16,128,12]{1,2,0:T(8,128)S(1)}, f32[16,128,12]{1,2,0:T(8,128)}, f32[1,16,128,12,64]{2,4,3,1,0:T(8,128)}) fusion(f32[16,12,64,128]{3,2,1,0:T(8,128)S(1)} %fusion.30, f32[1,16,128,12,64]{2,1,0,4,3:T(8,128)S(1)} %bitcast.656, f32[16,128,12]{1,2,0:T(8,128)S(1)} %copy-done.63, f32[16,128,12]{1,2,0:T(8,128)S(1)} %copy-done.58, ...), kind=kOutput, calls=%fused_computation.79 | convolution fusion | flops 2439462912 | bytes 26722304 | tf_op jit(solution)/shard_map/transpose(jvp(vmap(kijh,kjhp->kihp)))/dot_general | solution.py:36
  803.7 13.6 fusion.130
  817.3 13.7 fusion.131
  831.0 10.6 fusion.137
  841.7 8.2 fusion.132
  849.9 10.0 copy.668
  860.0 17.6 %bitcast_add_fusion.5 = f32[1,16,128,12,64]{2,4,3,1,0:T(8,128)S(1)} fusion(f32[16,12,64,128]{3,2,1,0:T(8,128)} %get-tuple-element.904, f32[16,128,12]{1,2,0:T(8,128)S(1)} %copy-done.62, f32[16,128,12]{1,2,0:T(8,128)S(1)} %copy-done.61, f32[16,128,128]{2,1,0:T(8,128)S(1)} %copy-done.48, pred[128,128]{1,0:T(8,128)(4,1)S(1)} %copy-done.92, ...), kind=kOutput, calls=%fused_computation.66 | convolution fusion | flops 2431647744 | bytes 20135936 | tf_op jit(solution)/shard_map/transpose(jvp(vmap(kijh,kjhp->kihp)))/dot_general | solution.py:36
  887.6 12.1 rev.42
  899.7 13.4 multiply_reduce_fusion.1
  921.3 42.1 %fusion.19 = (f32[16,128,12]{1,2,0:T(8,128)}, f32[16,128,12]{1,2,0:T(8,128)}, f32[16,128,128]{2,1,0:T(8,128)}, f32[16,128,128]{2,1,0:T(8,128)}, f32[16,128,12]{1,2,0:T(8,128)}, /*index=5*/f32[16,128,12]{1,2,0:T(8,128)}) fusion(f32[16,128,12]{1,2,0:T(8,128)S(1)} %copy-done.61, f32[16,128,128]{2,1,0:T(8,128)} %fusion.217, ...), kind=kOutput, calls=%fused_computation.53 | convolution fusion | flops 2484502528 | bytes 29966336 | tf_op jit(solution)/shard_map/transpose(jvp(vmap(kijh,kjhp->kihp)))/dot_general | solution.py:36
  981.0 8.3 rev.43
  1046.1 14.8 multiply_reduce_fusion.4
  1114.0 45.1 %reduce-scatter.12.cloned.1.call-done = f32[1,1024,768]{2,1,0:T(8,128)} async-done(((f32[1,2048,768]{2,1,0:T(8,128)}), f32[1,1024,768]{2,1,0:T(8,128)}) %reduce-scatter.12.cloned.1.call-update) | async-done | bytes 3145744 | tf_op jit(solution)/shard_map/reduce_scatter | solution.py:231
  1164.6 73.9 %reduce-scatter.10.cloned.1.call-done = f32[1,1024,768]{2,1,0:T(8,128)} async-done(((f32[1,2048,768]{2,1,0:T(8,128)}), f32[1,1024,768]{2,1,0:T(8,128)}) %reduce-scatter.10.cloned.1.call-update) | async-done | bytes 3145744 | tf_op jit(solution)/shard_map/reduce_scatter | solution.py:205
  1248.7 11.3 reduce.61
  1279.1 11.5 reduce.60
  1292.0 13.0 all-to-all-done.3
  1310.8 73.8 %all-reduce.29 = (f32[4,768]{1,0:T(4,128)}, f32[24]{0:T(128)}, f32[12]{0:T(128)}, f32[12]{0:T(128)}, f32[768]{0:T(1024)}) all-reduce(f32[4,768]{1,0:T(4,128)S(1)} %pad_add_fusion.7, f32[24]{0:T(128)S(1)} %get-tuple-element.843, f32[12]{0:T(128)S(1)} %exponential_multiply_fusion, ...), channel_id=1, replica_groups=mesh['dp'=16,'tensor'=2] {'dp'}, use_global_device_ids=true, to_apply=%region_46.47 | all-reduce | flops 3888 | bytes 31104 | tf_op jit(solution)/shard_map/psum | solution.py:254
  1386.1 65.8 %all-reduce.32.cloned.1.call-done = f32[768,128]{1,0:T(8,128)} async-done(((f32[768,128]{1,0:T(8,128)}), f32[768,128]{1,0:T(8,128)}) %all-reduce.32.cloned.1.call-update) | async-done | bytes 393232 | tf_op jit(solution)/shard_map/psum | solution.py:251
  1453.3 41.7 %all-reduce.28 = (f32[768]{0:T(1024)}, f32[4,128]{1,0:T(4,128)}) all-reduce(f32[768]{0:T(1024)S(1)} %get-tuple-element.766, f32[4,128]{1,0:T(4,128)S(1)} %pad_add_fusion.8), channel_id=1, replica_groups=mesh['dp'=16,'tensor'=2] {'dp','tensor'}, use_global_device_ids=true, to_apply=%region_37.38 | all-reduce | flops 1280 | bytes 10240 | tf_op jit(solution)/shard_map/psum | solution.py:251
  1504.7 10.0 reshape.1526
  1519.3 66.2 %reduce-scatter.16.cloned.1.call-done = f32[48,768]{1,0:T(8,128)} async-done(((f32[768,768]{1,0:T(8,128)}), f32[48,768]{1,0:T(8,128)}) %reduce-scatter.16.cloned.1.call-update) | async-done | bytes 147472 | tf_op jit(solution)/shard_map/reduce_scatter | solution.py:246
  1585.5 66.8 %reduce-scatter.20.cloned.1.call-done = f32[768,48]{0,1:T(8,128)} async-done(((f32[768,768]{0,1:T(8,128)}), f32[768,48]{0,1:T(8,128)}) %reduce-scatter.20.cloned.1.call-update) | async-done | bytes 147472 | tf_op jit(solution)/shard_map/reduce_scatter | solution.py:249
  (841 shorter events, 610.1 us)
Async XLA Ops:
  7.2 47.0 %copy-start.74 = (f32[768]{0:T(1024)S(1)}, f32[768]{0:T(1024)}, u32[]{:S(2)}) copy-start(f32[768]{0:T(1024)} %param.28) | copy-start | bytes 9220
  7.2 130.5 %all-gather.7.cloned.1.call-start = ((), (), s32[]{:S(2)}) async-start(), calls=%async_computation.11 | async-start | bytes 4718592 | tf_op jit(solution)/shard_map/all_gather | solution.py:147
  53.7 56.8 %copy-start.103 = (f32[768]{0:T(1024)S(1)}, f32[768]{0:T(1024)}, u32[]{:S(2)}) copy-start(f32[768]{0:T(1024)} %param.38) | copy-start | bytes 9220
  53.7 59.4 %copy-start.93 = (bf16[48,128]{1,0:T(8,128)(2,1)S(1)}, bf16[48,128]{1,0:T(8,128)(2,1)}, u32[]{:S(2)}) copy-start(bf16[48,128]{1,0:T(8,128)(2,1)} %param.31) | copy-start | bytes 36868
  56.8 100.4 %all-gather.9.cloned.1.call-start = ((), (), s32[]{:S(2)}) async-start(), calls=%async_computation.12 | async-start | bytes 1253376 | tf_op jit(solution)/shard_map/all_gather | solution.py:150
  57.5 446.2 %all-gather.11.cloned.1.call-start = ((), (), s32[]{:S(2)}) async-start(), calls=%async_computation.13 | async-start | bytes 1253376 | tf_op jit(solution)/shard_map/all_gather | solution.py:149
  58.3 77.2 %all-to-all-start.2 = ((bf16[16,1,64,768]{3,2,1,0:T(8,128)(2,1)}), bf16[16,1,64,768]{3,2,1,0:T(8,128)(2,1)S(1)}, u32[]{:S(2)}, u32[]{:S(2)}) async-start(bf16[16,1,64,768]{3,2,1,0:T(8,128)(2,1)} %param.25), calls=%async_computation.3 | async-start | bytes 3145728 | tf_op jit(solution)/shard_map/all_to_all | solution.py:133
  62.8 459.9 %all-gather.13.cloned.1.call-start = ((), (), s32[]{:S(2)}) async-start(), calls=%async_computation.14 | async-start | bytes 1253376 | tf_op jit(solution)/shard_map/all_gather | solution.py:153
  63.3 459.4 %all-gather.15.cloned.1.call-start = ((), (), s32[]{:S(2)}) async-start(), calls=%async_computation.16 | async-start | bytes 4718592 | tf_op jit(solution)/shard_map/all_gather | solution.py:201
  109.8 31.4 %copy-start.55 = (bf16[768,24]{0,1:T(8,128)(2,1)}, bf16[768,24]{0,1:T(8,128)(2,1)S(1)}, u32[]{:S(2)}) copy-start(bf16[768,24]{0,1:T(8,128)(2,1)S(1)} %reshape.1504) | copy-start | bytes 110596
  110.5 31.7 %copy-start.105 = (f32[12]{0:T(128)}, f32[12]{0:T(128)S(1)}, u32[]{:S(2)}) copy-start(f32[12]{0:T(128)S(1)} %exp.196) | copy-start | bytes 148
  137.1 959.7 %reduce-scatter.14.cloned.1.call-start = ((), (), s32[]{:S(2)}) async-start(), calls=%async_computation.18 | async-start | bytes 1572864 | tf_op jit(solution)/shard_map/reduce_scatter | solution.py:232
  145.8 36.7 %copy-start.67 = (f32[16,12]{1,0:T(8,128)}, f32[16,12]{1,0:T(8,128)S(1)}, u32[]{:S(2)}) copy-start(f32[16,12]{1,0:T(8,128)S(1)} %get-tuple-element.876) | copy-start | bytes 2308
  155.9 143.2 %copy-start.69 = (f32[16,12]{1,0:T(8,128)}, f32[16,12]{1,0:T(8,128)S(1)}, u32[]{:S(2)}) copy-start(f32[16,12]{1,0:T(8,128)S(1)} %get-tuple-element.878) | copy-start | bytes 2308
  157.1 116.0 %copy-start.42 = (f32[2048,12]{0,1:T(8,128)}, f32[2048,12]{0,1:T(8,128)S(1)}, u32[]{:S(2)}) copy-start(f32[2048,12]{0,1:T(8,128)S(1)} %get-tuple-element.883) | copy-start | bytes 294916
  188.4 79.7 %copy-start.9 = (f32[1,2048,64]{2,1,0:T(8,128)}, f32[1,2048,64]{2,1,0:T(8,128)S(1)}, u32[]{:S(2)}) copy-start(f32[1,2048,64]{2,1,0:T(8,128)S(1)} %get-tuple-element.880) | copy-start | bytes 1572868
  273.0 148.4 %copy-start.57 = (f32[16,128,12]{1,2,0:T(8,128)}, f32[16,128,12]{1,2,0:T(8,128)S(1)}, u32[]{:S(2)}) copy-start(f32[16,128,12]{1,2,0:T(8,128)S(1)} %copy.618) | copy-start | bytes 294916
  389.3 187.4 %copy-start.40 = (f32[16,128,12]{1,2,0:T(8,128)}, f32[16,128,12]{1,2,0:T(8,128)S(1)}, u32[]{:S(2)}) copy-start(f32[16,128,12]{1,2,0:T(8,128)S(1)} %copy.646) | copy-start | bytes 294916
  391.0 30.4 %copy-start.60 = (f32[16,128,12]{1,2,0:T(8,128)}, f32[16,128,12]{1,2,0:T(8,128)S(1)}, u32[]{:S(2)}) copy-start(f32[16,128,12]{1,2,0:T(8,128)S(1)} %copy.636) | copy-start | bytes 294916
  391.0 30.4 %copy-start.22 = (f32[16,128,768]{1,2,0:S(1)}, f32[16,128,768]{1,2,0}, u32[]{:S(2)}) copy-start(f32[16,128,768]{1,2,0} %fusion.216) | copy-start | bytes 18874372
  391.0 30.4 %copy-start.46 = (f32[16,128,128]{2,1,0:T(8,128)S(1)}, f32[16,128,128]{2,1,0:T(8,128)}, u32[]{:S(2)}) copy-start(f32[16,128,128]{2,1,0:T(8,128)} %fusion.215) | copy-start | bytes 3145732
  681.1 61.6 %copy-start.10 = (f32[1,2048,64]{2,1,0:T(8,128)S(1)}, f32[1,2048,64]{2,1,0:T(8,128)}, u32[]{:S(2)}) copy-start(f32[1,2048,64]{2,1,0:T(8,128)} %copy-done.9) | copy-start | bytes 1572868
  742.7 39.5 %slice-start.6 = ((s8[6291456]{0:T(1024)(128)(4,1)}), s8[4194304]{0:T(1024)(128)(4,1)S(1)}, s32[]{:S(2)}) async-start(s8[6291456]{0:T(1024)(128)(4,1)} %bitcast.654), calls=%async_computation.30 | async-start | bytes 8388608
  803.7 37.9 %slice-start.2 = ((s8[6291456]{0:T(1024)(128)(4,1)}), s8[4194304]{0:T(1024)(128)(4,1)S(1)}, s32[]{:S(2)}) async-start(s8[6291456]{0:T(1024)(128)(4,1)} %bitcast.599), calls=%async_computation.26 | async-start | bytes 8388608
  803.7 37.9 %slice-start.4 = ((s8[6291456]{0:T(1024)(128)(4,1)}), s8[4194304]{0:T(1024)(128)(4,1)S(1)}, s32[]{:S(2)}) async-start(s8[6291456]{0:T(1024)(128)(4,1)} %bitcast.607), calls=%async_computation.28 | async-start | bytes 8388608
  831.0 28.9 %slice-start = ((s8[6291456]{0:T(1024)(128)(4,1)}), s8[4194304]{0:T(1024)(128)(4,1)S(1)}, s32[]{:S(2)}) async-start(s8[6291456]{0:T(1024)(128)(4,1)} %bitcast.595), calls=%async_computation.24 | async-start | bytes 8388608
  921.3 46.8 %copy-start.51 = (f32[16,128,12]{1,2,0:T(8,128)S(1)}, f32[16,128,12]{1,2,0:T(8,128)}, u32[]{:S(2)}) copy-start(f32[16,128,12]{1,2,0:T(8,128)} %multiply_reduce_fusion.7) | copy-start | bytes 294916
  921.3 49.7 %copy-start.70 = (f32[16,12]{1,0:T(8,128)S(1)}, f32[16,12]{1,0:T(8,128)}, u32[]{:S(2)}) copy-start(f32[16,12]{1,0:T(8,128)} %copy-done.69) | copy-start | bytes 2308
  965.7 28.3 %copy-start.52 = (f32[16,128,12]{1,2,0:T(8,128)S(1)}, f32[16,128,12]{1,2,0:T(8,128)}, u32[]{:S(2)}) copy-start(f32[16,128,12]{1,2,0:T(8,128)} %multiply_reduce_fusion.6) | copy-start | bytes 294916
  977.1 28.4 %copy-start.66 = (f32[2048]{0:T(1024)S(1)}, f32[2048]{0:T(1024)}, u32[]{:S(2)}) copy-start(f32[2048]{0:T(1024)} %copy-done.65) | copy-start | bytes 24580
  1046.0 113.1 %reduce-scatter.12.cloned.1.call-start = ((), (), s32[]{:S(2)}) async-start(), calls=%async_computation.17 | async-start | bytes 9437184 | tf_op jit(solution)/shard_map/reduce_scatter | solution.py:231
  1082.6 155.9 %reduce-scatter.10.cloned.1.call-start = ((), (), s32[]{:S(2)}) async-start(), calls=%async_computation.15 | async-start | bytes 9437184 | tf_op jit(solution)/shard_map/reduce_scatter | solution.py:205
  1091.2 293.5 %reduce-scatter.22.cloned.1.call-start = ((), (), s32[]{:S(2)}) async-start(), calls=%async_computation.23 | async-start | bytes 417792
  1096.7 355.2 %all-reduce.32.cloned.1.call-start = ((), (), s32[]{:S(2)}) async-start(), calls=%async_computation.21 | async-start | bytes 786432 | tf_op jit(solution)/shard_map/psum | solution.py:251
  1099.2 420.1 %reduce-scatter.18.cloned.1.call-start = ((), (), s32[]{:S(2)}) async-start(), calls=%async_computation.20 | async-start | bytes 2506752 | tf_op jit(solution)/shard_map/reduce_scatter | solution.py:247
  1106.5 52.6 %copy-start.34 = (f32[1,1024,128]{2,1,0:T(8,128)S(1)}, f32[1,1024,128]{2,1,0:T(8,128)}, u32[]{:S(2)}) copy-start(f32[1,1024,128]{2,1,0:T(8,128)} %reduce-scatter.14.cloned.1.call-done) | copy-start | bytes 1572868
  1106.5 52.6 %copy-start.36 = (bf16[768,128]{1,0:T(8,128)(2,1)S(1)}, bf16[768,128]{1,0:T(8,128)(2,1)}, u32[]{:S(2)}) copy-start(bf16[768,128]{1,0:T(8,128)(2,1)} %all_gather.24) | copy-start | bytes 589828
  1106.6 52.6 %copy-start.77 = (f32[1024]{0:T(1024)S(1)}, f32[1024]{0:T(1024)}, u32[]{:S(2)}) copy-start(f32[1024]{0:T(1024)} %copy-done.76) | copy-start | bytes 12292
  1106.6 478.9 %reduce-scatter.16.cloned.1.call-start = ((), (), s32[]{:S(2)}) async-start(), calls=%async_computation.19 | async-start | bytes 2506752 | tf_op jit(solution)/shard_map/reduce_scatter | solution.py:246
  1114.0 124.6 %copy-start.30 = (bf16[16,1,64,768]{3,2,1,0:T(8,128)(2,1)S(1)}, bf16[16,1,64,768]{3,2,1,0:T(8,128)(2,1)}, u32[]{:S(2)}) copy-start(bf16[16,1,64,768]{3,2,1,0:T(8,128)(2,1)} %copy-done.29) | copy-start | bytes 4718596
  1114.0 124.6 %copy-start.79 = (f32[1,1024]{1,0:T(1,128)S(1)}, f32[1,1024]{1,0:T(1,128)}, u32[]{:S(2)}) copy-start(f32[1,1024]{1,0:T(1,128)} %copy-done.78) | copy-start | bytes 12292
  1261.3 43.6 %all-to-all-start.3 = ((bf16[16,2,24576]{2,1,0:T(2,128)(2,1)}), bf16[16,2,24576]{2,1,0:T(2,128)(2,1)S(1)}, u32[]{:S(2)}, u32[]{:S(2)}) async-start(bf16[16,2,24576]{2,1,0:T(2,128)(2,1)} %reshape.1527), calls=%async_computation.6 | async-start | bytes 3145728 | tf_op jit(solution)/shard_map/all_to_all | solution.py:262
  1267.7 384.6 %reduce-scatter.20.cloned.1.call-start = ((), (), s32[]{:S(2)}) async-start(), calls=%async_computation.22 | async-start | bytes 2506752 | tf_op jit(solution)/shard_map/reduce_scatter | solution.py:249
  1279.1 31.6 %copy-start.88 = (f32[12,64]{1,0:T(8,128)S(1)}, f32[12,64]{1,0:T(8,128)}, u32[]{:S(2)}) copy-start(f32[12,64]{1,0:T(8,128)} %get-tuple-element.761) | copy-start | bytes 9220
  1279.1 31.7 %copy-start.111 = (f32[12]{0:T(128)S(1)}, f32[12]{0:T(128)}, u32[]{:S(2)}) copy-start(f32[12]{0:T(128)} %param.36) | copy-start | bytes 148
  1279.1 31.7 %copy-start.107 = (f32[12]{0:T(128)S(1)}, f32[12]{0:T(128)}, u32[]{:S(2)}) copy-start(f32[12]{0:T(128)} %get-tuple-element.768) | copy-start | bytes 148
  1305.0 199.7 %all-to-all-start.1 = ((bf16[16,2,24576]{2,1,0:T(2,128)(2,1)}), bf16[16,2,24576]{2,1,0:T(2,128)(2,1)}, u32[]{:S(2)}, u32[]{:S(2)}) async-start(bf16[16,2,24576]{2,1,0:T(2,128)(2,1)} %reshape.1525), calls=%async_computation.2 | async-start | bytes 3145728 | tf_op jit(solution)/shard_map/all_to_all | solution.py:259
  1501.2 151.1 %copy-start.1 = (bf16[16,1,64,768]{3,2,1,0:T(8,128)(2,1)S(1)}, bf16[16,1,64,768]{3,2,1,0:T(8,128)(2,1)}, u32[]{:S(2)}) copy-start(bf16[16,1,64,768]{3,2,1,0:T(8,128)(2,1)} %param.24) | copy-start | bytes 4718596
  (89 other events, 863.2 us)
Sparse Core Ops, SparseCore 0:
  56.9 43.9 all-gather.6
  103.2 38.0 all-gather.8
  143.6 37.3 all-gather.10
  183.1 37.2 all-gather.12
  222.4 44.2 all-gather.14
  1046.2 19.6 reduce-scatter.13
  1082.7 76.3 reduce-scatter.11
  1161.4 77.0 reduce-scatter.9
  1242.4 68.1 reduce-scatter.21
  1315.8 136.0 all-reduce.31
  1456.8 62.4 reduce-scatter.17
  1523.5 61.9 reduce-scatter.15
  1590.3 61.9 reduce-scatter.19
where the time goes:
time: 1680 us; the launch traced here: 1660 us
  local copies, waits for them, and re-layouts  414 us (25%)
  matrix products  391 us (23%)
  waiting for transfers between devices  334 us (20%)
  other arithmetic  260 us (15%)
  blocking collectives  220 us (13%)
  between operations  18.3 us (1%)
  starting transfers between devices  18 us (1%)
    dot_general x6, matrix products, strict_scan(): jnp.einsum('kijh,kjhp->kihp', weights_in, blocked, precision=exact_prec)  165 us
    dynamic_slice x128, local copies, waits for them, and re-layouts, strict_scan(): _, entering = lax.scan(carry_step, start_state, (block_decay, block_states))  75.9 us
    reduce_scatter x1, waiting for transfers between devices, shards(): lax.psum_scatter(partial_row_block, 'tensor', scatter_dimension=1, tiled=...  73.9 us
    psum x1, blocking collectives, shards(): lax.psum((grad_convx, grad_bias, grad_alog, grad_skip, grad_gain), 'dp')  73.8 us
    reduce_scatter x1, waiting for transfers between devices, shards(): lax.psum_scatter(output_local, 'dp', scatter_dimension=1, tiled=True)  66.8 us
    reduce_scatter x1, waiting for transfers between devices, shards(): lax.psum_scatter(gate_wgrad, 'dp', scatter_dimension=0, tiled=True)  66.2 us
    dot_general x6, matrix products, strict_scan(): jnp.einsum('kjn,kjhp->khnp', in_maps, blocked * to_end[..., None], precis...  66 us
    psum x1, waiting for transfers between devices, shards(): lax.psum((bc_wgrad, norm_part, grad_convbc), ('dp', 'tensor'))  65.8 us
  transfers between devices with their start and end apart: 16, of which 7 were waited for; matrix products, arithmetic and copies ran while one was open for 32% of the time, Pallas kernels for 0%

commit v1 on v0

v1 whole, which is shorter than its diff:
```python
import functools
import jax
import jax.numpy as jnp
from jax import lax
from jax.experimental import pallas as pl
from jax.experimental.pallas import tpu as pltpu
from jax.sharding import Mesh
from jax.sharding import PartitionSpec as P

F32 = jnp.float32
BF = jnp.bfloat16
CH = 128
BLK = 256
ZR = 32
HIGH = lax.Precision.HIGHEST
VMEM_LIMIT = 60 * 1024 * 1024


def nn(a, b):
    return lax.dot_general(a, b, (((1,), (0,)), ((), ())), preferred_element_type=F32)


def nt(a, b):
    return lax.dot_general(a, b, (((1,), (1,)), ((), ())), preferred_element_type=F32)


def tn(a, b):
    return lax.dot_general(a, b, (((0,), (0,)), ((), ())), preferred_element_type=F32)


def running(rows, tri):
    return lax.dot_general(rows, tri, (((1,), (0,)), ((), ())), precision=HIGH, preferred_element_type=F32)


def softplus(z):
    return jnp.maximum(z, 0.0) + jnp.log1p(jnp.exp(-jnp.abs(z)))


def sigmoid(v):
    return 1.0 / (1.0 + jnp.exp(-v))


def tri(cond):
    r = lax.broadcasted_iota(jnp.int32, (CH, CH), 0)
    c = lax.broadcasted_iota(jnp.int32, (CH, CH), 1)
    return jnp.where(cond(r, c), 1.0, 0.0).astype(F32)


def interleave(core, a_ref, b_ref):
    parts = []
    for i in range(a_ref.shape[0]):
        a, b = a_ref[i].astype(F32), b_ref[i].astype(F32)
        parts += [jnp.where(core == 0, a, b), jnp.where(core == 0, b, a)]
    return jnp.concatenate(parts, 0)


def split_rows(core, v, own_ref, oth_ref):
    width = own_ref.shape[1]
    for i in range(own_ref.shape[0]):
        e = v[2 * i * width : (2 * i + 1) * width]
        o = v[(2 * i + 1) * width : (2 * i + 2) * width]
        own_ref[i] = jnp.where(core == 0, e, o).astype(own_ref.dtype)
        oth_ref[i] = jnp.where(core == 0, o, e).astype(oth_ref.dtype)


def decays(z, alog, mask):
    dt = softplus(z)
    a = -jnp.exp(alog) * dt
    cs = running(a, tri(lambda r, c: r <= c))
    return dt * mask, a, cs


def enter(meta, xa, xb, w, gain, taps, bias, alog, nrm, gate, ain, u, zt, sf, wt, halo, state, vfe):
    j = pl.program_id(0)
    core, length = meta[0], meta[1]
    dm = w.shape[0]
    inner = gate.shape[0]
    heads = inner // 64
    cat = inner + 2 * 64
    top = inner

    @pl.when(j == 0)
    def _():
        wt[0 : 2 * inner + 128, :] = w[:, inner : 3 * inner + 128].T
        wt[2 * inner + 128 : 2 * inner + 128 + ZR, :] = w[:, 3 * inner + 128 : 3 * inner + 256].T[0:ZR]
        halo[...] = jnp.zeros_like(halo)
        state[...] = jnp.zeros_like(state)

    x = interleave(core, xa, xb)
    r = lax.rsqrt(jnp.mean(x * x, axis=-1, keepdims=True) + 1e-05)
    normed = (x * r * gain[...]).astype(BF)
    nrm[...] = normed
    gate[...] = nt(wt[0:top, :], normed)
    for g in range(0, cat, 128):
        cur = nt(wt[top + g : top + g + 128, :], normed)
        full = jnp.concatenate([halo[g : g + 128, :], cur], 1)
        halo[g : g + 128, :] = cur[:, BLK - 128 :]
        ain[g : g + 128, :] = cur.astype(ain.dtype)
        t = taps[g : g + 128, :]
        acc = t[:, 3:4] * cur
        for k in (1, 2, 3):
            acc = acc + t[:, 3 - k : 4 - k] * pltpu.roll(full, k, 1)[:, 128:]
        u[g : g + 128, :] = acc
    z = nt(wt[top + cat : top + cat + ZR, :], normed) + bias[...]
    zt[...] = z
    for q in range(BLK // CH):
        lanes = slice(q * CH, (q + 1) * CH)
        pos = j * BLK + q * CH + lax.broadcasted_iota(jnp.int32, (1, CH), 1)
        mask = jnp.where(pos < length, 1.0, 0.0)
        mdt, a, cs = decays(z[:, lanes], alog[...], mask)
        tot = cs[:, CH - 1 : CH]
        wrow = mdt * jnp.exp(tot - cs)
        etot = jnp.exp(tot)
        bu = u[inner : inner + 64, lanes]
        bt = (bu * sigmoid(bu)).astype(BF)
        for h in range(heads):
            hs = slice(64 * h, 64 * h + 64)
            uh = u[hs, lanes]
            vfe[hs, :] = (uh * sigmoid(uh) * wrow[h : h + 1, :]).astype(BF)
        add = nt(vfe[...], bt)
        for h in range(heads):
            hs = slice(64 * h, 64 * h + 64)
            sf[q, hs, :] = state[hs, :].astype(sf.dtype)
            state[hs, :] = state[hs, :] * etot[h : h + 1, :] + add[hs, :]


def mix(meta, dskip, dya, dyb, wot, gate, u, zt, sf, gain, alog, own, oth, dgate, dxp, ddt, dap, dbc, zb, sbin, gwo, dgain, dsk, wo, gacc, gy, ynt, yin, dv, dye, vfe, vbe, sb, dsf, rows):
    i = pl.program_id(0)
    last = pl.num_programs(0) - 1
    j = last - i
    core, length = meta[0], meta[1]
    inner = gate.shape[0]
    heads = inner // 64

    @pl.when(i == 0)
    def _():
        wo[...] = wot[...].T
        gacc[...] = jnp.zeros_like(gacc)
        sb[...] = jnp.zeros_like(sb)
        dsf[...] = jnp.zeros_like(dsf)
        dgain[...] = jnp.zeros_like(dgain)
        dsk[...] = jnp.zeros_like(dsk)

    cot = interleave(core, dya, dyb)
    rowpos = j * BLK + lax.broadcasted_iota(jnp.int32, (BLK, 1), 0)
    cot = jnp.where(rowpos < length, cot, 0.0).astype(BF)
    gy[...] = nt(wo[...], cot).astype(BF).astype(F32)
    low = lax.broadcasted_iota(jnp.int32, (CH, CH), 0) > lax.broadcasted_iota(jnp.int32, (CH, CH), 1)
    up = lax.broadcasted_iota(jnp.int32, (CH, CH), 0) < lax.broadcasted_iota(jnp.int32, (CH, CH), 1)
    for q in reversed(range(BLK // CH)):
        lanes = slice(q * CH, (q + 1) * CH)
        pos = j * BLK + q * CH + lax.broadcasted_iota(jnp.int32, (1, CH), 1)
        mask = jnp.where(pos < length, 1.0, 0.0)
        mdt, a, cs = decays(zt[:, lanes], alog[...], mask)
        csf = cs[0:16]
        ecb = cs[16:32] - a[16:32]
        totf = cs[0:16, CH - 1 : CH]
        totb = cs[16:32, CH - 1 : CH]
        ccf = csf.T
        ccb = ecb.T
        ef = jnp.exp(csf)
        wf = jnp.exp(totf - csf)
        eb = jnp.exp(totb - ecb)
        wb = jnp.exp(ecb)
        etf = jnp.exp(totf)
        etb = jnp.exp(totb)
        bu = u[inner : inner + 64, lanes]
        cu = u[inner + 64 : inner + 128, lanes]
        bt = (bu * sigmoid(bu)).astype(BF)
        ct = (cu * sigmoid(cu)).astype(BF)
        gmat = tn(ct, bt)
        glow = jnp.where(low, gmat, 0.0)
        gup = jnp.where(up, gmat, 0.0)
        sbb = sb[...].astype(BF)
        sbin[q] = sbb
        dsb = dsf[...].astype(BF)
        yin[0:inner, :] = nn(sf[q], ct)
        yin[inner : 2 * inner, :] = nn(sbb, ct)
        dv[...] = nn(dsb, bt)
        dg_sum = jnp.zeros((CH, CH), F32)
        for h in range(heads):
            hs = slice(64 * h, 64 * h + 64)
            h1 = slice(h, h + 1)
            uh = u[hs, lanes]
            x = uh * sigmoid(uh)
            mf = mdt[h : h + 1, :]
            mb = mdt[16 + h : 17 + h, :]
            vf = x * mf
            vb = x * mb
            vf16 = vf.astype(BF)
            vb16 = vb.astype(BF)
            pm = jnp.exp(jnp.where(low, ccf[:, h1] - csf[h1, :], ecb[h1, :] - ccb[:, h1]))
            ml = (pm * glow).astype(BF)
            mu = (pm * gup).astype(BF)
            ybi = yin[inner + 64 * h : inner + 64 * h + 64, :] * eb[h1, :]
            yf = nt(vf16, ml) + yin[hs, :] * ef[h1, :]
            yb = nt(vb16, mu) + ybi
            yt = yf + yb + dskip[h] * x
            gt = gate[hs, lanes]
            sg = sigmoid(gt)
            sl = gt * sg
            g = yt * sl
            ri = lax.rsqrt(jnp.mean(g * g, axis=0, keepdims=True) + 1e-05)
            gh = g * ri
            gn = gain[hs, :]
            ynt[hs, lanes] = (gh * gn).astype(BF)
            gyh = gy[hs, lanes]
            dgain[hs, :] += gyh * gh
            ds = gyh * gn
            dg = ri * (ds - gh * jnp.mean(ds * gh, axis=0, keepdims=True))
            dgate[hs, lanes] = (dg * yt * (sg * (1.0 + gt * (1.0 - sg)))).astype(BF)
            dy = dg * sl
            dyb16 = dy.astype(BF)
            dvi = dv[hs, :] * wf[h1, :]
            dvf = nn(dyb16, ml) + dvi
            dvb = nn(dyb16, mu)
            dyr = dyb16.astype(F32)
            vfr = vf16.astype(F32)
            qm = tn(dyb16, x.astype(BF))
            dg_sum = dg_sum + qm * pm * jnp.where(low, mf, mb)
            sxf = jnp.sum(x * dvf, axis=0, keepdims=True)
            sxb = jnp.sum(x * dvb, axis=0, keepdims=True)
            rows[0, h1, :] = sxf
            rows[1, h1, :] = sxb
            rows[2, h1, :] = jnp.sum(dyr * yf - vfr * dvf, axis=0, keepdims=True)
            rows[3, h1, :] = jnp.sum(vb16.astype(F32) * dvb - dyr * yb, axis=0, keepdims=True)
            prod = jnp.sum(dsf[hs, :] * sf[q, hs, :].astype(F32), axis=0, keepdims=True)
            prod = jnp.sum(prod, axis=1, keepdims=True) * etf[h1, :]
            rows[4, h1, :] = jnp.sum(vfr * dvi, axis=0, keepdims=True) + prod * (1.0 / CH)
            rows[5, h1, :] = jnp.sum(dyr * ybi, axis=0, keepdims=True)
            dsk[h1, :] += jnp.sum(dy * x, axis=0, keepdims=True)
            dxp[hs, lanes] = dskip[h] * dy + mf * dvf + mb * dvb
            dye[hs, :] = (dy * ef[h1, :]).astype(BF)
            dye[inner + 64 * h : inner + 64 * h + 64, :] = (dy * eb[h1, :]).astype(BF)
            vfe[hs, :] = (vf * wf[h1, :]).astype(BF)
            vbe[hs, :] = (vb * wb[h1, :]).astype(BF)
        dgb = jnp.where(low | up, dg_sum, 0.0).astype(BF)
        dbc[64:128, lanes] = nt(bt, dgb) + tn(sf[q], dye[0:inner, :]) + tn(sbb, dye[inner : 2 * inner, :])
        dbc[0:64, lanes] = nn(ct, dgb) + tn(dsb, vfe[...])
        grow = nt(dye[...], ct)
        srow = nt(vbe[...], bt)
        zb[q] = grow[inner : 2 * inner, :].astype(zb.dtype)
        for h in range(heads):
            hs = slice(64 * h, 64 * h + 64)
            dsf[hs, :] = dsf[hs, :] * etf[h : h + 1, :] + grow[hs, :]
            sb[hs, :] = sb[hs, :] * etb[h : h + 1, :] + srow[hs, :]
        ddt[0:16, lanes] = rows[0] * mask
        ddt[16:32, lanes] = rows[1] * mask
        dap[0:16, lanes] = running(rows[2], tri(lambda r, c: r >= c)) + jnp.sum(rows[4], axis=1, keepdims=True)
        dap[16:32, lanes] = running(rows[3], tri(lambda r, c: r > c)) + jnp.sum(rows[5], axis=1, keepdims=True)
    o = tn(ynt[...], wo[...])
    split_rows(core, o, own, oth)
    gacc[...] += nn(ynt[...], cot)

    @pl.when(i == last)
    def _():
        gwo[...] = gacc[...].T.astype(gwo.dtype)


def carry(meta, u, zt, alog, dxp, ddt, dap, dbc, zb, sbin, du, dz, dbias, dal, dsb, dvs, vbe, row):
    j = pl.program_id(0)
    length = meta[1]
    inner = dxp.shape[0]
    heads = inner // 64

    @pl.when(j == 0)
    def _():
        dsb[...] = jnp.zeros_like(dsb)
        dbias[...] = jnp.zeros_like(dbias)
        dal[...] = jnp.zeros_like(dal)
        row[...] = jnp.zeros_like(row)

    for q in range(BLK // CH):
        lanes = slice(q * CH, (q + 1) * CH)
        pos = j * BLK + q * CH + lax.broadcasted_iota(jnp.int32, (1, CH), 1)
        mask = jnp.where(pos < length, 1.0, 0.0)
        z = zt[:, lanes]
        mdt, a, cs = decays(z, alog[...], mask)
        ecb = cs[16:32] - a[16:32]
        etb = jnp.exp(cs[16:32, CH - 1 : CH])
        wb = jnp.exp(ecb)
        mw = mdt[16:32] * wb
        bu = u[inner : inner + 64, lanes]
        cu = u[inner + 64 : inner + 128, lanes]
        sgb = sigmoid(bu)
        sgc = sigmoid(cu)
        bt = (bu * sgb).astype(BF)
        dsb16 = dsb[...].astype(BF)
        dvs[...] = nn(dsb16, bt)
        for h in range(heads):
            hs = slice(64 * h, 64 * h + 64)
            h1 = slice(h, h + 1)
            uh = u[hs, lanes]
            sg = sigmoid(uh)
            x = uh * sg
            raw = dvs[hs, :]
            row[0, h1, :] = jnp.sum(x * raw, axis=0, keepdims=True) * wb[h1, :]
            prod = jnp.sum(dsb[hs, :] * sbin[q, hs, :].astype(F32), axis=0, keepdims=True)
            row[1, h1, :] = jnp.broadcast_to(jnp.sum(prod, axis=1, keepdims=True) * etb[h1, :], (1, CH))
            dx = dxp[hs, lanes] + raw * mw[h1, :]
            du[hs, lanes] = dx * (sg * (1.0 + uh * (1.0 - sg)))
            vbe[hs, :] = (x * mw[h1, :]).astype(BF)
        db = dbc[0:64, lanes] + tn(dsb16, vbe[...])
        du[inner : inner + 64, lanes] = db * (sgb * (1.0 + bu * (1.0 - sgb)))
        du[inner + 64 : inner + 128, lanes] = dbc[64:128, lanes] * (sgc * (1.0 + cu * (1.0 - sgc)))
        for h in range(heads):
            hs = slice(64 * h, 64 * h + 64)
            dsb[hs, :] = dsb[hs, :] * etb[h : h + 1, :] + zb[q, hs, :].astype(F32)
        dab = dap[16:32, lanes] + running(mdt[16:32] * row[0], tri(lambda r, c: r > c)) + row[1]
        da = jnp.concatenate([dap[0:16, lanes], dab], 0)
        dd = jnp.concatenate([ddt[0:16, lanes], ddt[16:32, lanes] + row[0] * mask], 0)
        dal[...] += da * a
        dzz = (dd - jnp.exp(alog[...]) * da) * sigmoid(z)
        dbias[...] += dzz
        dz[:, lanes] = dzz.astype(dz.dtype)


def leave(meta, du, nxt, ain, dgate, dz, nrm, wt, taps, own, oth, gw, dtaps, acc, cat):
    j = pl.program_id(0)
    last = pl.num_programs(0) - 1
    core = meta[0]
    inner = dgate.shape[0]
    conv = inner + 128

    @pl.when(j == 0)
    def _():
        acc[...] = jnp.zeros_like(acc)
        dtaps[...] = jnp.zeros_like(dtaps)

    cat[0:inner, :] = dgate[...]
    for g in range(0, conv, 128):
        cur = du[g : g + 128, :]
        after = jnp.where(j == last, 0.0, nxt[g : g + 128, :])
        full = jnp.concatenate([cur, after], 1)
        a = ain[g : g + 128, :].astype(F32)
        t = taps[g : g + 128, :]
        total = t[:, 3:4] * cur
        p = a * cur
        dtaps[3, g : g + 128, :] += p[:, 0:128] + p[:, 128:256]
        for k in (1, 2, 3):
            moved = pltpu.roll(full, BLK + 128 - k, 1)[:, 0:BLK]
            total = total + t[:, 3 - k : 4 - k] * moved
            p = a * moved
            dtaps[3 - k, g : g + 128, :] += p[:, 0:128] + p[:, 128:256]
        cat[inner + g : inner + g + 128, :] = total.astype(BF)
    cat[inner + conv : inner + conv + ZR, :] = dz[...]
    gn = tn(cat[...], wt[...])
    split_rows(core, gn, own, oth)
    acc[...] += nn(cat[...], nrm[...])

    @pl.when(j == last)
    def _():
        gw[...] = acc[...].T.astype(gw.dtype)


def _params():
    return pltpu.CompilerParams(dimension_semantics=("arbitrary",), vmem_limit_bytes=VMEM_LIMIT)


def full(shape):
    return pl.BlockSpec(shape, lambda j, *_: (0,) * len(shape))


def sds(shape, dt):
    return jax.ShapeDtypeStruct(shape, dt)


def run_enter(meta, xa, xb, wpack, gain, taps, bias, alog):
    nblk, width, dm = xa.shape
    length = 2 * nblk * width
    inner = taps.shape[0] - 128
    nk = BLK // (2 * width)
    nb = length // BLK
    rowsb = pl.BlockSpec((nk, width, dm), lambda j, *_: (j, 0, 0))
    colb = lambda n: pl.BlockSpec((n, BLK), lambda j, *_: (0, j))
    wrows = 2 * inner + 128 + ZR
    return pl.pallas_call(
        enter,
        grid_spec=pltpu.PrefetchScalarGridSpec(
            num_scalar_prefetch=1,
            grid=(nb,),
            in_specs=[rowsb, rowsb, full(wpack.shape), full(gain.shape), full(taps.shape), full(bias.shape), full(alog.shape)],
            out_specs=[
                pl.BlockSpec((BLK, dm), lambda j, *_: (j, 0)),
                colb(inner),
                colb(inner + 128),
                colb(inner + 128),
                colb(ZR),
                pl.BlockSpec((BLK // CH, inner, 64), lambda j, *_: (j, 0, 0)),
                full((wrows, dm)),
            ],
            scratch_shapes=[
                pltpu.VMEM((inner + 128, 128), F32),
                pltpu.VMEM((inner, 64), F32),
                pltpu.VMEM((inner, CH), BF),
            ],
        ),
        out_shape=[
            sds((length, dm), BF),
            sds((inner, length), F32),
            sds((inner + 128, length), BF),
            sds((inner + 128, length), F32),
            sds((ZR, length), F32),
            sds((length // CH, inner, 64), BF),
            sds((wrows, dm), BF),
        ],
        compiler_params=_params(),
        cost_estimate=pl.CostEstimate(flops=2 * length * dm * wrows, bytes_accessed=30_000_000, transcendentals=4 * inner * length),
    )(meta, xa, xb, wpack, gain, taps, bias, alog)


def run_mix(meta, dskip, dya, dyb, wpack, gate, u, zt, sf, gain, alog):
    nblk, width, dm = dya.shape
    length = 2 * nblk * width
    inner = gate.shape[0]
    nk = BLK // (2 * width)
    nb = length // BLK
    rowsb = pl.BlockSpec((nk, width, dm), lambda i, *_: (nb - 1 - i, 0, 0))
    colb = lambda n: pl.BlockSpec((n, BLK), lambda i, *_: (0, nb - 1 - i))
    stb = pl.BlockSpec((BLK // CH, inner, 64), lambda i, *_: (nb - 1 - i, 0, 0))
    return pl.pallas_call(
        mix,
        grid_spec=pltpu.PrefetchScalarGridSpec(
            num_scalar_prefetch=2,
            grid=(nb,),
            in_specs=[rowsb, rowsb, pl.BlockSpec((dm, inner), lambda i, *_: (0, 0)), colb(inner), colb(inner + 128), colb(ZR), stb, full(gain.shape), full(alog.shape)],
            out_specs=[
                rowsb,
                rowsb,
                colb(inner),
                colb(inner),
                colb(ZR),
                colb(ZR),
                colb(128),
                stb,
                stb,
                full((dm, inner)),
                full((inner, CH)),
                full((16, CH)),
            ],
            scratch_shapes=[
                pltpu.VMEM((inner, dm), BF),
                pltpu.VMEM((inner, dm), F32),
                pltpu.VMEM((inner, BLK), F32),
                pltpu.VMEM((inner, BLK), BF),
                pltpu.VMEM((2 * inner, CH), F32),
                pltpu.VMEM((inner, CH), F32),
                pltpu.VMEM((2 * inner, CH), BF),
                pltpu.VMEM((inner, CH), BF),
                pltpu.VMEM((inner, CH), BF),
                pltpu.VMEM((inner, 64), F32),
                pltpu.VMEM((inner, 64), F32),
                pltpu.VMEM((6, 16, CH), F32),
            ],
        ),
        out_shape=[
            sds((nblk, width, dm), F32),
            sds((nblk, width, dm), BF),
            sds((inner, length), BF),
            sds((inner, length), F32),
            sds((ZR, length), F32),
            sds((ZR, length), F32),
            sds((128, length), F32),
            sds((length // CH, inner, 64), BF),
            sds((length // CH, inner, 64), BF),
            sds((dm, inner), BF),
            sds((inner, CH), F32),
            sds((16, CH), F32),
        ],
        compiler_params=_params(),
        cost_estimate=pl.CostEstimate(flops=40 * 10**9, bytes_accessed=50_000_000, transcendentals=10**7),
    )(meta, dskip, dya, dyb, wpack, gate, u, zt, sf, gain, alog)


def run_carry(meta, u, zt, alog, dxp, ddt, dap, dbc, zb, sbin):
    inner, length = dxp.shape
    nb = length // BLK
    colb = lambda n: pl.BlockSpec((n, BLK), lambda j, *_: (0, j))
    stb = pl.BlockSpec((BLK // CH, inner, 64), lambda j, *_: (j, 0, 0))
    return pl.pallas_call(
        carry,
        grid_spec=pltpu.PrefetchScalarGridSpec(
            num_scalar_prefetch=1,
            grid=(nb,),
            in_specs=[colb(inner + 128), colb(ZR), full(alog.shape), colb(inner), colb(ZR), colb(ZR), colb(128), stb, stb],
            out_specs=[colb(inner + 128), colb(ZR), full((ZR, CH)), full((ZR, CH))],
            scratch_shapes=[
                pltpu.VMEM((inner, 64), F32),
                pltpu.VMEM((inner, CH), F32),
                pltpu.VMEM((inner, CH), BF),
                pltpu.VMEM((2, 16, CH), F32),
            ],
        ),
        out_shape=[sds((inner + 128, length), F32), sds((ZR, length), BF), sds((ZR, CH), F32), sds((ZR, CH), F32)],
        compiler_params=_params(),
        cost_estimate=pl.CostEstimate(flops=10**9, bytes_accessed=30_000_000, transcendentals=10**6),
    )(meta, u, zt, alog, dxp, ddt, dap, dbc, zb, sbin)


def run_leave(meta, du, ain, dgate, dz, nrm, wt, taps, width):
    inner, length = dgate.shape
    dm = nrm.shape[1]
    nb = length // BLK
    nk = BLK // (2 * width)
    wrows = wt.shape[0]
    rowsb = pl.BlockSpec((nk, width, dm), lambda j, *_: (j, 0, 0))
    colb = lambda n: pl.BlockSpec((n, BLK), lambda j, *_: (0, j))
    nblk = length // (2 * width)
    return pl.pallas_call(
        leave,
        grid_spec=pltpu.PrefetchScalarGridSpec(
            num_scalar_prefetch=1,
            grid=(nb,),
            in_specs=[
                colb(inner + 128),
                pl.BlockSpec((inner + 128, 128), lambda j, *_: (0, jnp.minimum(2 * j + 2, 2 * nb - 1))),
                colb(inner + 128),
                colb(inner),
                colb(ZR),
                pl.BlockSpec((BLK, dm), lambda j, *_: (j, 0)),
                full(wt.shape),
                full(taps.shape),
            ],
            out_specs=[rowsb, rowsb, full((dm, wrows)), full((4, inner + 128, 128))],
            scratch_shapes=[pltpu.VMEM((wrows, dm), F32), pltpu.VMEM((wrows, BLK), BF)],
        ),
        out_shape=[sds((nblk, width, dm), F32), sds((nblk, width, dm), BF), sds((dm, wrows), BF), sds((4, inner + 128, 128), F32)],
        compiler_params=_params(),
        cost_estimate=pl.CostEstimate(flops=4 * length * dm * wrows, bytes_accessed=30_000_000, transcendentals=0),
    )(meta, du, du, ain, dgate, dz, nrm, wt, taps)


def permute_slots(rows, sender):
    def body(order, src, dst):
        dst[...] = src[...]

    shape = (1,) + rows.shape[1:]
    zeros = (0,) * (rows.ndim - 1)
    return pl.pallas_call(
        body,
        grid_spec=pltpu.PrefetchScalarGridSpec(
            num_scalar_prefetch=1,
            grid=(rows.shape[0],),
            in_specs=[pl.BlockSpec(shape, lambda i, order: (order[i],) + zeros)],
            out_specs=pl.BlockSpec(shape, lambda i, order: (i,) + zeros),
        ),
        out_shape=sds(rows.shape, rows.dtype),
        compiler_params=_params(),
    )(sender, rows)


SWAP = [(0, 1), (1, 0)]
CORNER = [(0, 0), (1, 2), (2, 1), (3, 3)]


def twin(v, axis):
    return lax.ppermute(v, axis, SWAP)


def corner(v):
    return lax.ppermute(v, ("core", "tensor"), CORNER)


def both(v, other, index):
    return jnp.stack([jnp.where(index == 0, v, other), jnp.where(index == 0, other, v)])


def gather_weights(pack):
    n = lax.axis_size("z")
    z, x, y = (lax.axis_index(a) for a in ("z", "x", "tensor"))
    line = jnp.zeros((n,) + pack.shape, pack.dtype)
    line = lax.dynamic_update_index_in_dim(line, pack, z, 0)
    for k in range(1, n):
        got = lax.ppermute(pack, "z", [(i, (i + k) % n) for i in range(n)])
        line = lax.dynamic_update_index_in_dim(line, got, (z - k) % n, 0)
    mid = pack.shape[1] // 2
    a, b = line[..., :mid], line[..., mid:]
    a = both(a, twin(a, "x"), x)
    b = both(b, twin(b, "tensor"), y)
    a = both(a, twin(a, "tensor"), y)
    b = both(b, twin(b, "x"), x)
    a = jnp.transpose(a, (2, 1, 0, 3, 4))
    b = jnp.transpose(b, (2, 0, 1, 3, 4))
    return jnp.concatenate([a, b], -1)


def halve(v, axis, dim):
    i = lax.axis_index(axis)
    keep = lax.dynamic_index_in_dim(v, i, dim, False)
    send = lax.dynamic_index_in_dim(v, 1 - i, dim, False).astype(BF)
    return keep.astype(F32) + twin(send, axis).astype(F32)


def scatter_sum(v, cut):
    n = lax.axis_size("z")
    z = lax.axis_index("z")
    a = halve(halve(v[..., :cut], "x", 1).astype(BF), "tensor", 1)
    b = halve(halve(v[..., cut:], "tensor", 2).astype(BF), "x", 1)
    c = jnp.concatenate([a, b], -1)
    total = lax.dynamic_index_in_dim(c, z, 0, False)
    low = c.astype(BF)
    for k in range(1, n):
        send = lax.dynamic_index_in_dim(low, (z + k) % n, 0, False)
        total = total + lax.ppermute(send, "z", [(i, (i + k) % n) for i in range(n)]).astype(F32)
    return total


def total_of(v):
    for axis in ("x", "tensor"):
        v = v + twin(v, axis)
    n = lax.axis_size("z")
    k = 1
    while k < n:
        v = v + lax.ppermute(v, "z", [(i, i ^ k) for i in range(n)])
        k *= 2
    return v


def pad_rows(fwd, bwd):
    h = fwd.shape[0]
    gap = jnp.zeros((16 - h,) + fwd.shape[1:], fwd.dtype)
    return jnp.concatenate([fwd, gap, bwd, gap], 0)


def shards(
    layer_in,
    out_grad,
    seq_lengths,
    slot_perm,
    norm_gain,
    w_gate,
    w_inner,
    w_bc,
    w_dt,
    conv_x,
    conv_bc,
    dt_bias,
    a_log,
    dskip,
    inner_gain,
    w_out,
):
    z, x, core, y = (lax.axis_index(a) for a in ("z", "x", "core", "tensor"))
    nz = lax.axis_size("z")
    group = ("tensor", "z", "x")
    seqs, _, width, dm = layer_in.shape
    inner = w_gate.shape[1]
    heads = a_log.shape[0]
    rows = w_gate.shape[0]
    slot = lax.axis_index(group)
    ids = jnp.arange(seqs, dtype=jnp.int32)
    sender = jnp.sum(jnp.where(slot_perm[None, :] == ids[:, None], ids[None, :], 0), axis=1)
    my_length = jnp.sum(jnp.where(slot_perm == slot, seq_lengths, 0))
    meta = jnp.stack([core.astype(jnp.int32), my_length.astype(jnp.int32)])

    dt_cols = jnp.transpose(w_dt.reshape(rows, heads, 2), (0, 2, 1))
    dt_cols = jnp.pad(dt_cols, ((0, 0), (0, 0), (0, 16 - heads))).reshape(rows, ZR)
    pack = jnp.concatenate([w_out.T, w_gate, w_inner, w_bc, jnp.pad(dt_cols, ((0, 0), (0, 128 - ZR)))], 1)
    tiny = jnp.concatenate([dt_bias, a_log, dskip, jnp.zeros((inner - 4 * heads,), F32)])
    mine = corner(jnp.concatenate([conv_x, inner_gain[None], tiny[None], jnp.zeros((2, inner), F32)], 0))
    taps = jnp.concatenate([mine[0:4].T, conv_bc.T], 0)
    gain_u = mine[4][:, None]
    bias = mine[5, 0 : 2 * heads].reshape(heads, 2)
    alog = mine[5, 2 * heads : 3 * heads]
    skip = mine[5, 3 * heads : 4 * heads]
    bias = pad_rows(bias[:, 0:1], bias[:, 1:2])
    alog = pad_rows(alog[:, None], alog[:, None])

    rows_own = lax.all_to_all(permute_slots(layer_in[:, 0], sender), group, 0, 0, tiled=True)
    rows_oth = twin(rows_own, "core")
    weights = gather_weights(corner(pack)).reshape(dm, pack.shape[1])
    cot_own = lax.all_to_all(out_grad[:, 0], group, 0, 0, tiled=True)
    cot_oth = twin(cot_own, "core")

    nrm, gate, ain, u, zt, sf, wt = run_enter(meta, rows_own, rows_oth, weights, norm_gain[None], taps, bias, alog)
    own, oth, dgate, dxp, ddt, dap, dbc, zb, sbin, gwo, dgain, dsk = run_mix(
        meta, skip, cot_own, cot_oth, weights, gate, u, zt, sf, gain_u, alog
    )
    position = (2 * jnp.arange(rows_own.shape[0], dtype=jnp.int32)[:, None] + core) * width
    position = position + jnp.arange(width, dtype=jnp.int32)[None, :]
    mask = (position < my_length).astype(F32)[..., None]
    xf = rows_own.astype(F32)
    out_rows = xf + mask * (own + twin(oth, "core").astype(F32))
    output = lax.all_to_all(out_rows.astype(BF), group, 0, 0, tiled=True)
    gwo_sum = scatter_sum(gwo.reshape(nz, 2, 2, rows, inner), inner // 2)

    du, dz, dbias, dal = run_carry(meta, u, zt, alog, dxp, ddt, dap, dbc, zb, sbin)
    gown, goth, gw, dtaps = run_leave(meta, du, ain, dgate, dz, nrm, wt, taps, width)
    gn = gown + twin(goth, "core").astype(F32)
    inv = lax.rsqrt(jnp.mean(xf * xf, axis=-1, keepdims=True) + 1e-05)
    unit = xf * inv
    scaled = gn * norm_gain
    norm_part = jnp.sum(gn * unit, axis=(0, 1))
    back = cot_own.astype(F32) + inv * (scaled - unit * jnp.mean(scaled * unit, axis=-1, keepdims=True))
    input_grad = lax.all_to_all(back.astype(BF), group, 0, 0, tiled=True)

    gw_sum = scatter_sum(gw.reshape(nz, 2, 2, rows, gw.shape[1]), inner)
    bc_part = gw_sum[:, 2 * inner : 2 * inner + 128]
    bc_part = bc_part + twin(bc_part, "core")
    grads = corner(
        jnp.concatenate([gwo_sum, gw_sum[:, : 2 * inner], bc_part, gw_sum[:, 2 * inner + 128 :]], 1).astype(BF)
    ).astype(F32)
    out_sum = grads[:, :inner].T
    gate_sum = grads[:, inner : 2 * inner]
    inner_sum = grads[:, 2 * inner : 3 * inner]
    bc_sum = grads[:, 3 * inner : 3 * inner + 128]
    dt_sum = grads[:, 3 * inner + 128 :].reshape(rows, 2, 16)[:, :, :heads]
    dt_sum = jnp.transpose(dt_sum, (0, 2, 1)).reshape(rows, 2 * heads)

    dtap = jnp.sum(dtaps, axis=-1)
    dbias = jnp.sum(dbias, axis=1).reshape(2, 16)[:, :heads].T.reshape(2 * heads)
    dal = jnp.sum(dal, axis=1).reshape(2, 16)[:, :heads].sum(0)
    dskips = jnp.sum(dsk, axis=1)[:heads]
    half = [dtap[:, :inner].reshape(-1), jnp.sum(dgain, axis=1), dbias, dal, dskips]
    summed = [norm_part, dtap[:, inner:].reshape(-1)]
    sizes = [v.shape[0] for v in half + summed]
    vec = jnp.concatenate(half + summed)
    vec = total_of(jnp.pad(vec, (0, -vec.shape[0] % 1024)).reshape(-1, 128)).reshape(-1)
    pair = lax.ppermute(vec, "core", SWAP)
    here = jnp.where(core == y, vec, pair)
    joint = vec + pair
    cuts = [sum(sizes[:i]) for i in range(len(sizes) + 1)]
    convx_g, gain_g, bias_g, alog_g, skip_g = (here[cuts[i] : cuts[i + 1]] for i in range(5))
    norm_g, convbc_g = (joint[cuts[i] : cuts[i + 1]] for i in (5, 6))
    return (
        output[:, None],
        input_grad[:, None],
        norm_g,
        gate_sum,
        inner_sum,
        bc_sum,
        dt_sum,
        convx_g.reshape(4, inner),
        convbc_g.reshape(4, 128),
        bias_g,
        alog_g,
        skip_g,
        gain_g,
        out_sum,
    )


def solution(mesh):
    dp, tensor = mesh.devices.shape
    fine = Mesh(mesh.devices.reshape(dp // 4, 2, 2, tensor), ("z", "x", "core", "tensor"))
    d = ("z", "x", "core")
    t = "tensor"
    return jax.shard_map(
        shards,
        mesh=fine,
        in_specs=(
            P(None, t, d, None),
            P(None, t, d, None),
            P(),
            P(),
            P(),
            P(d, t),
            P(d, t),
            P(d, None),
            P(d, t),
            P(None, t),
            P(),
            P(t),
            P(t),
            P(t),
            P(t),
            P(t, d),
        ),
        out_specs=(
            P(None, t, d, None),
            P(None, t, d, None),
            P(),
            P(d, t),
            P(d, t),
            P(d, None),
            P(d, t),
            P(None, t),
            P(),
            P(t),
            P(t),
            P(t),
            P(t),
            P(t, d),
        ),
        check_vma=False,
    )
```

time: 1680 us -> 464 us (0.28)
  matrix products: 391 us -> 0 us
  local copies, waits for them, and re-layouts: 414 us -> 38.9 us
  other arithmetic: 260 us -> 37.2 us
  blocking collectives: 220 us -> 0 us
  waiting for transfers between devices: 334 us -> 141 us
  Pallas kernels: 0 us -> 174 us
  starting transfers between devices: 18 us -> 65 us
  between operations: 18.3 us -> 1.34 us
    dot_general x36 -> x0, matrix products: 369 us -> none  [the longest x6 165 us: strict_scan(): jnp.einsum('kijh,kjhp->kihp', weights_in, blocked, precision=exact_prec)]
    reduce_scatter x6 -> x0, waiting for transfers between devices: 253 us -> none  [the longest x1 73.9 us: shards(): lax.psum_scatter(partial_row_block, 'tensor', scatter_dimension=1, tiled=...]
    pallas_call x0 -> x5, Pallas kernels: none -> 174 us  [the longest x1 84.6 us: run_mix(): pl.pallas_call(mix, grid_spec=pltpu.PrefetchScalarGridSpec(num_scalar_pre...]
    ppermute x0 -> x34, waiting for transfers between devices: none -> 141 us  [the longest x3 51 us: gather_weights(): got = lax.ppermute(pack, 'z', [(i, (i + k) % n) for i in range(n)])]
    psum x2 -> x0, blocking collectives: 116 us -> none  [the longest x1 73.8 us: shards(): lax.psum((grad_convx, grad_bias, grad_alog, grad_skip, grad_gain), 'dp')]
    reduce_sum x44 -> x10, other arithmetic: 99.4 us -> 8.15 us  [the longest x1 3.66 us: shards(): norm_part = jnp.sum(gn * unit, axis=(0, 1))]
    rev x10 -> x0, local copies, waits for them, and re-layouts: 84.1 us -> none  [the longest x2 24.5 us: mixer(): jnp.flip(strict_scan(jnp.flip(backward_v, 0), jnp.flip(state_in, 0), jnp....]
    dynamic_slice x130 -> x2, local copies, waits for them, and re-layouts: 78.5 us -> 1.68 us  [halve(): keep = lax.dynamic_index_in_dim(v, i, dim, False)]
  transfers between devices with their start and end apart: 16 -> 38, of which waited for: 7 -> 14; matrix products, arithmetic and copies ran while one was open for 32% -> 14% of each run, Pallas kernels for 0% -> 8%
where the time goes in v1:
time: 464 us; the launch traced here: 457 us
  Pallas kernels  174 us (38%)
  waiting for transfers between devices  141 us (30%)
  starting transfers between devices  65 us (14%)
  local copies, waits for them, and re-layouts  38.9 us (8%)
  other arithmetic  37.2 us (8%)
    pallas_call x1, Pallas kernels, run_mix(): pl.pallas_call(mix, grid_spec=pltpu.PrefetchScalarGridSpec(num_scalar_pre...  84.6 us
    ppermute x3, waiting for transfers between devices, gather_weights(): got = lax.ppermute(pack, 'z', [(i, (i + k) % n) for i in range(n)])  51 us
    ppermute x19, waiting for transfers between devices, twin(): return lax.ppermute(v, axis, SWAP)  41.9 us
    pallas_call x1, Pallas kernels, run_leave(): pl.pallas_call(leave, grid_spec=pltpu.PrefetchScalarGridSpec(num_scalar_p...  35.7 us
    pallas_call x1, Pallas kernels, run_enter(): pl.pallas_call(enter, grid_spec=pltpu.PrefetchScalarGridSpec(num_scalar_p...  28.1 us
    ppermute x19, starting transfers between devices, twin(): return lax.ppermute(v, axis, SWAP)  25.1 us
    ppermute x6, waiting for transfers between devices, scatter_sum(): lax.ppermute(send, 'z', [(i, (i + k) % n) for i in range(n)]).astype(F32)  21 us
    ppermute x2, waiting for transfers between devices, total_of(): v = v + lax.ppermute(v, 'z', [(i, i ^ k) for i in range(n)])  18.4 us
  transfers between devices with their start and end apart: 38, of which 14 were waited for; matrix products, arithmetic and copies ran while one was open for 14% of the time, Pallas kernels for 8%

profile of v1, /device:TPU:9, one launch (start us, length us, event | category | flops | bytes accessed | tf_op | source)
XLA Modules:
  0.0 457.4 jit_solution(4300633162068705550)
XLA Ops:
  4.8 3.7 collective-permute-start.2
  10.1 1.4 maximum_maximum_fusion
  11.5 1.9 collective-permute-start
  14.7 10.0 %shard_map.263 = bf16[16,64,768]{2,1,0:T(8,128)(2,1)} custom-call(s32[16]{0:T(128)} %select_reduce_fusion.order, bf16[16,64,768]{2,1,0:T(8,128)(2,1)} %bitcast.166), custom_call_target="tpu_custom_call" | custom-call | tf_op jit(solution)/shard_map/pallas_call | solution.py:539
  24.7 5.8 %all-to-all-start = ((bf16[16,64,768]{2,1,0:T(8,128)(2,1)}), bf16[16,64,768]{2,1,0:T(8,128)(2,1)S(1)}, u32[]{:S(2)}, u32[]{:S(2)}) async-start(bf16[16,64,768]{2,1,0:T(8,128)(2,1)} %shard_map.263), calls=%async_computation | async-start | bytes 3145728 | tf_op jit(solution)/shard_map/all_to_all | solution.py:669
  31.2 1.3 fusion.30
  34.7 1.3 collective-permute-start.5
  36.2 44.5 %collective-permute-done.3 = bf16[48,2560]{1,0:T(8,128)(2,1)S(1)} collective-permute-done((bf16[48,2560]{1,0:T(8,128)(2,1)S(1)}, bf16[48,2560]{1,0:T(8,128)(2,1)S(1)}, u32[]{:S(2)}, u32[]{:S(2)}) %collective-permute-start.3) | collective-permute-done | bytes 245792 | tf_op jit(solution)/shard_map/ppermute | solution.py:574
  80.6 5.2 %collective-permute-done.4 = bf16[48,2560]{1,0:T(8,128)(2,1)S(1)} collective-permute-done((bf16[48,2560]{1,0:T(8,128)(2,1)S(1)}, bf16[48,2560]{1,0:T(8,128)(2,1)S(1)}, u32[]{:S(2)}, u32[]{:S(2)}) %collective-permute-start.4) | collective-permute-done | bytes 245792 | tf_op jit(solution)/shard_map/ppermute | solution.py:574
  92.4 1.3 slice_bitcast_fusion.7
  94.5 4.5 all-to-all-start.1
  100.3 1.3 select_bitcast_fusion.7
  106.6 1.3 copy.178
  111.6 1.7 copy.180.taps
  114.3 1.4 pad_maximum_fusion.6
  115.7 20.8 %collective-permute-done.7 = bf16[2,4,48,1280]{3,2,1,0:T(8,128)(2,1)} collective-permute-done((bf16[2,4,48,1280]{3,2,1,0:T(8,128)(2,1)}, bf16[2,4,48,1280]{3,2,1,0:T(8,128)(2,1)}, u32[]{:S(2)}, u32[]{:S(2)}) %collective-permute-start.7) | collective-permute-done | bytes 983072 | tf_op jit(solution)/shard_map/ppermute | solution.py:557
  136.5 2.7 select_bitcast_fusion.3
  139.2 4.5 collective-permute-start.10
  143.7 2.3 select_bitcast_fusion.1
  146.0 2.1 collective-permute-start.1
  148.2 1.5 maximum_bitcast_fusion.1
  149.9 2.0 pad_maximum_fusion
  152.4 28.1 %shard_map.264 = (bf16[2048,768]{1,0:T(8,128)(2,1)}, f32[768,2048]{1,0:T(8,128)}, bf16[896,2048]{1,0:T(8,128)(2,1)}, f32[896,2048]{1,0:T(8,128)}, f32[32,2048]{1...) custom-call(s32[2]{0:T(128)} %pad_add_fusion.meta, bf16[16,64,768]{2,1,0:T(8,128)(2,1)} %copy-done, ...), custom_call_target="tpu_custom_call" | custom-call | flops 5335154688 | bytes 30000000 | tf_op jit(solution)/shard_map/pallas_call | solution.py:377
  180.5 84.6 %shard_map.265 = (f32[16,64,768]{2,1,0:T(8,128)}, bf16[16,64,768]{2,1,0:T(8,128)(2,1)}, bf16[768,2048]{1,0:T(8,128)(2,1)}, f32[768,2048]{1,0:T(8,128)}, f32[32,2...) custom-call(s32[2]{0:T(128)} %pad_add_fusion.meta, ...), custom_call_target="tpu_custom_call" | custom-call | flops 40000000000 | bytes 50000000 | tf_op jit(solution)/shard_map/pallas_call | solution.py:421
  265.1 1.4 fusion.35
  266.5 16.0 %shard_map.266 = (f32[896,2048]{1,0:T(8,128)}, bf16[32,2048]{1,0:T(8,128)(2,1)}, f32[32,128]{1,0:T(8,128)}, f32[32,128]{1,0:T(8,128)}) custom-call(s32[2]{0:T(128)} %pad_add_fusion.meta, f32[896,2048]{1,0:T(8,128)} %get-tuple-element.42.u, f32[32,2048]{1,0:T(8,128)} %get-tuple-element.43.zt, f32[32,1]{1,0:T(8,128)} %get-tuple-element.206.alog, ...), custom_call_target="tpu_custom_call" | custom-call | flops 1000000000 | bytes 30000000 | tf_op jit(solution)/shard_map/pallas_call | solution.py:480
  282.4 35.7 %shard_map.267 = (f32[16,64,768]{2,1,0:T(8,128)}, bf16[16,64,768]{2,1,0:T(8,128)(2,1)}, bf16[768,1696]{1,0:T(8,128)(2,1)}, f32[4,896,128]{2,1,0:T(8,128)}) custom-call(s32[2]{0:T(128)} %pad_add_fusion.meta, f32[896,2048]{1,0:T(8,128)} %get-tuple-element.53.du.nxt, f32[896,2048]{1,0:T(8,128)} %get-tuple-element.53.du.nxt, ...), custom_call_target="tpu_custom_call" | custom-call | flops 10670309376 | bytes 30000000 | tf_op jit(solution)/shard_map/pallas_call | solution.py:509
  319.0 1.4 slice.163
  336.1 3.7 fusion.8
  340.3 4.2 fusion.7
  344.5 4.9 %all-to-all-start.2 = ((bf16[16,64,768]{2,1,0:T(8,128)(2,1)}), bf16[16,64,768]{2,1,0:T(8,128)(2,1)S(1)}, u32[]{:S(2)}, u32[]{:S(2)}) async-start(bf16[16,64,768]{2,1,0:T(8,128)(2,1)} %get-tuple-element.175), calls=%async_computation.2 | async-start | bytes 3145728 | tf_op jit(solution)/shard_map/all_to_all | solution.py:684
  353.4 1.4 fusion.11
  356.1 7.9 %collective-permute-done.19 = bf16[4,48,384]{2,1,0:T(8,128)(2,1)S(1)} collective-permute-done((bf16[4,48,384]{2,1,0:T(8,128)(2,1)S(1)}, bf16[4,48,384]{2,1,0:T(8,128)(2,1)S(1)}, u32[]{:S(2)}, u32[]{:S(2)}) %collective-permute-start.19) | collective-permute-done | bytes 147488 | tf_op jit(solution)/shard_map/ppermute | solution.py:557
  364.0 11.3 %collective-permute-done.26 = bf16[4,48,768]{2,1,0:T(8,128)(2,1)S(1)} collective-permute-done((bf16[4,48,768]{2,1,0:T(8,128)(2,1)S(1)}, bf16[4,48,768]{2,1,0:T(8,128)(2,1)S(1)}, u32[]{:S(2)}, u32[]{:S(2)}) %collective-permute-start.26) | collective-permute-done | bytes 294944 | tf_op jit(solution)/shard_map/ppermute | solution.py:557
  376.3 1.4 collective-permute-start.30
  377.7 1.4 collective-permute-start.31
  379.3 2.8 collective-permute-start.23
  382.0 15.6 %collective-permute-done.29 = bf16[48,1696]{1,0:T(8,128)(2,1)S(1)} collective-permute-done((bf16[48,1696]{1,0:T(8,128)(2,1)S(1)}, bf16[48,1696]{1,0:T(8,128)(2,1)S(1)}, u32[]{:S(2)}, u32[]{:S(2)}) %collective-permute-start.29) | collective-permute-done | bytes 162848 | tf_op jit(solution)/shard_map/ppermute | solution.py:604
  397.7 3.7 collective-permute-done.30
  401.4 1.7 collective-permute-done.31
  403.2 2.6 collective-permute-start.32
  405.7 4.7 %all-to-all-start.3 = ((bf16[16,64,768]{2,1,0:T(8,128)(2,1)}), bf16[16,64,768]{2,1,0:T(8,128)(2,1)}, u32[]{:S(2)}, u32[]{:S(2)}) async-start(bf16[16,64,768]{2,1,0:T(8,128)(2,1)} %get-tuple-element.174), calls=%async_computation.3 | async-start | bytes 3145728 | tf_op jit(solution)/shard_map/all_to_all | solution.py:695
  412.0 3.9 collective-permute-start.33
  415.8 1.4 collective-permute-done.13
  418.4 8.1 %collective-permute-done.33 = bf16[48,2464]{1,0:T(8,128)(2,1)S(1)} collective-permute-done((bf16[48,2464]{1,0:T(8,128)(2,1)S(1)}, bf16[48,2464]{1,0:T(8,128)(2,1)S(1)}, u32[]{:S(2)}, u32[]{:S(2)}) %collective-permute-start.33) | collective-permute-done | bytes 236576 | tf_op jit(solution)/shard_map/ppermute | solution.py:561
  427.2 11.6 %collective-permute-done.15 = f32[48,128]{1,0:T(8,128)S(1)} collective-permute-done((f32[48,128]{1,0:T(8,128)S(1)}, f32[48,128]{1,0:T(8,128)S(1)}, u32[]{:S(2)}, u32[]{:S(2)}) %collective-permute-start.15) | collective-permute-done | bytes 24608 | tf_op jit(solution)/shard_map/ppermute | solution.py:614
  438.9 6.8 %collective-permute-done.16 = f32[48,128]{1,0:T(8,128)S(1)} collective-permute-done((f32[48,128]{1,0:T(8,128)S(1)}, f32[48,128]{1,0:T(8,128)S(1)}, u32[]{:S(2)}, u32[]{:S(2)}) %collective-permute-start.16) | collective-permute-done | bytes 24608 | tf_op jit(solution)/shard_map/ppermute | solution.py:614
  454.7 2.7 copy.225
  (214 shorter events, 64.4 us)
Async XLA Ops:
  4.8 27.6 %collective-permute-start.2 = (bf16[48,2560]{1,0:T(8,128)(2,1)S(1)}, bf16[48,2560]{1,0:T(8,128)(2,1)S(1)}, u32[]{:S(2)}, u32[]{:S(2)}) collective-permute-start(bf16[48,2560]{1,0:T(8,128)(2,1)S(1)} %pad_dynamic-update-slice_fusion), channel_id=1, source_target_pairs={{0,0},{1,2},{2,1},{3,3},{4,4},{5,6},{6,5},{7,7},{8,8},{9,10},{10,9... | collective-permute-start | bytes 737288 | tf_op jit(solution)/shard_map/ppermute | solution.py:561
  11.5 80.9 %collective-permute-start = (f32[8,768]{1,0:T(8,128)}, f32[8,768]{1,0:T(8,128)}, u32[]{:S(2)}, u32[]{:S(2)}) collective-permute-start(f32[8,768]{1,0:T(8,128)} %maximum_maximum_fusion), channel_id=1, source_target_pairs={{0,0},{1,2},{2,1},{3,3},{4,4},{5,6},{6,5},{7,7},{8,8},{9,10},{10,9... | collective-permute-start | bytes 73736 | tf_op jit(solution)/shard_map/ppermute | solution.py:561
  24.7 69.8 %all-to-all-start = ((bf16[16,64,768]{2,1,0:T(8,128)(2,1)}), bf16[16,64,768]{2,1,0:T(8,128)(2,1)S(1)}, u32[]{:S(2)}, u32[]{:S(2)}) async-start(bf16[16,64,768]{2,1,0:T(8,128)(2,1)} %shard_map.263), calls=%async_computation | async-start | bytes 3145728 | tf_op jit(solution)/shard_map/all_to_all | solution.py:669
  32.5 48.1 %collective-permute-start.3 = (bf16[48,2560]{1,0:T(8,128)(2,1)S(1)}, bf16[48,2560]{1,0:T(8,128)(2,1)S(1)}, u32[]{:S(2)}, u32[]{:S(2)}) collective-permute-start(bf16[48,2560]{1,0:T(8,128)(2,1)S(1)} %collective-permute-done.2), channel_id=1, source_target_pairs={{0,8},{8,16},{16,24},{24,0},{1,9},{9,17},{17,25},{25,1},{2,10},{10... | collective-permute-start | bytes 737288 | tf_op jit(solution)/shard_map/ppermute | solution.py:574
  33.7 52.2 %collective-permute-start.4 = (bf16[48,2560]{1,0:T(8,128)(2,1)S(1)}, bf16[48,2560]{1,0:T(8,128)(2,1)S(1)}, u32[]{:S(2)}, u32[]{:S(2)}) collective-permute-start(bf16[48,2560]{1,0:T(8,128)(2,1)S(1)} %collective-permute-done.2), channel_id=1, source_target_pairs={{0,16},{8,24},{16,0},{24,8},{1,17},{9,25},{17,1},{25,9},{2,18},{10... | collective-permute-start | bytes 737288 | tf_op jit(solution)/shard_map/ppermute | solution.py:574
  34.7 52.5 %collective-permute-start.5 = (bf16[48,2560]{1,0:T(8,128)(2,1)S(1)}, bf16[48,2560]{1,0:T(8,128)(2,1)S(1)}, u32[]{:S(2)}, u32[]{:S(2)}) collective-permute-start(bf16[48,2560]{1,0:T(8,128)(2,1)S(1)} %collective-permute-done.2), channel_id=1, source_target_pairs={{0,24},{8,0},{16,8},{24,16},{1,25},{9,1},{17,9},{25,17},{2,26},{10... | collective-permute-start | bytes 737288 | tf_op jit(solution)/shard_map/ppermute | solution.py:574
  36.1 55.7 %copy-start.20 = (f32[768]{0:T(1024)S(1)}, f32[768]{0:T(1024)}, u32[]{:S(2)}) copy-start(f32[768]{0:T(1024)} %param.20) | copy-start | bytes 9220
  88.1 11.4 %collective-permute-start.6 = (bf16[4,48,1280]{2,1,0:T(8,128)(2,1)}, bf16[4,48,1280]{2,1,0:T(8,128)(2,1)S(1)}, u32[]{:S(2)}, u32[]{:S(2)}) collective-permute-start(bf16[4,48,1280]{2,1,0:T(8,128)(2,1)} %get-tuple-element.186), channel_id=1, source_target_pairs={{0,4},{4,0},{1,5},{5,1},{2,6},{6,2},{3,7},{7,3},{8,12},{12,8},{9,1... | collective-permute-start | bytes 1474568 | tf_op jit(solution)/shard_map/ppermute | solution.py:557
  89.4 10.9 %collective-permute-start.8 = (bf16[4,48,1280]{2,1,0:T(8,128)(2,1)S(1)}, bf16[4,48,1280]{2,1,0:T(8,128)(2,1)}, u32[]{:S(2)}, u32[]{:S(2)}) collective-permute-start(bf16[4,48,1280]{2,1,0:T(8,128)(2,1)S(1)} %get-tuple-element.187), channel_id=1, source_target_pairs={{0,1},{1,0},{2,3},{3,2},{4,5},{5,4},{6,7},{7,6},{8,9},{9,8},{10,11... | collective-permute-start | bytes 1474568 | tf_op jit(solution)/shard_map/ppermute | solution.py:557
  94.5 57.5 %copy-start = (bf16[16,64,768]{2,1,0:T(8,128)(2,1)}, bf16[16,64,768]{2,1,0:T(8,128)(2,1)S(1)}, u32[]{:S(2)}) copy-start(bf16[16,64,768]{2,1,0:T(8,128)(2,1)S(1)} %all-to-all-done.xa) | copy-start | bytes 4718596
  94.5 51.5 %all-to-all-start.1 = ((bf16[16,64,768]{2,1,0:T(8,128)(2,1)}), bf16[16,64,768]{2,1,0:T(8,128)(2,1)}, u32[]{:S(2)}, u32[]{:S(2)}) async-start(bf16[16,64,768]{2,1,0:T(8,128)(2,1)} %bitcast.165), calls=%async_computation.1 | async-start | bytes 3145728 | tf_op jit(solution)/shard_map/all_to_all | solution.py:672
  103.4 33.1 %copy-start.6 = (bf16[1,4,48,1280]{3,2,1,0:T(8,128)(2,1)S(1)}, bf16[1,4,48,1280]{3,2,1,0:T(8,128)(2,1)}, u32[]{:S(2)}) copy-start(bf16[1,4,48,1280]{3,2,1,0:T(8,128)(2,1)} %copy-done.5) | copy-start | bytes 1474564
  103.4 33.1 %collective-permute-start.7 = (bf16[2,4,48,1280]{3,2,1,0:T(8,128)(2,1)}, bf16[2,4,48,1280]{3,2,1,0:T(8,128)(2,1)}, u32[]{:S(2)}, u32[]{:S(2)}) collective-permute-start(bf16[2,4,48,1280]{3,2,1,0:T(8,128)(2,1)} %pad_maximum_fusion.2), channel_id=1, source_target_pairs={{0,1},{1,0},{2,3},{3,2},{4,5},{5,4},{6,7},{7,6},{8,9},{9,8},{10,11... | collective-permute-start | bytes 2949128 | tf_op jit(solution)/shard_map/ppermute | solution.py:557
  104.6 31.9 %copy-start.8 = (bf16[1,4,48,1280]{3,2,1,0:T(8,128)(2,1)S(1)}, bf16[1,4,48,1280]{3,2,1,0:T(8,128)(2,1)}, u32[]{:S(2)}) copy-start(bf16[1,4,48,1280]{3,2,1,0:T(8,128)(2,1)} %copy-done.7) | copy-start | bytes 1474564
  109.7 34.0 %collective-permute-start.9 = (bf16[2,4,48,1280]{3,2,0,1:T(8,128)(2,1)}, bf16[2,4,48,1280]{3,2,0,1:T(8,128)(2,1)}, u32[]{:S(2)}, u32[]{:S(2)}) collective-permute-start(bf16[2,4,48,1280]{3,2,0,1:T(8,128)(2,1)} %pad_maximum_fusion.3), channel_id=1, source_target_pairs={{0,4},{4,0},{1,5},{5,1},{2,6},{6,2},{3,7},{7,3},{8,12},{12,8},{9,1... | collective-permute-start | bytes 2949128 | tf_op jit(solution)/shard_map/ppermute | solution.py:557
  139.2 13.1 %collective-permute-start.10 = (bf16[16,64,768]{2,1,0:T(8,128)(2,1)S(1)}, bf16[16,64,768]{2,1,0:T(8,128)(2,1)}, u32[]{:S(2)}, u32[]{:S(2)}) collective-permute-start(bf16[16,64,768]{2,1,0:T(8,128)(2,1)S(1)} %all-to-all-done.xa), channel_id=1, source_target_pairs={{0,2},{2,0},{1,3},{3,1},{4,6},{6,4},{5,7},{7,5},{8,10},{10,8},{9,1... | collective-permute-start | bytes 4718600 | tf_op jit(solution)/shard_map/ppermute | solution.py:557
  146.0 34.4 %collective-permute-start.1 = (bf16[16,64,768]{2,1,0:T(8,128)(2,1)}, bf16[16,64,768]{2,1,0:T(8,128)(2,1)}, u32[]{:S(2)}, u32[]{:S(2)}) collective-permute-start(bf16[16,64,768]{2,1,0:T(8,128)(2,1)} %all-to-all-done.1.dya), channel_id=1, source_target_pairs={{0,2},{2,0},{1,3},{3,1},{4,6},{6,4},{5,7},{7,5},{8,10},{10,8},{9,1... | collective-permute-start | bytes 4718600 | tf_op jit(solution)/shard_map/ppermute | solution.py:557
  266.5 51.8 %copy-start.14 = (bf16[4,2,2,48,384]{4,3,2,1,0:T(8,128)(2,1)}, bf16[4,2,2,48,384]{4,3,2,1,0:T(8,128)(2,1)S(1)}, u32[]{:S(2)}) copy-start(bf16[4,2,2,48,384]{4,3,2,1,0:T(8,128)(2,1)S(1)} %get-tuple-element.180) | copy-start | bytes 1769476
  318.2 17.9 %collective-permute-start.12 = (bf16[16,64,768]{2,1,0:T(8,128)(2,1)}, bf16[16,64,768]{2,1,0:T(8,128)(2,1)}, u32[]{:S(2)}, u32[]{:S(2)}) collective-permute-start(bf16[16,64,768]{2,1,0:T(8,128)(2,1)} %get-tuple-element.60), channel_id=1, source_target_pairs={{0,2},{2,0},{1,3},{3,1},{4,6},{6,4},{5,7},{7,5},{8,10},{10,8},{9,1... | collective-permute-start | bytes 4718600 | tf_op jit(solution)/shard_map/ppermute | solution.py:557
  320.6 9.5 %copy-start.3 = (bf16[4,2,2,48,928]{4,3,2,1,0:T(8,128)(2,1)}, bf16[4,2,2,48,928]{4,3,2,1,0:T(8,128)(2,1)S(1)}, u32[]{:S(2)}) copy-start(bf16[4,2,2,48,928]{4,3,2,1,0:T(8,128)(2,1)S(1)} %slice.164) | copy-start | bytes 4276228
  320.7 10.5 %collective-permute-start.20 = (bf16[4,2,48,384]{3,2,1,0:T(8,128)(2,1)}, bf16[4,2,48,384]{3,2,1,0:T(8,128)(2,1)}, u32[]{:S(2)}, u32[]{:S(2)}) collective-permute-start(bf16[4,2,48,384]{3,2,1,0:T(8,128)(2,1)} %dynamic-slice_bitcast_fusion.3), channel_id=1, source_target_pairs={{0,1},{1,0},{2,3},{3,2},{4,5},{5,4},{6,7},{7,6},{8,9},{9,8},{10,11... | collective-permute-start | bytes 884744 | tf_op jit(solution)/shard_map/ppermute | solution.py:557
  323.0 10.9 %collective-permute-start.18 = (bf16[4,2,48,384]{3,2,0,1:T(8,128)(2,1)}, bf16[4,2,48,384]{3,2,0,1:T(8,128)(2,1)}, u32[]{:S(2)}, u32[]{:S(2)}) collective-permute-start(bf16[4,2,48,384]{3,2,0,1:T(8,128)(2,1)} %bitcast.158), channel_id=1, source_target_pairs={{0,4},{4,0},{1,5},{5,1},{2,6},{6,2},{3,7},{7,3},{8,12},{12,8},{9,1... | collective-permute-start | bytes 884744 | tf_op jit(solution)/shard_map/ppermute | solution.py:557
  325.6 26.0 %collective-permute-start.25 = (bf16[4,2,48,768]{3,2,0,1:T(8,128)(2,1)}, bf16[4,2,48,768]{3,2,0,1:T(8,128)(2,1)}, u32[]{:S(2)}, u32[]{:S(2)}) collective-permute-start(bf16[4,2,48,768]{3,2,0,1:T(8,128)(2,1)} %bitcast.157), channel_id=1, source_target_pairs={{0,4},{4,0},{1,5},{5,1},{2,6},{6,2},{3,7},{7,3},{8,12},{12,8},{9,1... | collective-permute-start | bytes 1769480 | tf_op jit(solution)/shard_map/ppermute | solution.py:557
  327.4 8.6 %copy-start.1 = (bf16[16,64,768]{2,1,0:T(8,128)(2,1)S(1)}, bf16[16,64,768]{2,1,0:T(8,128)(2,1)}, u32[]{:S(2)}) copy-start(bf16[16,64,768]{2,1,0:T(8,128)(2,1)} %copy-done) | copy-start | bytes 4718596
  328.8 6.2 %copy-start.18 = (bf16[4,1,2,48,384]{4,3,2,1,0:T(8,128)(2,1)S(1)}, bf16[4,1,2,48,384]{4,3,2,1,0:T(8,128)(2,1)}, u32[]{:S(2)}) copy-start(bf16[4,1,2,48,384]{4,3,2,1,0:T(8,128)(2,1)} %get-tuple-element.193) | copy-start | bytes 884740
  328.8 10.9 %collective-permute-start.11 = (bf16[16,64,768]{2,1,0:T(8,128)(2,1)}, bf16[16,64,768]{2,1,0:T(8,128)(2,1)S(1)}, u32[]{:S(2)}, u32[]{:S(2)}) collective-permute-start(bf16[16,64,768]{2,1,0:T(8,128)(2,1)} %get-tuple-element.46), channel_id=1, source_target_pairs={{0,2},{2,0},{1,3},{3,1},{4,6},{6,4},{5,7},{7,5},{8,10},{10,8},{9,1... | collective-permute-start | bytes 4718600 | tf_op jit(solution)/shard_map/ppermute | solution.py:557
  331.1 22.2 %collective-permute-start.27 = (bf16[4,2,48,928]{3,2,1,0:T(8,128)(2,1)}, bf16[4,2,48,928]{3,2,1,0:T(8,128)(2,1)}, u32[]{:S(2)}, u32[]{:S(2)}) collective-permute-start(bf16[4,2,48,928]{3,2,1,0:T(8,128)(2,1)} %dynamic-slice_bitcast_fusion), channel_id=1, source_target_pairs={{0,1},{1,0},{2,3},{3,2},{4,5},{5,4},{6,7},{7,6},{8,9},{9,8},{10,11... | collective-permute-start | bytes 2138120 | tf_op jit(solution)/shard_map/ppermute | solution.py:557
  333.8 16.9 %collective-permute-start.21 = (bf16[4,48,384]{2,1,0:T(8,128)(2,1)}, bf16[4,48,384]{2,1,0:T(8,128)(2,1)}, u32[]{:S(2)}, u32[]{:S(2)}) collective-permute-start(bf16[4,48,384]{2,1,0:T(8,128)(2,1)} %dynamic-slice_bitcast_fusion.7), channel_id=1, source_target_pairs={{0,4},{4,0},{1,5},{5,1},{2,6},{6,2},{3,7},{7,3},{8,12},{12,8},{9,1... | collective-permute-start | bytes 442376 | tf_op jit(solution)/shard_map/ppermute | solution.py:557
  344.5 6.2 %copy-start.17 = (bf16[4,2,48,384]{3,2,1,0:T(8,128)(2,1)S(1)}, bf16[4,2,48,384]{3,2,1,0:T(8,128)(2,1)}, u32[]{:S(2)}) copy-start(bf16[4,2,48,384]{3,2,1,0:T(8,128)(2,1)} %copy-done.16) | copy-start | bytes 884740
  344.5 7.2 %copy-start.13 = (bf16[4,1,2,48,768]{4,3,2,1,0:T(8,128)(2,1)S(1)}, bf16[4,1,2,48,768]{4,3,2,1,0:T(8,128)(2,1)}, u32[]{:S(2)}) copy-start(bf16[4,1,2,48,768]{4,3,2,1,0:T(8,128)(2,1)} %get-tuple-element.182) | copy-start | bytes 1769476
  344.5 61.2 %all-to-all-start.2 = ((bf16[16,64,768]{2,1,0:T(8,128)(2,1)}), bf16[16,64,768]{2,1,0:T(8,128)(2,1)S(1)}, u32[]{:S(2)}, u32[]{:S(2)}) async-start(bf16[16,64,768]{2,1,0:T(8,128)(2,1)} %get-tuple-element.175), calls=%async_computation.2 | async-start | bytes 3145728 | tf_op jit(solution)/shard_map/all_to_all | solution.py:684
  349.5 14.5 %collective-permute-start.19 = (bf16[4,48,384]{2,1,0:T(8,128)(2,1)S(1)}, bf16[4,48,384]{2,1,0:T(8,128)(2,1)S(1)}, u32[]{:S(2)}, u32[]{:S(2)}) collective-permute-start(bf16[4,48,384]{2,1,0:T(8,128)(2,1)S(1)} %dynamic-slice_bitcast_fusion.8), channel_id=1, source_target_pairs={{0,1},{1,0},{2,3},{3,2},{4,5},{5,4},{6,7},{7,6},{8,9},{9,8},{10,11... | collective-permute-start | bytes 442376 | tf_op jit(solution)/shard_map/ppermute | solution.py:557
  352.9 22.3 %collective-permute-start.26 = (bf16[4,48,768]{2,1,0:T(8,128)(2,1)S(1)}, bf16[4,48,768]{2,1,0:T(8,128)(2,1)S(1)}, u32[]{:S(2)}, u32[]{:S(2)}) collective-permute-start(bf16[4,48,768]{2,1,0:T(8,128)(2,1)S(1)} %dynamic-slice_bitcast_fusion.2), channel_id=1, source_target_pairs={{0,1},{1,0},{2,3},{3,2},{4,5},{5,4},{6,7},{7,6},{8,9},{9,8},{10,11... | collective-permute-start | bytes 884744 | tf_op jit(solution)/shard_map/ppermute | solution.py:557
  354.8 20.5 %collective-permute-start.28 = (bf16[4,48,928]{2,1,0:T(8,128)(2,1)S(1)}, bf16[4,48,928]{2,1,0:T(8,128)(2,1)S(1)}, u32[]{:S(2)}, u32[]{:S(2)}) collective-permute-start(bf16[4,48,928]{2,1,0:T(8,128)(2,1)S(1)} %dynamic-slice_bitcast_fusion.1), channel_id=1, source_target_pairs={{0,4},{4,0},{1,5},{5,1},{2,6},{6,2},{3,7},{7,3},{8,12},{12,8},{9,1... | collective-permute-start | bytes 1069064 | tf_op jit(solution)/shard_map/ppermute | solution.py:557
  375.6 22.1 %collective-permute-start.29 = (bf16[48,1696]{1,0:T(8,128)(2,1)S(1)}, bf16[48,1696]{1,0:T(8,128)(2,1)S(1)}, u32[]{:S(2)}, u32[]{:S(2)}) collective-permute-start(bf16[48,1696]{1,0:T(8,128)(2,1)S(1)} %get-tuple-element.188), channel_id=1, source_target_pairs={{0,8},{8,16},{16,24},{24,0},{1,9},{9,17},{17,25},{25,1},{2,10},{10... | collective-permute-start | bytes 488456 | tf_op jit(solution)/shard_map/ppermute | solution.py:604
  376.3 25.1 %collective-permute-start.30 = (bf16[48,1696]{1,0:T(8,128)(2,1)S(1)}, bf16[48,1696]{1,0:T(8,128)(2,1)S(1)}, u32[]{:S(2)}, u32[]{:S(2)}) collective-permute-start(bf16[48,1696]{1,0:T(8,128)(2,1)S(1)} %get-tuple-element.190), channel_id=1, source_target_pairs={{0,16},{8,24},{16,0},{24,8},{1,17},{9,25},{17,1},{25,9},{2,18},{10... | collective-permute-start | bytes 488456 | tf_op jit(solution)/shard_map/ppermute | solution.py:604
  377.7 25.4 %collective-permute-start.31 = (bf16[48,1696]{1,0:T(8,128)(2,1)S(1)}, bf16[48,1696]{1,0:T(8,128)(2,1)S(1)}, u32[]{:S(2)}, u32[]{:S(2)}) collective-permute-start(bf16[48,1696]{1,0:T(8,128)(2,1)S(1)} %get-tuple-element.189), channel_id=1, source_target_pairs={{0,24},{8,0},{16,8},{24,16},{1,25},{9,1},{17,9},{25,17},{2,26},{10... | collective-permute-start | bytes 488456 | tf_op jit(solution)/shard_map/ppermute | solution.py:604
  379.1 31.3 %collective-permute-start.22 = (bf16[48,768]{1,0:T(8,128)(2,1)S(1)}, bf16[48,768]{1,0:T(8,128)(2,1)S(1)}, u32[]{:S(2)}, u32[]{:S(2)}) collective-permute-start(bf16[48,768]{1,0:T(8,128)(2,1)S(1)} %get-tuple-element.195), channel_id=1, source_target_pairs={{0,8},{8,16},{16,24},{24,0},{1,9},{9,17},{17,25},{25,1},{2,10},{10... | collective-permute-start | bytes 221192 | tf_op jit(solution)/shard_map/ppermute | solution.py:604
  379.3 31.2 %collective-permute-start.23 = (bf16[48,768]{1,0:T(8,128)(2,1)S(1)}, bf16[48,768]{1,0:T(8,128)(2,1)S(1)}, u32[]{:S(2)}, u32[]{:S(2)}) collective-permute-start(bf16[48,768]{1,0:T(8,128)(2,1)S(1)} %get-tuple-element.197), channel_id=1, source_target_pairs={{0,16},{8,24},{16,0},{24,8},{1,17},{9,25},{17,1},{25,9},{2,18},{10... | collective-permute-start | bytes 221192 | tf_op jit(solution)/shard_map/ppermute | solution.py:604
  397.7 12.8 %collective-permute-start.24 = (bf16[48,768]{1,0:T(8,128)(2,1)S(1)}, bf16[48,768]{1,0:T(8,128)(2,1)S(1)}, u32[]{:S(2)}, u32[]{:S(2)}) collective-permute-start(bf16[48,768]{1,0:T(8,128)(2,1)S(1)} %get-tuple-element.196), channel_id=1, source_target_pairs={{0,24},{8,0},{16,8},{24,16},{1,25},{9,1},{17,9},{25,17},{2,26},{10... | collective-permute-start | bytes 221192 | tf_op jit(solution)/shard_map/ppermute | solution.py:604
  403.2 7.4 %collective-permute-start.32 = (f32[48,128]{1,0:T(8,128)S(1)}, f32[48,128]{1,0:T(8,128)S(1)}, u32[]{:S(2)}, u32[]{:S(2)}) collective-permute-start(f32[48,128]{1,0:T(8,128)S(1)} %slice.166), channel_id=1, source_target_pairs={{0,2},{2,0},{1,3},{3,1},{4,6},{6,4},{5,7},{7,5},{8,10},{10,8},{9,1... | collective-permute-start | bytes 73736 | tf_op jit(solution)/shard_map/ppermute | solution.py:557
  405.7 47.8 %all-to-all-start.3 = ((bf16[16,64,768]{2,1,0:T(8,128)(2,1)}), bf16[16,64,768]{2,1,0:T(8,128)(2,1)}, u32[]{:S(2)}, u32[]{:S(2)}) async-start(bf16[16,64,768]{2,1,0:T(8,128)(2,1)} %get-tuple-element.174), calls=%async_computation.3 | async-start | bytes 3145728 | tf_op jit(solution)/shard_map/all_to_all | solution.py:695
  410.7 6.6 %collective-permute-start.13 = (f32[48,128]{1,0:T(8,128)S(1)}, f32[48,128]{1,0:T(8,128)S(1)}, u32[]{:S(2)}, u32[]{:S(2)}) collective-permute-start(f32[48,128]{1,0:T(8,128)S(1)} %pad_bitcast_fusion), channel_id=1, source_target_pairs={{0,4},{4,0},{1,5},{5,1},{2,6},{6,2},{3,7},{7,3},{8,12},{12,8},{9,1... | collective-permute-start | bytes 73736 | tf_op jit(solution)/shard_map/ppermute | solution.py:557
  412.0 14.6 %collective-permute-start.33 = (bf16[48,2464]{1,0:T(8,128)(2,1)S(1)}, bf16[48,2464]{1,0:T(8,128)(2,1)S(1)}, u32[]{:S(2)}, u32[]{:S(2)}) collective-permute-start(bf16[48,2464]{1,0:T(8,128)(2,1)S(1)} %pad_maximum_fusion.5), channel_id=1, source_target_pairs={{0,0},{1,2},{2,1},{3,3},{4,4},{5,6},{6,5},{7,7},{8,8},{9,10},{10,9... | collective-permute-start | bytes 709640 | tf_op jit(solution)/shard_map/ppermute | solution.py:561
  417.3 9.7 %collective-permute-start.14 = (f32[48,128]{1,0:T(8,128)S(1)}, f32[48,128]{1,0:T(8,128)S(1)}, u32[]{:S(2)}, u32[]{:S(2)}) collective-permute-start(f32[48,128]{1,0:T(8,128)S(1)} %fusion.32), channel_id=1, source_target_pairs={{0,1},{1,0},{2,3},{3,2},{4,5},{5,4},{6,7},{7,6},{8,9},{9,8},{10,11... | collective-permute-start | bytes 73736 | tf_op jit(solution)/shard_map/ppermute | solution.py:557
  426.9 11.9 %collective-permute-start.15 = (f32[48,128]{1,0:T(8,128)S(1)}, f32[48,128]{1,0:T(8,128)S(1)}, u32[]{:S(2)}, u32[]{:S(2)}) collective-permute-start(f32[48,128]{1,0:T(8,128)S(1)} %fusion.40), channel_id=1, source_target_pairs={{0,8},{8,0},{16,24},{24,16},{1,9},{9,1},{17,25},{25,17},{2,10},{10... | collective-permute-start | bytes 73736 | tf_op jit(solution)/shard_map/ppermute | solution.py:614
  438.8 6.9 %collective-permute-start.16 = (f32[48,128]{1,0:T(8,128)S(1)}, f32[48,128]{1,0:T(8,128)S(1)}, u32[]{:S(2)}, u32[]{:S(2)}) collective-permute-start(f32[48,128]{1,0:T(8,128)S(1)} %add.246), channel_id=1, source_target_pairs={{0,16},{8,24},{16,0},{24,8},{1,17},{9,25},{17,1},{25,9},{2,18},{10... | collective-permute-start | bytes 73736 | tf_op jit(solution)/shard_map/ppermute | solution.py:614
  445.7 4.2 collective-permute-start.17
  (18 other events, 55.2 us)

commit v2 on v1

--- a/solution.py
+++ b/solution.py
@@ -12,6 +12,7 @@
 CH = 128
 BLK = 256
 ZR = 32
+MT = False
 HIGH = lax.Precision.HIGHEST
 VMEM_LIMIT = 60 * 1024 * 1024
 
@@ -70,10 +71,27 @@
     return dt * mask, a, cs
 
 
-def enter(meta, xa, xb, w, gain, taps, bias, alog, nrm, gate, ain, u, zt, sf, wt, halo, state, vfe):
+def block_row(meta, k, dx, dy, sign):
+    n = meta[5]
+    z = lax.rem(meta[2] + sign * k + n, n)
+    return (z * 2 + (meta[3] ^ dx)) * 2 + (meta[4] ^ dy)
+
+
+def put_rows(w, meta, ref, first, count, dx, dy):
+    if count == 0:
+        w[...] = ref[...]
+        return
+    rows = ref.shape[1]
+    for i in range(count):
+        at = pl.multiple_of(block_row(meta, first + i, dx, dy, -1) * rows, 16)
+        w[pl.ds(at, rows), :] = ref[i]
+
+
+def enter(near, meta, xa, xb, *refs):
+    pieces, refs = refs[: len(near)], refs[len(near) :]
+    gain, taps, bias, alog, nrm, gate, ain, u, zt, sf, wt, wo, halo, state, vfe, w = refs
     j = pl.program_id(0)
     core, length = meta[0], meta[1]
-    dm = w.shape[0]
     inner = gate.shape[0]
     heads = inner // 64
     cat = inner + 2 * 64
@@ -81,6 +99,9 @@
 
     @pl.when(j == 0)
     def _():
+        for ref, (first, count, dx, dy) in zip(pieces, near):
+            put_rows(w, meta, ref, first, count, dx, dy)
+        wo[...] = w[:, 0:inner].T
         wt[0 : 2 * inner + 128, :] = w[:, inner : 3 * inner + 128].T
         wt[2 * inner + 128 : 2 * inner + 128 + ZR, :] = w[:, 3 * inner + 128 : 3 * inner + 256].T[0:ZR]
         halo[...] = jnp.zeros_like(halo)
@@ -124,7 +145,32 @@
             state[hs, :] = state[hs, :] * etot[h : h + 1, :] + add[hs, :]
 
 
-def mix(meta, dskip, dya, dyb, wot, gate, u, zt, sf, gain, alog, own, oth, dgate, dxp, ddt, dap, dbc, zb, sbin, gwo, dgain, dsk, wo, gacc, gy, ynt, yin, dv, dye, vfe, vbe, sb, dsf, rows):
+def send_rows(meta, src, outs):
+    if len(outs) == 1:
+        outs[0][...] = src[...]
+        return
+    rows = outs[0].shape[2]
+    ahead, behind = outs[0].shape[1], outs[2].shape[1]
+    for other in range(2):
+        for k in range(ahead):
+            for ref, dx in ((outs[0], 1), (outs[1], 0)):
+                at = pl.multiple_of(block_row(meta, k, dx, other, 1) * rows, 16)
+                ref[other, k] = src[pl.ds(at, rows), :].astype(BF)
+        for k in range(behind):
+            for ref, dy in ((outs[2], 1), (outs[3], 0)):
+                at = pl.multiple_of(block_row(meta, ahead + k, other, dy, 1) * rows, 16)
+                ref[other, k] = src[pl.ds(at, rows), :].astype(BF)
+
+
+def message_shapes(plan, dm, cols):
+    if plan is None:
+        return [sds((dm, cols), F32)]
+    ahead, behind, rows = plan
+    return [sds((2, n, rows, cols), BF) for n in (ahead, ahead, behind, behind)]
+
+
+def mix(meta, dskip, dya, dyb, wo, gate, u, zt, sf, gain, alog, own, oth, dgate, dxp, ddt, dap, dbc, zb, sbin, dgain, dsk, *refs):
+    *gwo, gacc, gy, ynt, yin, dv, dye, vfe, vbe, sb, dsf, rows, xs, yfs, ybs, dys, mls, mus, pds = refs
     i = pl.program_id(0)
     last = pl.num_programs(0) - 1
     j = last - i
@@ -134,7 +180,6 @@
 
     @pl.when(i == 0)
     def _():
-        wo[...] = wot[...].T
         gacc[...] = jnp.zeros_like(gacc)
         sb[...] = jnp.zeros_like(sb)
         dsf[...] = jnp.zeros_like(dsf)
@@ -171,30 +216,47 @@
         gmat = tn(ct, bt)
         glow = jnp.where(low, gmat, 0.0)
         gup = jnp.where(up, gmat, 0.0)
+        gmat = tn(bt, ct)
+        tlow = jnp.where(up, gmat, 0.0)
+        tup = jnp.where(low, gmat, 0.0)
         sbb = sb[...].astype(BF)
         sbin[q] = sbb
         dsb = dsf[...].astype(BF)
         yin[0:inner, :] = nn(sf[q], ct)
         yin[inner : 2 * inner, :] = nn(sbb, ct)
         dv[...] = nn(dsb, bt)
-        dg_sum = jnp.zeros((CH, CH), F32)
         for h in range(heads):
             hs = slice(64 * h, 64 * h + 64)
             h1 = slice(h, h + 1)
             uh = u[hs, lanes]
             x = uh * sigmoid(uh)
+            xs[hs, :] = x
             mf = mdt[h : h + 1, :]
             mb = mdt[16 + h : 17 + h, :]
-            vf = x * mf
-            vb = x * mb
-            vf16 = vf.astype(BF)
-            vb16 = vb.astype(BF)
+            vf16 = (x * mf).astype(BF)
+            vb16 = (x * mb).astype(BF)
             pm = jnp.exp(jnp.where(low, ccf[:, h1] - csf[h1, :], ecb[h1, :] - ccb[:, h1]))
             ml = (pm * glow).astype(BF)
             mu = (pm * gup).astype(BF)
+            mls[h] = ml
+            mus[h] = mu
+            pds[h] = pm * jnp.where(low, mf, mb)
+            if MT:
+                pt = jnp.exp(jnp.where(up, csf[h1, :] - ccf[:, h1], ccb[:, h1] - ecb[h1, :]))
+                ml = (pt * tlow).astype(BF)
+                mu = (pt * tup).astype(BF)
+                yfs[hs, :] = nn(vf16, ml) + yin[hs, :] * ef[h1, :]
+                ybs[hs, :] = nn(vb16, mu)
+            else:
+                yfs[hs, :] = nt(vf16, ml) + yin[hs, :] * ef[h1, :]
+                ybs[hs, :] = nt(vb16, mu)
+        for h in range(heads):
+            hs = slice(64 * h, 64 * h + 64)
+            h1 = slice(h, h + 1)
+            x = xs[hs, :]
             ybi = yin[inner + 64 * h : inner + 64 * h + 64, :] * eb[h1, :]
-            yf = nt(vf16, ml) + yin[hs, :] * ef[h1, :]
-            yb = nt(vb16, mu) + ybi
+            yf = yfs[hs, :]
+            yb = ybs[hs, :] + ybi
             yt = yf + yb + dskip[h] * x
             gt = gate[hs, lanes]
             sg = sigmoid(gt)
@@ -211,27 +273,38 @@
             dgate[hs, lanes] = (dg * yt * (sg * (1.0 + gt * (1.0 - sg)))).astype(BF)
             dy = dg * sl
             dyb16 = dy.astype(BF)
+            dys[hs, :] = dyb16
+            dyr = dyb16.astype(F32)
+            rows[2, h1, :] = jnp.sum(dyr * yf, axis=0, keepdims=True)
+            rows[3, h1, :] = -jnp.sum(dyr * yb, axis=0, keepdims=True)
+            rows[5, h1, :] = jnp.sum(dyr * ybi, axis=0, keepdims=True)
+            dsk[h1, :] += jnp.sum(dy * x, axis=0, keepdims=True)
+            dxp[hs, lanes] = dskip[h] * dy
+            dye[hs, :] = (dy * ef[h1, :]).astype(BF)
+            dye[inner + 64 * h : inner + 64 * h + 64, :] = (dy * eb[h1, :]).astype(BF)
+        dg_sum = jnp.zeros((CH, CH), F32)
+        for h in range(heads):
+            hs = slice(64 * h, 64 * h + 64)
+            h1 = slice(h, h + 1)
+            x = xs[hs, :]
+            mf = mdt[h : h + 1, :]
+            mb = mdt[16 + h : 17 + h, :]
+            vf = x * mf
+            vb = x * mb
+            vfr = vf.astype(BF).astype(F32)
+            dyb16 = dys[hs, :]
             dvi = dv[hs, :] * wf[h1, :]
-            dvf = nn(dyb16, ml) + dvi
-            dvb = nn(dyb16, mu)
-            dyr = dyb16.astype(F32)
-            vfr = vf16.astype(F32)
-            qm = tn(dyb16, x.astype(BF))
-            dg_sum = dg_sum + qm * pm * jnp.where(low, mf, mb)
-            sxf = jnp.sum(x * dvf, axis=0, keepdims=True)
-            sxb = jnp.sum(x * dvb, axis=0, keepdims=True)
-            rows[0, h1, :] = sxf
-            rows[1, h1, :] = sxb
-            rows[2, h1, :] = jnp.sum(dyr * yf - vfr * dvf, axis=0, keepdims=True)
-            rows[3, h1, :] = jnp.sum(vb16.astype(F32) * dvb - dyr * yb, axis=0, keepdims=True)
+            dvf = nn(dyb16, mls[h]) + dvi
+            dvb = nn(dyb16, mus[h])
+            dg_sum = dg_sum + tn(dyb16, x.astype(BF)) * pds[h]
+            rows[0, h1, :] = jnp.sum(x * dvf, axis=0, keepdims=True)
+            rows[1, h1, :] = jnp.sum(x * dvb, axis=0, keepdims=True)
+            rows[2, h1, :] += -jnp.sum(vfr * dvf, axis=0, keepdims=True)
+            rows[3, h1, :] += jnp.sum(vb.astype(BF).astype(F32) * dvb, axis=0, keepdims=True)
             prod = jnp.sum(dsf[hs, :] * sf[q, hs, :].astype(F32), axis=0, keepdims=True)
             prod = jnp.sum(prod, axis=1, keepdims=True) * etf[h1, :]
             rows[4, h1, :] = jnp.sum(vfr * dvi, axis=0, keepdims=True) + prod * (1.0 / CH)
-            rows[5, h1, :] = jnp.sum(dyr * ybi, axis=0, keepdims=True)
-            dsk[h1, :] += jnp.sum(dy * x, axis=0, keepdims=True)
-            dxp[hs, lanes] = dskip[h] * dy + mf * dvf + mb * dvb
-            dye[hs, :] = (dy * ef[h1, :]).astype(BF)
-            dye[inner + 64 * h : inner + 64 * h + 64, :] = (dy * eb[h1, :]).astype(BF)
+            dxp[hs, lanes] += mf * dvf + mb * dvb
             vfe[hs, :] = (vf * wf[h1, :]).astype(BF)
             vbe[hs, :] = (vb * wb[h1, :]).astype(BF)
         dgb = jnp.where(low | up, dg_sum, 0.0).astype(BF)
@@ -254,7 +327,8 @@
 
     @pl.when(i == last)
     def _():
-        gwo[...] = gacc[...].T.astype(gwo.dtype)
+        gacc[...] = gacc[...].T
+        send_rows(meta, gacc, gwo)
 
 
 def carry(meta, u, zt, alog, dxp, ddt, dap, dbc, zb, sbin, du, dz, dbias, dal, dsb, dvs, vbe, row):
@@ -315,17 +389,22 @@
         dz[:, lanes] = dzz.astype(dz.dtype)
 
 
-def leave(meta, du, nxt, ain, dgate, dz, nrm, wt, taps, own, oth, gw, dtaps, acc, cat):
+def lane_sums(v):
+    ones = jnp.ones((8, v.shape[1]), F32)
+    return lax.dot_general(ones, v, (((1,), (1,)), ((), ())), precision=HIGH, preferred_element_type=F32)[0:1]
+
+
+def weigh(meta, du, nxt, ain, dgate, dz, nrm, taps, wt, gain, dgain, dbias, dal, dsk, cat, small, *refs):
+    *gw, acc, flat, dtaps = refs
     j = pl.program_id(0)
     last = pl.num_programs(0) - 1
-    core = meta[0]
     inner = dgate.shape[0]
     conv = inner + 128
 
     @pl.when(j == 0)
     def _():
+        dtaps[...] = jnp.zeros_like(dtaps)
         acc[...] = jnp.zeros_like(acc)
-        dtaps[...] = jnp.zeros_like(dtaps)
 
     cat[0:inner, :] = dgate[...]
     for g in range(0, conv, 128):
@@ -344,13 +423,27 @@
             dtaps[3 - k, g : g + 128, :] += p[:, 0:128] + p[:, 128:256]
         cat[inner + g : inner + g + 128, :] = total.astype(BF)
     cat[inner + conv : inner + conv + ZR, :] = dz[...]
-    gn = tn(cat[...], wt[...])
-    split_rows(core, gn, own, oth)
     acc[...] += nn(cat[...], nrm[...])
 
     @pl.when(j == last)
     def _():
-        gw[...] = acc[...].T.astype(gw.dtype)
+        flat[...] = acc[...].T
+        send_rows(meta, flat, gw)
+        small[...] = jnp.zeros_like(small)
+        for k in range(4):
+            small[k : k + 1, :] = lane_sums(dtaps[k])
+        small[4:5, 0:inner] = lane_sums(dgain[...])
+        norm = jnp.zeros((1, nrm.shape[1]), F32)
+        for g in range(0, acc.shape[0], 32):
+            norm = norm + jnp.sum(acc[g : g + 32, :] * wt[g : g + 32, :].astype(F32), axis=0, keepdims=True)
+        small[5:6, 0:inner] = norm / gain[...]
+        for i, ref in enumerate((dbias, dal, dsk)):
+            small[6:7, 128 * i : 128 * i + ref.shape[0]] = lane_sums(ref[...])
+
+
+def leave(meta, cat, wt, own, oth):
+    gn = tn(cat[...], wt[...])
+    split_rows(meta[0], gn, own, oth)
 
 
 def _params():
@@ -365,7 +458,7 @@
     return jax.ShapeDtypeStruct(shape, dt)
 
 
-def run_enter(meta, xa, xb, wpack, gain, taps, bias, alog):
+def run_enter(meta, xa, xb, pieces, near, gain, taps, bias, alog):
     nblk, width, dm = xa.shape
     length = 2 * nblk * width
     inner = taps.shape[0] - 128
@@ -375,11 +468,13 @@
     colb = lambda n: pl.BlockSpec((n, BLK), lambda j, *_: (0, j))
     wrows = 2 * inner + 128 + ZR
     return pl.pallas_call(
-        enter,
+        functools.partial(enter, near),
         grid_spec=pltpu.PrefetchScalarGridSpec(
             num_scalar_prefetch=1,
             grid=(nb,),
-            in_specs=[rowsb, rowsb, full(wpack.shape), full(gain.shape), full(taps.shape), full(bias.shape), full(alog.shape)],
+            in_specs=[rowsb, rowsb]
+            + [full(p.shape) for p in pieces]
+            + [full(gain.shape), full(taps.shape), full(bias.shape), full(alog.shape)],
             out_specs=[
                 pl.BlockSpec((BLK, dm), lambda j, *_: (j, 0)),
                 colb(inner),
@@ -388,11 +483,13 @@
                 colb(ZR),
                 pl.BlockSpec((BLK // CH, inner, 64), lambda j, *_: (j, 0, 0)),
                 full((wrows, dm)),
+                full((inner, dm)),
             ],
             scratch_shapes=[
                 pltpu.VMEM((inner + 128, 128), F32),
                 pltpu.VMEM((inner, 64), F32),
                 pltpu.VMEM((inner, CH), BF),
+                pltpu.VMEM((dm, pieces[0].shape[-1]), BF),
             ],
         ),
         out_shape=[
@@ -403,18 +500,20 @@
             sds((ZR, length), F32),
             sds((length // CH, inner, 64), BF),
             sds((wrows, dm), BF),
+            sds((inner, dm), BF),
         ],
         compiler_params=_params(),
         cost_estimate=pl.CostEstimate(flops=2 * length * dm * wrows, bytes_accessed=30_000_000, transcendentals=4 * inner * length),
-    )(meta, xa, xb, wpack, gain, taps, bias, alog)
-
-
-def run_mix(meta, dskip, dya, dyb, wpack, gate, u, zt, sf, gain, alog):
+    )(meta, xa, xb, *pieces, gain, taps, bias, alog)
+
+
+def run_mix(plan, meta, dskip, dya, dyb, wo, gate, u, zt, sf, gain, alog):
     nblk, width, dm = dya.shape
     length = 2 * nblk * width
     inner = gate.shape[0]
     nk = BLK // (2 * width)
     nb = length // BLK
+    sent = message_shapes(plan, dm, inner)
     rowsb = pl.BlockSpec((nk, width, dm), lambda i, *_: (nb - 1 - i, 0, 0))
     colb = lambda n: pl.BlockSpec((n, BLK), lambda i, *_: (0, nb - 1 - i))
     stb = pl.BlockSpec((BLK // CH, inner, 64), lambda i, *_: (nb - 1 - i, 0, 0))
@@ -423,7 +522,7 @@
         grid_spec=pltpu.PrefetchScalarGridSpec(
             num_scalar_prefetch=2,
             grid=(nb,),
-            in_specs=[rowsb, rowsb, pl.BlockSpec((dm, inner), lambda i, *_: (0, 0)), colb(inner), colb(inner + 128), colb(ZR), stb, full(gain.shape), full(alog.shape)],
+            in_specs=[rowsb, rowsb, full((inner, dm)), colb(inner), colb(inner + 128), colb(ZR), stb, full(gain.shape), full(alog.shape)],
             out_specs=[
                 rowsb,
                 rowsb,
@@ -434,12 +533,11 @@
                 colb(128),
                 stb,
                 stb,
-                full((dm, inner)),
                 full((inner, CH)),
                 full((16, CH)),
-            ],
+            ]
+            + [full(m.shape) for m in sent],
             scratch_shapes=[
-                pltpu.VMEM((inner, dm), BF),
                 pltpu.VMEM((inner, dm), F32),
                 pltpu.VMEM((inner, BLK), F32),
                 pltpu.VMEM((inner, BLK), BF),
@@ -451,6 +549,13 @@
                 pltpu.VMEM((inner, 64), F32),
                 pltpu.VMEM((inner, 64), F32),
                 pltpu.VMEM((6, 16, CH), F32),
+                pltpu.VMEM((inner, CH), F32),
+                pltpu.VMEM((inner, CH), F32),
+                pltpu.VMEM((inner, CH), F32),
+                pltpu.VMEM((inner, CH), BF),
+                pltpu.VMEM((inner // 64, CH, CH), BF),
+                pltpu.VMEM((inner // 64, CH, CH), BF),
+                pltpu.VMEM((inner // 64, CH, CH), F32),
             ],
         ),
         out_shape=[
@@ -463,13 +568,13 @@
             sds((128, length), F32),
             sds((length // CH, inner, 64), BF),
             sds((length // CH, inner, 64), BF),
-            sds((dm, inner), BF),
             sds((inner, CH), F32),
             sds((16, CH), F32),
-        ],
+        ]
+        + sent,
         compiler_params=_params(),
         cost_estimate=pl.CostEstimate(flops=40 * 10**9, bytes_accessed=50_000_000, transcendentals=10**7),
-    )(meta, dskip, dya, dyb, wpack, gate, u, zt, sf, gain, alog)
+    )(meta, dskip, dya, dyb, wo, gate, u, zt, sf, gain, alog)
 
 
 def run_carry(meta, u, zt, alog, dxp, ddt, dap, dbc, zb, sbin):
@@ -497,17 +602,15 @@
     )(meta, u, zt, alog, dxp, ddt, dap, dbc, zb, sbin)
 
 
-def run_leave(meta, du, ain, dgate, dz, nrm, wt, taps, width):
+def run_weigh(plan, meta, du, ain, dgate, dz, nrm, taps, *rest):
     inner, length = dgate.shape
     dm = nrm.shape[1]
     nb = length // BLK
-    nk = BLK // (2 * width)
-    wrows = wt.shape[0]
-    rowsb = pl.BlockSpec((nk, width, dm), lambda j, *_: (j, 0, 0))
+    wrows = 2 * inner + 128 + ZR
+    sent = message_shapes(plan, dm, wrows)
     colb = lambda n: pl.BlockSpec((n, BLK), lambda j, *_: (0, j))
-    nblk = length // (2 * width)
     return pl.pallas_call(
-        leave,
+        weigh,
         grid_spec=pltpu.PrefetchScalarGridSpec(
             num_scalar_prefetch=1,
             grid=(nb,),
@@ -518,37 +621,61 @@
                 colb(inner),
                 colb(ZR),
                 pl.BlockSpec((BLK, dm), lambda j, *_: (j, 0)),
+                full(taps.shape),
+            ]
+            + [full(r.shape) for r in rest],
+            out_specs=[colb(wrows), full((8, inner + 128))] + [full(m.shape) for m in sent],
+            scratch_shapes=[
+                pltpu.VMEM((wrows, dm), F32),
+                pltpu.VMEM((dm, wrows), F32),
+                pltpu.VMEM((4, inner + 128, 128), F32),
+            ],
+        ),
+        out_shape=[sds((wrows, length), BF), sds((8, inner + 128), F32)] + sent,
+        compiler_params=_params(),
+        cost_estimate=pl.CostEstimate(flops=2 * length * dm * wrows, bytes_accessed=30_000_000, transcendentals=0),
+    )(meta, du, du, ain, dgate, dz, nrm, taps, *rest)
+
+
+def run_leave(meta, cat, wt, width):
+    wrows, length = cat.shape
+    dm = wt.shape[1]
+    nk = BLK // (2 * width)
+    nblk = length // (2 * width)
+    rowsb = pl.BlockSpec((nk, width, dm), lambda j, *_: (j, 0, 0))
+    return pl.pallas_call(
+        leave,
+        grid_spec=pltpu.PrefetchScalarGridSpec(
+            num_scalar_prefetch=1,
+            grid=(length // BLK,),
+            in_specs=[
+                pl.BlockSpec((wrows, BLK), lambda j, *_: (0, j)),
                 full(wt.shape),
-                full(taps.shape),
             ],
-            out_specs=[rowsb, rowsb, full((dm, wrows)), full((4, inner + 128, 128))],
-            scratch_shapes=[pltpu.VMEM((wrows, dm), F32), pltpu.VMEM((wrows, BLK), BF)],
+            out_specs=[rowsb, rowsb],
         ),
-        out_shape=[sds((nblk, width, dm), F32), sds((nblk, width, dm), BF), sds((dm, wrows), BF), sds((4, inner + 128, 128), F32)],
+        out_shape=[sds((nblk, width, dm), F32), sds((nblk, width, dm), BF)],
         compiler_params=_params(),
-        cost_estimate=pl.CostEstimate(flops=4 * length * dm * wrows, bytes_accessed=30_000_000, transcendentals=0),
-    )(meta, du, du, ain, dgate, dz, nrm, wt, taps)
+        cost_estimate=pl.CostEstimate(flops=10**6, bytes_accessed=20_000_000, transcendentals=0),
+    )(meta, cat, wt)
 
 
 def permute_slots(rows, sender):
     def body(order, src, dst):
-        dst[...] = src[...]
-
-    shape = (1,) + rows.shape[1:]
-    zeros = (0,) * (rows.ndim - 1)
+        for i in range(rows.shape[0]):
+            dst[i] = src[order[i]]
+
     return pl.pallas_call(
         body,
         grid_spec=pltpu.PrefetchScalarGridSpec(
-            num_scalar_prefetch=1,
-            grid=(rows.shape[0],),
-            in_specs=[pl.BlockSpec(shape, lambda i, order: (order[i],) + zeros)],
-            out_specs=pl.BlockSpec(shape, lambda i, order: (i,) + zeros),
+            num_scalar_prefetch=1, grid=(1,), in_specs=[full(rows.shape)], out_specs=full(rows.shape)
         ),
         out_shape=sds(rows.shape, rows.dtype),
         compiler_params=_params(),
     )(sender, rows)
 
 
+WIDE = 60 * 10**9
 SWAP = [(0, 1), (1, 0)]
 CORNER = [(0, 0), (1, 2), (2, 1), (3, 3)]
 
@@ -561,59 +688,86 @@
     return lax.ppermute(v, ("core", "tensor"), CORNER)
 
 
-def both(v, other, index):
-    return jnp.stack([jnp.where(index == 0, v, other), jnp.where(index == 0, other, v)])
-
-
-def gather_weights(pack):
-    n = lax.axis_size("z")
-    z, x, y = (lax.axis_index(a) for a in ("z", "x", "tensor"))
-    line = jnp.zeros((n,) + pack.shape, pack.dtype)
-    line = lax.dynamic_update_index_in_dim(line, pack, z, 0)
-    for k in range(1, n):
-        got = lax.ppermute(pack, "z", [(i, (i + k) % n) for i in range(n)])
-        line = lax.dynamic_update_index_in_dim(line, got, (z - k) % n, 0)
-    mid = pack.shape[1] // 2
-    a, b = line[..., :mid], line[..., mid:]
-    a = both(a, twin(a, "x"), x)
-    b = both(b, twin(b, "tensor"), y)
-    a = both(a, twin(a, "tensor"), y)
-    b = both(b, twin(b, "x"), x)
-    a = jnp.transpose(a, (2, 1, 0, 3, 4))
-    b = jnp.transpose(b, (2, 0, 1, 3, 4))
-    return jnp.concatenate([a, b], -1)
-
-
-def halve(v, axis, dim):
-    i = lax.axis_index(axis)
-    keep = lax.dynamic_index_in_dim(v, i, dim, False)
-    send = lax.dynamic_index_in_dim(v, 1 - i, dim, False).astype(BF)
-    return keep.astype(F32) + twin(send, axis).astype(F32)
-
-
-def scatter_sum(v, cut):
-    n = lax.axis_size("z")
-    z = lax.axis_index("z")
-    a = halve(halve(v[..., :cut], "x", 1).astype(BF), "tensor", 1)
-    b = halve(halve(v[..., cut:], "tensor", 2).astype(BF), "x", 1)
-    c = jnp.concatenate([a, b], -1)
-    total = lax.dynamic_index_in_dim(c, z, 0, False)
-    low = c.astype(BF)
-    for k in range(1, n):
-        send = lax.dynamic_index_in_dim(low, (z + k) % n, 0, False)
-        total = total + lax.ppermute(send, "z", [(i, (i + k) % n) for i in range(n)]).astype(F32)
-    return total
-
-
-def total_of(v):
-    for axis in ("x", "tensor"):
-        v = v + twin(v, axis)
-    n = lax.axis_size("z")
-    k = 1
-    while k < n:
-        v = v + lax.ppermute(v, "z", [(i, i ^ k) for i in range(n)])
-        k *= 2
-    return v
+def after(v, *others, wide=False):
+    def body(*refs):
+        pass
+
+    space = pl.BlockSpec(memory_space=pl.ANY)
+    return pl.pallas_call(
+        body,
+        in_specs=[space] * (1 + len(others)),
+        out_specs=space,
+        out_shape=sds(v.shape, v.dtype),
+        input_output_aliases={0: 0},
+        cost_estimate=pl.CostEstimate(flops=WIDE if wide else 0, bytes_accessed=0, transcendentals=0),
+    )(v, *others)
+
+
+def ahead_of(n, k):
+    return [(i, (i + k) % n) for i in range(n)]
+
+
+def gather_weights(pack, plan, moved):
+    if plan is None:
+        return [lax.all_gather(pack, ("z", "x", "tensor"), tiled=True)], [(0, 0, 0, 0)], moved, []
+    ahead, behind, _ = plan
+    got = [pack] + [lax.ppermute(pack, "z", ahead_of(ahead + behind, k)) for k in range(1, ahead + behind)]
+    moved = after(moved, *got[1:])
+    a, b = jnp.stack(got[:ahead]), jnp.stack(got[ahead:])
+    a = after(a, moved, b, wide=True)
+    b = after(b, a)
+    both = [(i, 3 - i) for i in range(4)]
+    by, bx, bxy = twin(b, "tensor"), twin(b, "x"), lax.ppermute(b, ("x", "tensor"), both)
+    ax, ay, axy = twin(a, "x"), twin(a, "tensor"), lax.ppermute(a, ("x", "tensor"), both)
+    near = [(0, ahead, 0, 0), (0, ahead, 1, 0), (0, ahead, 0, 1), (0, ahead, 1, 1)]
+    far = [(ahead, behind, 0, 0), (ahead, behind, 0, 1), (ahead, behind, 1, 0), (ahead, behind, 1, 1)]
+    return [a, ax, ay, axy, b, by, bx, bxy], near + far, moved, [ax, ay, axy, by, bx, bxy]
+
+
+def add(kept, got):
+    return kept.astype(F32) + got.astype(F32)
+
+
+class ChipSum:
+    def __init__(self, sent, plan):
+        self.now, self.plan, self.got = sent, plan, []
+
+    def send(self, step):
+        s = self.now
+        if self.plan is None:
+            if step == 2:
+                self.got = [lax.psum_scatter(s[0], ("z", "x", "tensor"), scatter_dimension=0, tiled=True)]
+        elif step == 0:
+            self.got = [twin(s[0], "x"), twin(s[2], "tensor")]
+        elif step == 1:
+            self.got = [twin(s[1], "tensor"), twin(s[3], "x")]
+        else:
+            n = len(s)
+            self.got = [lax.ppermute(s[k], "z", ahead_of(n, k)) for k in range(1, n)]
+
+    def hold(self, v):
+        if self.plan is not None:
+            at = 1 if len(self.now) == 4 and self.now[1].ndim == 4 else 0
+            for i in (at, at + 2):
+                self.now[i] = after(self.now[i], v)
+
+    def add(self, step):
+        s, g = self.now, self.got
+        self.got = []
+        if self.plan is None:
+            self.now = g if step == 2 else s
+        elif step == 0:
+            a, b = add(s[1], g[0]), add(s[3], g[1])
+            self.now = [a[0], a[1].astype(BF), b[0], b[1].astype(BF)]
+        elif step == 1:
+            a, b = add(s[0], g[0]), add(s[2], g[1])
+            low = [a[k].astype(BF) for k in range(1, a.shape[0])] + [b[k].astype(BF) for k in range(b.shape[0])]
+            self.now = [a[0]] + low
+        else:
+            total = s[0]
+            for piece in g:
+                total = add(total, piece)
+            self.now = [total]
 
 
 def pad_rows(fwd, bwd):
@@ -651,7 +805,7 @@
     ids = jnp.arange(seqs, dtype=jnp.int32)
     sender = jnp.sum(jnp.where(slot_perm[None, :] == ids[:, None], ids[None, :], 0), axis=1)
     my_length = jnp.sum(jnp.where(slot_perm == slot, seq_lengths, 0))
-    meta = jnp.stack([core.astype(jnp.int32), my_length.astype(jnp.int32)])
+    meta = jnp.stack([core, my_length, z, x, y, jnp.int32(nz)]).astype(jnp.int32)
 
     dt_cols = jnp.transpose(w_dt.reshape(rows, heads, 2), (0, 2, 1))
     dt_cols = jnp.pad(dt_cols, ((0, 0), (0, 0), (0, 16 - heads))).reshape(rows, ZR)
@@ -666,40 +820,76 @@
     bias = pad_rows(bias[:, 0:1], bias[:, 1:2])
     alog = pad_rows(alog[:, None], alog[:, None])
 
-    rows_own = lax.all_to_all(permute_slots(layer_in[:, 0], sender), group, 0, 0, tiled=True)
+    ahead = nz // 2
+    plan = (ahead, nz - ahead, rows) if rows % 16 == 0 else None
+    moved = permute_slots(layer_in[:, 0], sender)
+    pieces, near, moved, early = gather_weights(corner(pack), plan, moved)
+    rows_own = lax.all_to_all(moved, group, 0, 0, tiled=True)
+    dy = after(out_grad[:, 0], *early)
+    rows_own = after(rows_own, *early)
     rows_oth = twin(rows_own, "core")
-    weights = gather_weights(corner(pack)).reshape(dm, pack.shape[1])
-    cot_own = lax.all_to_all(out_grad[:, 0], group, 0, 0, tiled=True)
+    cot_own = lax.all_to_all(dy, group, 0, 0, tiled=True)
+
+    nrm, gate, ain, u, zt, sf, wt, wo = run_enter(meta, rows_own, rows_oth, pieces, near, norm_gain[None], taps, bias, alog)
+    cot_own = after(cot_own, zt)
     cot_oth = twin(cot_own, "core")
-
-    nrm, gate, ain, u, zt, sf, wt = run_enter(meta, rows_own, rows_oth, weights, norm_gain[None], taps, bias, alog)
-    own, oth, dgate, dxp, ddt, dap, dbc, zb, sbin, gwo, dgain, dsk = run_mix(
-        meta, skip, cot_own, cot_oth, weights, gate, u, zt, sf, gain_u, alog
+    own, oth, dgate, dxp, ddt, dap, dbc, zb, sbin, dgain, dsk, *gwo = run_mix(
+        plan, meta, skip, cot_own, cot_oth, wo, gate, u, zt, sf, gain_u, alog
     )
     position = (2 * jnp.arange(rows_own.shape[0], dtype=jnp.int32)[:, None] + core) * width
     position = position + jnp.arange(width, dtype=jnp.int32)[None, :]
     mask = (position < my_length).astype(F32)[..., None]
     xf = rows_own.astype(F32)
-    out_rows = xf + mask * (own + twin(oth, "core").astype(F32))
-    output = lax.all_to_all(out_rows.astype(BF), group, 0, 0, tiled=True)
-    gwo_sum = scatter_sum(gwo.reshape(nz, 2, 2, rows, inner), inner // 2)
-
-    du, dz, dbias, dal = run_carry(meta, u, zt, alog, dxp, ddt, dap, dbc, zb, sbin)
-    gown, goth, gw, dtaps = run_leave(meta, du, ain, dgate, dz, nrm, wt, taps, width)
-    gn = gown + twin(goth, "core").astype(F32)
+    oth = twin(oth, "core")
+    out_grads = ChipSum(gwo, plan)
+    out_grads.send(0)
+    du, dz, dbias, dal = run_carry(meta, u, zt, alog, after(dxp, own, wide=True), ddt, dap, dbc, zb, sbin)
+    out_rows = (xf + mask * add(after(own, du), oth)).astype(BF)
+    output = lax.all_to_all(out_rows, group, 0, 0, tiled=True)
+    out_grads.hold(out_rows)
+    out_grads.add(0)
+    out_grads.send(1)
+    du = after(du, out_rows, wide=True)
+    cat, small, *gw = run_weigh(
+        plan, meta, du, ain, dgate, dz, nrm, taps, wt, norm_gain[None], dgain, dbias, dal, dsk
+    )
+    grads_in = ChipSum(gw, plan)
+    grads_in.send(0)
+    got = twin(small, "x")
+    gown, goth = run_leave(meta, after(cat, small, wide=True), wt, width)
+
+    gn = add(gown, twin(goth, "core"))
     inv = lax.rsqrt(jnp.mean(xf * xf, axis=-1, keepdims=True) + 1e-05)
     unit = xf * inv
     scaled = gn * norm_gain
-    norm_part = jnp.sum(gn * unit, axis=(0, 1))
     back = cot_own.astype(F32) + inv * (scaled - unit * jnp.mean(scaled * unit, axis=-1, keepdims=True))
-    input_grad = lax.all_to_all(back.astype(BF), group, 0, 0, tiled=True)
-
-    gw_sum = scatter_sum(gw.reshape(nz, 2, 2, rows, gw.shape[1]), inner)
+    back = back.astype(BF)
+    input_grad = lax.all_to_all(after(back, output), group, 0, 0, tiled=True)
+    small = after(small, back) + got
+    small = small + twin(small, "tensor")
+    grads_in.hold(back)
+    grads_in.add(0)
+    grads_in.send(1)
+    out_grads.hold(back)
+    out_grads.add(1)
+    out_grads.send(2)
+    out_grads.add(2)
+    k = 1
+    while k < nz:
+        small = small + lax.ppermute(small, "z", [(i, i ^ k) for i in range(nz)])
+        k *= 2
+    pair = twin(small, "core")
+    grads_in.add(1)
+    if plan is not None:
+        grads_in.now = [after(v, input_grad) for v in grads_in.now]
+    grads_in.send(2)
+    grads_in.add(2)
+    gw_sum, gwo_sum = grads_in.now[0], out_grads.now[0]
+
     bc_part = gw_sum[:, 2 * inner : 2 * inner + 128]
     bc_part = bc_part + twin(bc_part, "core")
-    grads = corner(
-        jnp.concatenate([gwo_sum, gw_sum[:, : 2 * inner], bc_part, gw_sum[:, 2 * inner + 128 :]], 1).astype(BF)
-    ).astype(F32)
+    grads = jnp.concatenate([gwo_sum, gw_sum[:, : 2 * inner], bc_part, gw_sum[:, 2 * inner + 128 :]], 1)
+    grads = corner(grads.astype(BF)).astype(F32)
     out_sum = grads[:, :inner].T
     gate_sum = grads[:, inner : 2 * inner]
     inner_sum = grads[:, 2 * inner : 3 * inner]
@@ -707,35 +897,23 @@
     dt_sum = grads[:, 3 * inner + 128 :].reshape(rows, 2, 16)[:, :, :heads]
     dt_sum = jnp.transpose(dt_sum, (0, 2, 1)).reshape(rows, 2 * heads)
 
-    dtap = jnp.sum(dtaps, axis=-1)
-    dbias = jnp.sum(dbias, axis=1).reshape(2, 16)[:, :heads].T.reshape(2 * heads)
-    dal = jnp.sum(dal, axis=1).reshape(2, 16)[:, :heads].sum(0)
-    dskips = jnp.sum(dsk, axis=1)[:heads]
-    half = [dtap[:, :inner].reshape(-1), jnp.sum(dgain, axis=1), dbias, dal, dskips]
-    summed = [norm_part, dtap[:, inner:].reshape(-1)]
-    sizes = [v.shape[0] for v in half + summed]
-    vec = jnp.concatenate(half + summed)
-    vec = total_of(jnp.pad(vec, (0, -vec.shape[0] % 1024)).reshape(-1, 128)).reshape(-1)
-    pair = lax.ppermute(vec, "core", SWAP)
-    here = jnp.where(core == y, vec, pair)
-    joint = vec + pair
-    cuts = [sum(sizes[:i]) for i in range(len(sizes) + 1)]
-    convx_g, gain_g, bias_g, alog_g, skip_g = (here[cuts[i] : cuts[i + 1]] for i in range(5))
-    norm_g, convbc_g = (joint[cuts[i] : cuts[i + 1]] for i in (5, 6))
+    here = jnp.where(core == y, small, pair)
+    joint = small + pair
+    heads_of = lambda at: here[6, at : at + ZR].reshape(2, 16)[:, :heads]
     return (
         output[:, None],
         input_grad[:, None],
-        norm_g,
+        joint[5, :inner],
         gate_sum,
         inner_sum,
         bc_sum,
         dt_sum,
-        convx_g.reshape(4, inner),
-        convbc_g.reshape(4, 128),
-        bias_g,
-        alog_g,
-        skip_g,
-        gain_g,
+        here[0:4, :inner],
+        joint[0:4, inner:],
+        heads_of(0).T.reshape(2 * heads),
+        heads_of(128).sum(0),
+        here[6, 256 : 256 + heads],
+        here[4, :inner],
         out_sum,
     )
 

time: 464 us -> 390 us (0.84); the launches traced: 457 us -> 389 us
  Pallas kernels: 174 us -> 145 us
  waiting for transfers between devices: 141 us -> 114 us
  local copies, waits for them, and re-layouts: 38.9 us -> 31.4 us
  other arithmetic: 37.2 us -> 30.5 us
    ppermute x12 -> x13, waiting for transfers between devices: 90.5 us -> 39.6 us  [the longest x6 14.8 us: send(): self.got = [lax.ppermute(s[k], 'z', ahead_of(n, k)) for k in range(1, n)]]
    pallas_call x1 -> x24, Pallas kernels: 28.1 us -> 59.3 us  [the longest x1 30.1 us: run_weigh(): pl.pallas_call(weigh, grid_spec=pltpu.PrefetchScalarGridSpec(num_scalar_p...]
    pallas_call x1, Pallas kernels: 84.6 us -> 53.7 us  [run_mix(): pl.pallas_call(mix, grid_spec=pltpu.PrefetchScalarGridSpec(num_scalar_pre...]
    pallas_call x1, Pallas kernels: 35.7 us -> 12.7 us  [run_leave(): pl.pallas_call(leave, grid_spec=pltpu.PrefetchScalarGridSpec(num_scalar_p...]
    all_to_all x4, waiting for transfers between devices: 0.01 us -> 22.7 us  [the longest x1 22.7 us: shards(): input_grad = lax.all_to_all(after(back, output), group, 0, 0, tiled=True)]
    add x7 -> x10, other arithmetic: 1.16 us -> 8.8 us  [the longest x6 8.03 us: add(): return kept.astype(F32) + got.astype(F32)]
    pallas_call x1, Pallas kernels: 9.96 us -> 3.31 us  [permute_slots(): pl.pallas_call(body, grid_spec=pltpu.PrefetchScalarGridSpec(num_scalar_pr...]
    convert_element_type x0 -> x8, local copies, waits for them, and re-layouts: none -> 5.48 us  [the longest x4 3.31 us: add(): self.now = [a[0], a[1].astype(BF), b[0], b[1].astype(BF)]]
  transfers between devices with their start and end apart: 38 -> 40, of which waited for: 14 -> 18; matrix products, arithmetic and copies ran while one was open for 14% -> 11% of each run, Pallas kernels for 8% -> 24%
where the time goes in v2:
time: 390 us; the launch traced here: 389 us
  Pallas kernels  145 us (37%)
  waiting for transfers between devices  114 us (29%)
  starting transfers between devices  65.9 us (17%)
  local copies, waits for them, and re-layouts  31.4 us (8%)
  other arithmetic  30.5 us (8%)
    pallas_call x1, Pallas kernels, run_mix(): pl.pallas_call(mix, grid_spec=pltpu.PrefetchScalarGridSpec(num_scalar_pre...  53.7 us
    ppermute x20, waiting for transfers between devices, twin(): return lax.ppermute(v, axis, SWAP)  42.2 us
    pallas_call x1, Pallas kernels, run_weigh(): pl.pallas_call(weigh, grid_spec=pltpu.PrefetchScalarGridSpec(num_scalar_p...  30.1 us
    pallas_call x1, Pallas kernels, run_enter(): pl.pallas_call(functools.partial(enter, near), grid_spec=pltpu.PrefetchSc...  29.2 us
    all_to_all x1, waiting for transfers between devices, shards(): input_grad = lax.all_to_all(after(back, output), group, 0, 0, tiled=True)  22.7 us
    ppermute x20, starting transfers between devices, twin(): return lax.ppermute(v, axis, SWAP)  22.4 us
    pallas_call x1, Pallas kernels, run_carry(): pl.pallas_call(carry, grid_spec=pltpu.PrefetchScalarGridSpec(num_scalar_p...  16 us
    ppermute x6, waiting for transfers between devices, send(): self.got = [lax.ppermute(s[k], 'z', ahead_of(n, k)) for k in range(1, n)]  14.8 us
  transfers between devices with their start and end apart: 40, of which 18 were waited for; matrix products, arithmetic and copies ran while one was open for 11% of the time, Pallas kernels for 24%

profile of v2, /device:TPU:9, one launch (start us, length us, event | category | flops | bytes accessed | tf_op | source)
XLA Modules:
  0.0 388.6 jit_solution(15524406093368979627)
XLA Ops:
  0.7 2.8 copy.173
  3.7 3.7 collective-permute-start
  7.4 4.2 %collective-permute-done = bf16[48,2560]{1,0:T(8,128)(2,1)S(1)} collective-permute-done((bf16[48,2560]{1,0:T(8,128)(2,1)S(1)}, bf16[48,2560]{1,0:T(8,128)(2,1)S(1)}, u32[]{:S(2)}, u32[]{:S(2)}) %collective-permute-start) | collective-permute-done | bytes 245792 | tf_op jit(solution)/shard_map/ppermute | solution.py:688
  11.6 1.3 collective-permute-start.1
  13.8 1.2 collective-permute-start.3
  15.7 3.3 shard_map.263.refs_0_
  19.0 6.9 %collective-permute-done.1.refs_1_ = bf16[48,2560]{1,0:T(8,128)(2,1)S(1)} collective-permute-done((bf16[48,2560]{1,0:T(8,128)(2,1)S(1)}, bf16[48,2560]{1,0:T(8,128)(2,1)S(1)}, u32[]{:S(2)}, u32[]{:S(2)}) %collective-permute-start.1) | collective-permute-done | bytes 245792 | tf_op jit(solution)/shard_map/ppermute | solution.py:714
  25.9 2.6 collective-permute-done.2.refs_2_
  30.4 5.8 %all-to-all-start = ((bf16[16,64,768]{2,1,0:T(8,128)(2,1)}), bf16[16,64,768]{2,1,0:T(8,128)(2,1)S(1)}, u32[]{:S(2)}, u32[]{:S(2)}) async-start(bf16[16,64,768]{2,1,0:T(8,128)(2,1)} %shard_map.264.refs_1_), calls=%async_computation | async-start | bytes 3145728 | tf_op jit(solution)/shard_map/all_to_all | solution.py:827
  42.9 29.0 %collective-permute-done.7.refs_4_.refs_5_ = bf16[2,48,2560]{2,1,0:T(8,128)(2,1)S(1)} collective-permute-done((bf16[2,48,2560]{2,1,0:T(8,128)(2,1)}, bf16[2,48,2560]{2,1,0:T(8,128)(2,1)S(1)}, u32[]{:S(2)}, u32[]{:S(2)}) %collective-permute-start.7) | collective-permute-done | bytes 491552 | tf_op jit(solution)/shard_map/ppermute | solution.py:684
  71.9 1.9 collective-permute-start.6
  73.8 2.7 collective-permute-done.9.refs_6_.refs_7_
  76.5 9.9 %collective-permute-done.4.refs_1_ = bf16[2,48,2560]{2,1,0:T(8,128)(2,1)S(1)} collective-permute-done((bf16[2,48,2560]{2,1,0:T(8,128)(2,1)}, bf16[2,48,2560]{2,1,0:T(8,128)(2,1)S(1)}, u32[]{:S(2)}, u32[]{:S(2)}) %collective-permute-start.4) | collective-permute-done | bytes 491552 | tf_op jit(solution)/shard_map/ppermute | solution.py:684
  86.4 11.2 %collective-permute-done.6.refs_3_ = bf16[2,48,2560]{2,1,0:T(8,128)(2,1)} collective-permute-done((bf16[2,48,2560]{2,1,0:T(8,128)(2,1)}, bf16[2,48,2560]{2,1,0:T(8,128)(2,1)}, u32[]{:S(2)}, u32[]{:S(2)}) %collective-permute-start.6) | collective-permute-done | bytes 491552 | tf_op jit(solution)/shard_map/ppermute | solution.py:721
  97.7 5.8 %all-to-all-start.1 = ((bf16[16,64,768]{2,1,0:T(8,128)(2,1)}), bf16[16,64,768]{2,1,0:T(8,128)(2,1)S(1)}, u32[]{:S(2)}, u32[]{:S(2)}) async-start(bf16[16,64,768]{2,1,0:T(8,128)(2,1)} %shard_map.268), calls=%async_computation.1 | async-start | bytes 3145728 | tf_op jit(solution)/shard_map/all_to_all | solution.py:831
  103.6 1.9 collective-permute-start.11
  105.8 3.7 collective-permute-start.10
  110.7 1.2 stack.47.meta
  112.0 4.1 %collective-permute-done.10 = f32[8,768]{1,0:T(8,128)S(1)} collective-permute-done((f32[8,768]{1,0:T(8,128)S(1)}, f32[8,768]{1,0:T(8,128)S(1)}, u32[]{:S(2)}, u32[]{:S(2)}) %collective-permute-start.10) | collective-permute-done | bytes 24608 | tf_op jit(solution)/shard_map/ppermute | solution.py:688
  118.5 29.2 %shard_map.269 = (bf16[2048,768]{1,0:T(8,128)(2,1)}, f32[768,2048]{1,0:T(8,128)}, bf16[896,2048]{1,0:T(8,128)(2,1)}, f32[896,2048]{1,0:T(8,128)}, f32[32,2048]{1...) custom-call(s32[6]{0:T(128)} %stack.47.meta, ...), custom_call_target="tpu_custom_call" | custom-call | flops 5335154688 | bytes 30000000 | tf_op jit(solution)/shard_map/pallas_call | solution.py:470
  150.6 1.9 collective-permute-done.12.dyb
  153.8 53.7 %shard_map.271 = (f32[16,64,768]{2,1,0:T(8,128)}, bf16[16,64,768]{2,1,0:T(8,128)(2,1)}, bf16[768,2048]{1,0:T(8,128)(2,1)}, f32[768,2048]{1,0:T(8,128)}, f32[32,2...) custom-call(s32[6]{0:T(128)} %stack.47.meta, ...), custom_call_target="tpu_custom_call" | custom-call | flops 40000000000 | bytes 50000000 | tf_op jit(solution)/shard_map/pallas_call | solution.py:520
  207.7 16.0 %shard_map.273 = (f32[896,2048]{1,0:T(8,128)}, bf16[32,2048]{1,0:T(8,128)(2,1)}, f32[32,128]{1,0:T(8,128)}, f32[32,128]{1,0:T(8,128)}) custom-call(s32[6]{0:T(128)} %stack.47.meta, f32[896,2048]{1,0:T(8,128)} %get-tuple-element.52.u, f32[32,2048]{1,0:T(8,128)} %get-tuple-element.49.refs_1_.zt, f32[32,1]{1,0:T(8,128)} %get-tuple-element.200.refs_11_.alog, ...), custom_call_target="tpu_custom_call" | custom-call | flops 1000000000 | bytes 30000000 | tf_op jit(solution)/shard_map/pallas_call | solution.py:585
  225.1 3.9 %fusion.8 = (f32[16,64]{1,0:T(8,128)S(1)}, bf16[16,64,768]{2,1,0:T(8,128)(2,1)}) fusion(bf16[16,64,768]{2,1,0:T(8,128)(2,1)S(1)} %copy-done.3, f32[16,64,768]{2,1,0:T(8,128)} %shard_map.274, bf16[16,64,768]{2,1,0:T(8,128)(2,1)S(1)} %collective-permute-done.13, f32[16,64]{1,0:T(8,128)S(1)} %fusion.24), kind=kLoop, calls=%fused_computation.11 | loop fusion | flops 6290432 | bytes 7872512 | tf_op jit(solution)/shard_map/reduce_sum | solution.py:862
  229.0 3.8 all-to-all-start.2
  232.8 30.1 %shard_map.276 = (bf16[1696,2048]{1,0:T(8,128)(2,1)}, f32[8,896]{1,0:T(8,128)}, bf16[2,2,48,1696]{3,2,1,0:T(8,128)(2,1)}, bf16[2,2,48,1696]{3,2,1,0:T(8,128)(2,1...) custom-call(s32[6]{0:T(128)} %stack.47.meta, f32[896,2048]{1,0:T(8,128)} %shard_map.275.du.nxt, ...), custom_call_target="tpu_custom_call" | custom-call | flops 5335154688 | bytes 30000000 | tf_op jit(solution)/shard_map/pallas_call | solution.py:612
  262.9 1.2 collective-permute-start.15
  264.1 12.7 %shard_map.278 = (f32[16,64,768]{2,1,0:T(8,128)}, bf16[16,64,768]{2,1,0:T(8,128)(2,1)}) custom-call(s32[6]{0:T(128)} %stack.47.meta, bf16[1696,2048]{1,0:T(8,128)(2,1)} %shard_map.277.cat, bf16[1696,768]{1,0:T(8,128)(2,1)} %get-tuple-element.67.wt), custom_call_target="tpu_custom_call" | custom-call | flops 1000000 | bytes 20000000 | tf_op jit(solution)/shard_map/pallas_call | solution.py:646
  276.8 1.8 collective-permute-start.14
  282.5 1.2 collective-permute-start.21
  284.9 1.7 slice_bitcast_fusion.3.refs_0_
  287.6 3.4 fusion.2
  291.4 3.7 fusion.6.refs_0_.refs_1_
  296.9 2.1 collective-permute-start.25
  300.3 1.2 collective-permute-start.22
  303.5 1.4 convert_add_fusion.2
  306.7 2.5 convert_add_fusion.1
  309.4 2.1 collective-permute-start.18
  312.6 4.8 %all-to-all-start.3 = ((bf16[16,64,768]{2,1,0:T(8,128)(2,1)}), bf16[16,64,768]{2,1,0:T(8,128)(2,1)S(1)}, u32[]{:S(2)}, u32[]{:S(2)}) async-start(bf16[16,64,768]{2,1,0:T(8,128)(2,1)} %shard_map.279), calls=%async_computation.3 | async-start | bytes 3145728 | tf_op jit(solution)/shard_map/all_to_all | solution.py:867
  317.4 1.8 fusion.13
  320.5 4.2 %collective-permute-start.19 = (f32[8,896]{1,0:T(8,128)S(1)}, f32[8,896]{1,0:T(8,128)S(1)}, u32[]{:S(2)}, u32[]{:S(2)}) collective-permute-start(f32[8,896]{1,0:T(8,128)S(1)} %add.137), channel_id=1, source_target_pairs={{0,2},{2,0},{1,3},{3,1},{4,6},{6,4},{5,7},{7,5},{8,10},{10,8},{9,1... | collective-permute-start | bytes 86024 | tf_op jit(solution)/shard_map/ppermute | solution.py:684
  328.8 1.2 fusion.10
  330.8 22.7 %all-to-all-done.3.refs_1_ = bf16[16,64,768]{2,1,0:T(8,128)(2,1)S(1)} async-done(((bf16[16,64,768]{2,1,0:T(8,128)(2,1)}), bf16[16,64,768]{2,1,0:T(8,128)(2,1)S(1)}, u32[]{:S(2)}, u32[]{:S(2)}) %all-to-all-start.3) | async-done | bytes 1572896 | tf_op jit(solution)/shard_map/all_to_all | solution.py:867
  356.8 2.2 collective-permute-done.29
  359.1 3.6 collective-permute-done.32
  362.7 8.9 %collective-permute-done.33 = bf16[48,1696]{1,0:T(8,128)(2,1)S(1)} collective-permute-done((bf16[48,1696]{1,0:T(8,128)(2,1)}, bf16[48,1696]{1,0:T(8,128)(2,1)S(1)}, u32[]{:S(2)}, u32[]{:S(2)}) %collective-permute-start.33) | collective-permute-done | bytes 162848 | tf_op jit(solution)/shard_map/ppermute | solution.py:746
  376.5 3.1 collective-permute-start.35
  382.5 1.7 collective-permute-done.35
  (232 shorter events, 56.1 us)
Async XLA Ops:
  0.6 14.4 %copy-start.37 = (s32[16]{0:T(128)S(1)}, s32[16]{0:T(128)}, u32[]{:S(2)}) copy-start(s32[16]{0:T(128)} %param.19) | copy-start | bytes 196
  3.7 7.9 %collective-permute-start = (bf16[48,2560]{1,0:T(8,128)(2,1)S(1)}, bf16[48,2560]{1,0:T(8,128)(2,1)S(1)}, u32[]{:S(2)}, u32[]{:S(2)}) collective-permute-start(bf16[48,2560]{1,0:T(8,128)(2,1)S(1)} %pad_dynamic-update-slice_fusion), channel_id=1, source_target_pairs={{0,0},{1,2},{2,1},{3,3},{4,4},{5,6},{6,5},{7,7},{8,8},{9,10},{10,9... | collective-permute-start | bytes 737288 | tf_op jit(solution)/shard_map/ppermute | solution.py:688
  11.6 14.3 %collective-permute-start.1 = (bf16[48,2560]{1,0:T(8,128)(2,1)S(1)}, bf16[48,2560]{1,0:T(8,128)(2,1)S(1)}, u32[]{:S(2)}, u32[]{:S(2)}) collective-permute-start(bf16[48,2560]{1,0:T(8,128)(2,1)S(1)} %collective-permute-done), channel_id=1, source_target_pairs={{0,8},{8,16},{16,24},{24,0},{1,9},{9,17},{17,25},{25,1},{2,10},{10... | collective-permute-start | bytes 737288 | tf_op jit(solution)/shard_map/ppermute | solution.py:714
  12.9 15.6 %collective-permute-start.2 = (bf16[48,2560]{1,0:T(8,128)(2,1)S(1)}, bf16[48,2560]{1,0:T(8,128)(2,1)S(1)}, u32[]{:S(2)}, u32[]{:S(2)}) collective-permute-start(bf16[48,2560]{1,0:T(8,128)(2,1)S(1)} %collective-permute-done), channel_id=1, source_target_pairs={{0,16},{8,24},{16,0},{24,8},{1,17},{9,25},{17,1},{25,9},{2,18},{10... | collective-permute-start | bytes 737288 | tf_op jit(solution)/shard_map/ppermute | solution.py:714
  13.8 15.8 %collective-permute-start.3 = (bf16[48,2560]{1,0:T(8,128)(2,1)S(1)}, bf16[48,2560]{1,0:T(8,128)(2,1)S(1)}, u32[]{:S(2)}, u32[]{:S(2)}) collective-permute-start(bf16[48,2560]{1,0:T(8,128)(2,1)S(1)} %collective-permute-done), channel_id=1, source_target_pairs={{0,24},{8,0},{16,8},{24,16},{1,25},{9,1},{17,9},{25,17},{2,26},{10... | collective-permute-start | bytes 737288 | tf_op jit(solution)/shard_map/ppermute | solution.py:714
  30.4 67.3 %all-to-all-start = ((bf16[16,64,768]{2,1,0:T(8,128)(2,1)}), bf16[16,64,768]{2,1,0:T(8,128)(2,1)S(1)}, u32[]{:S(2)}, u32[]{:S(2)}) async-start(bf16[16,64,768]{2,1,0:T(8,128)(2,1)} %shard_map.264.refs_1_), calls=%async_computation | async-start | bytes 3145728 | tf_op jit(solution)/shard_map/all_to_all | solution.py:827
  37.9 34.0 %collective-permute-start.7 = (bf16[2,48,2560]{2,1,0:T(8,128)(2,1)}, bf16[2,48,2560]{2,1,0:T(8,128)(2,1)S(1)}, u32[]{:S(2)}, u32[]{:S(2)}) collective-permute-start(bf16[2,48,2560]{2,1,0:T(8,128)(2,1)} %shard_map.266.refs_4_), channel_id=1, source_target_pairs={{0,1},{1,0},{2,3},{3,2},{4,5},{5,4},{6,7},{7,6},{8,9},{9,8},{10,11... | collective-permute-start | bytes 1474568 | tf_op jit(solution)/shard_map/ppermute | solution.py:684
  39.1 34.7 %collective-permute-start.8 = (bf16[2,48,2560]{2,1,0:T(8,128)(2,1)}, bf16[2,48,2560]{2,1,0:T(8,128)(2,1)S(1)}, u32[]{:S(2)}, u32[]{:S(2)}) collective-permute-start(bf16[2,48,2560]{2,1,0:T(8,128)(2,1)} %shard_map.266.refs_4_), channel_id=1, source_target_pairs={{0,4},{4,0},{1,5},{5,1},{2,6},{6,2},{3,7},{7,3},{8,12},{12,8},{9,1... | collective-permute-start | bytes 1474568 | tf_op jit(solution)/shard_map/ppermute | solution.py:684
  40.2 36.3 %collective-permute-start.9 = (bf16[2,48,2560]{2,1,0:T(8,128)(2,1)}, bf16[2,48,2560]{2,1,0:T(8,128)(2,1)S(1)}, u32[]{:S(2)}, u32[]{:S(2)}) collective-permute-start(bf16[2,48,2560]{2,1,0:T(8,128)(2,1)} %shard_map.266.refs_4_), channel_id=1, source_target_pairs={{0,5},{1,4},{4,1},{5,0},{2,7},{3,6},{6,3},{7,2},{8,13},{9,12},{12,... | collective-permute-start | bytes 1474568 | tf_op jit(solution)/shard_map/ppermute | solution.py:720
  40.5 45.9 %collective-permute-start.4 = (bf16[2,48,2560]{2,1,0:T(8,128)(2,1)}, bf16[2,48,2560]{2,1,0:T(8,128)(2,1)S(1)}, u32[]{:S(2)}, u32[]{:S(2)}) collective-permute-start(bf16[2,48,2560]{2,1,0:T(8,128)(2,1)} %shard_map.265.refs_1_.refs_0_), channel_id=1, source_target_pairs={{0,4},{4,0},{1,5},{5,1},{2,6},{6,2},{3,7},{7,3},{8,12},{12,8},{9,1... | collective-permute-start | bytes 1474568 | tf_op jit(solution)/shard_map/ppermute | solution.py:684
  41.7 44.7 %collective-permute-start.5 = (bf16[2,48,2560]{2,1,0:T(8,128)(2,1)}, bf16[2,48,2560]{2,1,0:T(8,128)(2,1)}, u32[]{:S(2)}, u32[]{:S(2)}) collective-permute-start(bf16[2,48,2560]{2,1,0:T(8,128)(2,1)} %shard_map.265.refs_1_.refs_0_), channel_id=1, source_target_pairs={{0,1},{1,0},{2,3},{3,2},{4,5},{5,4},{6,7},{7,6},{8,9},{9,8},{10,11... | collective-permute-start | bytes 1474568 | tf_op jit(solution)/shard_map/ppermute | solution.py:684
  71.9 25.8 %copy-start.11 = (bf16[2,48,2560]{2,1,0:T(8,128)(2,1)}, bf16[2,48,2560]{2,1,0:T(8,128)(2,1)S(1)}, u32[]{:S(2)}) copy-start(bf16[2,48,2560]{2,1,0:T(8,128)(2,1)S(1)} %collective-permute-done.7.refs_4_.refs_5_) | copy-start | bytes 1474564
  71.9 25.8 %collective-permute-start.6 = (bf16[2,48,2560]{2,1,0:T(8,128)(2,1)}, bf16[2,48,2560]{2,1,0:T(8,128)(2,1)}, u32[]{:S(2)}, u32[]{:S(2)}) collective-permute-start(bf16[2,48,2560]{2,1,0:T(8,128)(2,1)} %shard_map.265.refs_1_.refs_0_), channel_id=1, source_target_pairs={{0,5},{1,4},{4,1},{5,0},{2,7},{3,6},{6,3},{7,2},{8,13},{9,12},{12,... | collective-permute-start | bytes 1474568 | tf_op jit(solution)/shard_map/ppermute | solution.py:721
  73.8 23.9 %copy-start.12 = (bf16[2,48,2560]{2,1,0:T(8,128)(2,1)}, bf16[2,48,2560]{2,1,0:T(8,128)(2,1)S(1)}, u32[]{:S(2)}) copy-start(bf16[2,48,2560]{2,1,0:T(8,128)(2,1)S(1)} %collective-permute-done.8.refs_5_.refs_6_) | copy-start | bytes 1474564
  76.5 21.2 %copy-start.13 = (bf16[2,48,2560]{2,1,0:T(8,128)(2,1)}, bf16[2,48,2560]{2,1,0:T(8,128)(2,1)S(1)}, u32[]{:S(2)}) copy-start(bf16[2,48,2560]{2,1,0:T(8,128)(2,1)S(1)} %collective-permute-done.9.refs_6_.refs_7_) | copy-start | bytes 1474564
  97.7 50.1 %all-to-all-start.1 = ((bf16[16,64,768]{2,1,0:T(8,128)(2,1)}), bf16[16,64,768]{2,1,0:T(8,128)(2,1)S(1)}, u32[]{:S(2)}, u32[]{:S(2)}) async-start(bf16[16,64,768]{2,1,0:T(8,128)(2,1)} %shard_map.268), calls=%async_computation.1 | async-start | bytes 3145728 | tf_op jit(solution)/shard_map/all_to_all | solution.py:831
  103.6 14.9 %collective-permute-start.11 = (bf16[16,64,768]{2,1,0:T(8,128)(2,1)}, bf16[16,64,768]{2,1,0:T(8,128)(2,1)}, u32[]{:S(2)}, u32[]{:S(2)}) collective-permute-start(bf16[16,64,768]{2,1,0:T(8,128)(2,1)} %shard_map.267.xa), channel_id=1, source_target_pairs={{0,2},{2,0},{1,3},{3,1},{4,6},{6,4},{5,7},{7,5},{8,10},{10,8},{9,1... | collective-permute-start | bytes 4718600 | tf_op jit(solution)/shard_map/ppermute | solution.py:684
  105.8 10.3 %collective-permute-start.10 = (f32[8,768]{1,0:T(8,128)S(1)}, f32[8,768]{1,0:T(8,128)S(1)}, u32[]{:S(2)}, u32[]{:S(2)}) collective-permute-start(f32[8,768]{1,0:T(8,128)S(1)} %maximum_maximum_fusion), channel_id=1, source_target_pairs={{0,0},{1,2},{2,1},{3,3},{4,4},{5,6},{6,5},{7,7},{8,8},{9,10},{10,9... | collective-permute-start | bytes 73736 | tf_op jit(solution)/shard_map/ppermute | solution.py:688
  148.9 3.6 collective-permute-start.12
  207.5 17.5 %collective-permute-start.13 = (bf16[16,64,768]{2,1,0:T(8,128)(2,1)}, bf16[16,64,768]{2,1,0:T(8,128)(2,1)S(1)}, u32[]{:S(2)}, u32[]{:S(2)}) collective-permute-start(bf16[16,64,768]{2,1,0:T(8,128)(2,1)} %get-tuple-element.62), channel_id=1, source_target_pairs={{0,2},{2,0},{1,3},{3,1},{4,6},{6,4},{5,7},{7,5},{8,10},{10,8},{9,1... | collective-permute-start | bytes 4718600 | tf_op jit(solution)/shard_map/ppermute | solution.py:684
  223.7 54.9 %collective-permute-start.23 = (bf16[2,2,48,768]{3,2,1,0:T(8,128)(2,1)}, bf16[2,2,48,768]{3,2,1,0:T(8,128)(2,1)}, u32[]{:S(2)}, u32[]{:S(2)}) collective-permute-start(bf16[2,2,48,768]{3,2,1,0:T(8,128)(2,1)} %get-tuple-element.79), channel_id=1, source_target_pairs={{0,1},{1,0},{2,3},{3,2},{4,5},{5,4},{6,7},{7,6},{8,9},{9,8},{10,11... | collective-permute-start | bytes 884744 | tf_op jit(solution)/shard_map/ppermute | solution.py:684
  223.8 57.7 %collective-permute-start.20 = (bf16[2,2,48,768]{3,2,1,0:T(8,128)(2,1)}, bf16[2,2,48,768]{3,2,1,0:T(8,128)(2,1)S(1)}, u32[]{:S(2)}, u32[]{:S(2)}) collective-permute-start(bf16[2,2,48,768]{3,2,1,0:T(8,128)(2,1)} %get-tuple-element.77), channel_id=1, source_target_pairs={{0,4},{4,0},{1,5},{5,1},{2,6},{6,2},{3,7},{7,3},{8,12},{12,8},{9,1... | collective-permute-start | bytes 884744 | tf_op jit(solution)/shard_map/ppermute | solution.py:684
  229.0 82.5 %all-to-all-start.2 = ((bf16[16,64,768]{2,1,0:T(8,128)(2,1)}), bf16[16,64,768]{2,1,0:T(8,128)(2,1)S(1)}, u32[]{:S(2)}, u32[]{:S(2)}) async-start(bf16[16,64,768]{2,1,0:T(8,128)(2,1)} %get-tuple-element.187.refs_1_), calls=%async_computation.2 | async-start | bytes 3145728 | tf_op jit(solution)/shard_map/all_to_all | solution.py:848
  262.9 37.4 %collective-permute-start.15 = (f32[8,896]{1,0:T(8,128)}, f32[8,896]{1,0:T(8,128)S(1)}, u32[]{:S(2)}, u32[]{:S(2)}) collective-permute-start(f32[8,896]{1,0:T(8,128)} %get-tuple-element.73.refs_1_.refs_0_), channel_id=1, source_target_pairs={{0,4},{4,0},{1,5},{5,1},{2,6},{6,2},{3,7},{7,3},{8,12},{12,8},{9,1... | collective-permute-start | bytes 86024 | tf_op jit(solution)/shard_map/ppermute | solution.py:684
  264.1 14.5 %copy-start.16 = (bf16[2,2,48,768]{3,2,1,0:T(8,128)(2,1)S(1)}, bf16[2,2,48,768]{3,2,1,0:T(8,128)(2,1)}, u32[]{:S(2)}) copy-start(bf16[2,2,48,768]{3,2,1,0:T(8,128)(2,1)} %shard_map.283) | copy-start | bytes 884740
  276.8 10.5 %collective-permute-start.14 = (bf16[16,64,768]{2,1,0:T(8,128)(2,1)}, bf16[16,64,768]{2,1,0:T(8,128)(2,1)}, u32[]{:S(2)}, u32[]{:S(2)}) collective-permute-start(bf16[16,64,768]{2,1,0:T(8,128)(2,1)} %get-tuple-element.75), channel_id=1, source_target_pairs={{0,2},{2,0},{1,3},{3,1},{4,6},{6,4},{5,7},{7,5},{8,10},{10,8},{9,1... | collective-permute-start | bytes 4718600 | tf_op jit(solution)/shard_map/ppermute | solution.py:684
  281.2 14.0 %collective-permute-start.24 = (bf16[2,48,768]{2,1,0:T(8,128)(2,1)}, bf16[2,48,768]{2,1,0:T(8,128)(2,1)}, u32[]{:S(2)}, u32[]{:S(2)}) collective-permute-start(bf16[2,48,768]{2,1,0:T(8,128)(2,1)} %fusion.16), channel_id=1, source_target_pairs={{0,4},{4,0},{1,5},{5,1},{2,6},{6,2},{3,7},{7,3},{8,12},{12,8},{9,1... | collective-permute-start | bytes 442376 | tf_op jit(solution)/shard_map/ppermute | solution.py:684
  282.5 16.4 %collective-permute-start.21 = (bf16[2,48,768]{2,1,0:T(8,128)(2,1)S(1)}, bf16[2,48,768]{2,1,0:T(8,128)(2,1)S(1)}, u32[]{:S(2)}, u32[]{:S(2)}) collective-permute-start(bf16[2,48,768]{2,1,0:T(8,128)(2,1)S(1)} %fusion.15), channel_id=1, source_target_pairs={{0,1},{1,0},{2,3},{3,2},{4,5},{5,4},{6,7},{7,6},{8,9},{9,8},{10,11... | collective-permute-start | bytes 442376 | tf_op jit(solution)/shard_map/ppermute | solution.py:684
  283.8 18.5 %collective-permute-start.27 = (bf16[2,2,48,1696]{3,2,1,0:T(8,128)(2,1)}, bf16[2,2,48,1696]{3,2,1,0:T(8,128)(2,1)}, u32[]{:S(2)}, u32[]{:S(2)}) collective-permute-start(bf16[2,2,48,1696]{3,2,1,0:T(8,128)(2,1)} %get-tuple-element.81), channel_id=1, source_target_pairs={{0,4},{4,0},{1,5},{5,1},{2,6},{6,2},{3,7},{7,3},{8,12},{12,8},{9,1... | collective-permute-start | bytes 1953800 | tf_op jit(solution)/shard_map/ppermute | solution.py:684
  287.4 19.2 %collective-permute-start.30 = (bf16[2,2,48,1696]{3,2,1,0:T(8,128)(2,1)}, bf16[2,2,48,1696]{3,2,1,0:T(8,128)(2,1)}, u32[]{:S(2)}, u32[]{:S(2)}) collective-permute-start(bf16[2,2,48,1696]{3,2,1,0:T(8,128)(2,1)} %get-tuple-element.83), channel_id=1, source_target_pairs={{0,1},{1,0},{2,3},{3,2},{4,5},{5,4},{6,7},{7,6},{8,9},{9,8},{10,11... | collective-permute-start | bytes 1953800 | tf_op jit(solution)/shard_map/ppermute | solution.py:684
  296.9 23.6 %collective-permute-start.25 = (bf16[48,768]{1,0:T(8,128)(2,1)}, bf16[48,768]{1,0:T(8,128)(2,1)S(1)}, u32[]{:S(2)}, u32[]{:S(2)}) collective-permute-start(bf16[48,768]{1,0:T(8,128)(2,1)} %get-tuple-element.192), channel_id=1, source_target_pairs={{0,16},{8,24},{16,0},{24,8},{1,17},{9,25},{17,1},{25,9},{2,18},{10... | collective-permute-start | bytes 221192 | tf_op jit(solution)/shard_map/ppermute | solution.py:746
  299.0 25.7 %collective-permute-start.26 = (bf16[48,768]{1,0:T(8,128)(2,1)}, bf16[48,768]{1,0:T(8,128)(2,1)}, u32[]{:S(2)}, u32[]{:S(2)}) collective-permute-start(bf16[48,768]{1,0:T(8,128)(2,1)} %get-tuple-element.193), channel_id=1, source_target_pairs={{0,24},{8,0},{16,8},{24,16},{1,25},{9,1},{17,9},{25,17},{2,26},{10... | collective-permute-start | bytes 221192 | tf_op jit(solution)/shard_map/ppermute | solution.py:746
  300.3 24.4 %collective-permute-start.22 = (bf16[48,768]{1,0:T(8,128)(2,1)S(1)}, bf16[48,768]{1,0:T(8,128)(2,1)}, u32[]{:S(2)}, u32[]{:S(2)}) collective-permute-start(bf16[48,768]{1,0:T(8,128)(2,1)S(1)} %fusion.21), channel_id=1, source_target_pairs={{0,8},{8,16},{16,24},{24,0},{1,9},{9,17},{17,25},{25,1},{2,10},{10... | collective-permute-start | bytes 221192 | tf_op jit(solution)/shard_map/ppermute | solution.py:746
  302.3 3.4 collective-permute-start.16
  305.7 20.1 %collective-permute-start.28 = (bf16[2,48,1696]{2,1,0:T(8,128)(2,1)}, bf16[2,48,1696]{2,1,0:T(8,128)(2,1)}, u32[]{:S(2)}, u32[]{:S(2)}) collective-permute-start(bf16[2,48,1696]{2,1,0:T(8,128)(2,1)} %fusion.12), channel_id=1, source_target_pairs={{0,1},{1,0},{2,3},{3,2},{4,5},{5,4},{6,7},{7,6},{8,9},{9,8},{10,11... | collective-permute-start | bytes 976904 | tf_op jit(solution)/shard_map/ppermute | solution.py:684
  306.6 2.8 collective-permute-start.17
  309.4 9.9 %collective-permute-start.18 = (f32[8,896]{1,0:T(8,128)S(1)}, f32[8,896]{1,0:T(8,128)S(1)}, u32[]{:S(2)}, u32[]{:S(2)}) collective-permute-start(f32[8,896]{1,0:T(8,128)S(1)} %add.136), channel_id=1, source_target_pairs={{0,16},{8,24},{16,0},{24,8},{1,17},{9,25},{17,1},{25,9},{2,18},{10... | collective-permute-start | bytes 86024 | tf_op jit(solution)/shard_map/ppermute | solution.py:879
  312.6 40.8 %all-to-all-start.3 = ((bf16[16,64,768]{2,1,0:T(8,128)(2,1)}), bf16[16,64,768]{2,1,0:T(8,128)(2,1)S(1)}, u32[]{:S(2)}, u32[]{:S(2)}) async-start(bf16[16,64,768]{2,1,0:T(8,128)(2,1)} %shard_map.279), calls=%async_computation.3 | async-start | bytes 3145728 | tf_op jit(solution)/shard_map/all_to_all | solution.py:867
  319.3 9.5 %collective-permute-start.31 = (bf16[2,48,1696]{2,1,0:T(8,128)(2,1)}, bf16[2,48,1696]{2,1,0:T(8,128)(2,1)}, u32[]{:S(2)}, u32[]{:S(2)}) collective-permute-start(bf16[2,48,1696]{2,1,0:T(8,128)(2,1)} %fusion.13), channel_id=1, source_target_pairs={{0,4},{4,0},{1,5},{5,1},{2,6},{6,2},{3,7},{7,3},{8,12},{12,8},{9,1... | collective-permute-start | bytes 976904 | tf_op jit(solution)/shard_map/ppermute | solution.py:684
  320.5 5.2 %collective-permute-start.19 = (f32[8,896]{1,0:T(8,128)S(1)}, f32[8,896]{1,0:T(8,128)S(1)}, u32[]{:S(2)}, u32[]{:S(2)}) collective-permute-start(f32[8,896]{1,0:T(8,128)S(1)} %add.137), channel_id=1, source_target_pairs={{0,2},{2,0},{1,3},{3,1},{4,6},{6,4},{5,7},{7,5},{8,10},{10,8},{9,1... | collective-permute-start | bytes 86024 | tf_op jit(solution)/shard_map/ppermute | solution.py:684
  330.8 25.3 %copy-start.10 = (f32[2,48,1696]{2,1,0:T(8,128)S(1)}, f32[2,48,1696]{2,1,0:T(8,128)}, u32[]{:S(2)}) copy-start(f32[2,48,1696]{2,1,0:T(8,128)} %copy-done.9) | copy-start | bytes 1953796
  354.6 4.5 %collective-permute-start.29 = (bf16[48,1696]{1,0:T(8,128)(2,1)}, bf16[48,1696]{1,0:T(8,128)(2,1)S(1)}, u32[]{:S(2)}, u32[]{:S(2)}) collective-permute-start(bf16[48,1696]{1,0:T(8,128)(2,1)} %shard_map.287), channel_id=1, source_target_pairs={{0,8},{8,16},{16,24},{24,0},{1,9},{9,17},{17,25},{25,1},{2,10},{10... | collective-permute-start | bytes 488456 | tf_op jit(solution)/shard_map/ppermute | solution.py:746
  354.6 8.1 %collective-permute-start.32 = (bf16[48,1696]{1,0:T(8,128)(2,1)}, bf16[48,1696]{1,0:T(8,128)(2,1)S(1)}, u32[]{:S(2)}, u32[]{:S(2)}) collective-permute-start(bf16[48,1696]{1,0:T(8,128)(2,1)} %shard_map.289), channel_id=1, source_target_pairs={{0,16},{8,24},{16,0},{24,8},{1,17},{9,25},{17,1},{25,9},{2,18},{10... | collective-permute-start | bytes 488456 | tf_op jit(solution)/shard_map/ppermute | solution.py:746
  355.8 15.8 %collective-permute-start.33 = (bf16[48,1696]{1,0:T(8,128)(2,1)}, bf16[48,1696]{1,0:T(8,128)(2,1)S(1)}, u32[]{:S(2)}, u32[]{:S(2)}) collective-permute-start(bf16[48,1696]{1,0:T(8,128)(2,1)} %shard_map.290), channel_id=1, source_target_pairs={{0,24},{8,0},{16,8},{24,16},{1,25},{9,1},{17,9},{25,17},{2,26},{10... | collective-permute-start | bytes 488456 | tf_op jit(solution)/shard_map/ppermute | solution.py:746
  356.8 29.5 %copy-start.5 = (bf16[16,64,768]{2,1,0:T(8,128)(2,1)S(1)}, bf16[16,64,768]{2,1,0:T(8,128)(2,1)}, u32[]{:S(2)}) copy-start(bf16[16,64,768]{2,1,0:T(8,128)(2,1)} %copy-done.4) | copy-start | bytes 4718596
  372.7 14.8 %copy-start.1 = (bf16[16,64,768]{2,1,0:T(8,128)(2,1)S(1)}, bf16[16,64,768]{2,1,0:T(8,128)(2,1)}, u32[]{:S(2)}) copy-start(bf16[16,64,768]{2,1,0:T(8,128)(2,1)} %copy-done) | copy-start | bytes 4718596
  373.4 1.7 collective-permute-start.34
  376.5 7.7 %collective-permute-start.35 = (bf16[48,2464]{1,0:T(8,128)(2,1)}, bf16[48,2464]{1,0:T(8,128)(2,1)S(1)}, u32[]{:S(2)}, u32[]{:S(2)}) collective-permute-start(bf16[48,2464]{1,0:T(8,128)(2,1)} %pad_maximum_fusion.2), channel_id=1, source_target_pairs={{0,0},{1,2},{2,1},{3,3},{4,4},{5,6},{6,5},{7,7},{8,8},{9,10},{10,9... | collective-permute-start | bytes 709640 | tf_op jit(solution)/shard_map/ppermute | solution.py:688
  (32 other events, 120.2 us)

commit v3 on v2

--- a/solution.py
+++ b/solution.py
@@ -372,11 +372,11 @@
             prod = jnp.sum(dsb[hs, :] * sbin[q, hs, :].astype(F32), axis=0, keepdims=True)
             row[1, h1, :] = jnp.broadcast_to(jnp.sum(prod, axis=1, keepdims=True) * etb[h1, :], (1, CH))
             dx = dxp[hs, lanes] + raw * mw[h1, :]
-            du[hs, lanes] = dx * (sg * (1.0 + uh * (1.0 - sg)))
+            du[hs, lanes] = (dx * (sg * (1.0 + uh * (1.0 - sg)))).astype(BF)
             vbe[hs, :] = (x * mw[h1, :]).astype(BF)
         db = dbc[0:64, lanes] + tn(dsb16, vbe[...])
-        du[inner : inner + 64, lanes] = db * (sgb * (1.0 + bu * (1.0 - sgb)))
-        du[inner + 64 : inner + 128, lanes] = dbc[64:128, lanes] * (sgc * (1.0 + cu * (1.0 - sgc)))
+        du[inner : inner + 64, lanes] = (db * (sgb * (1.0 + bu * (1.0 - sgb)))).astype(BF)
+        du[inner + 64 : inner + 128, lanes] = (dbc[64:128, lanes] * (sgc * (1.0 + cu * (1.0 - sgc)))).astype(BF)
         for h in range(heads):
             hs = slice(64 * h, 64 * h + 64)
             dsb[hs, :] = dsb[hs, :] * etb[h : h + 1, :] + zb[q, hs, :].astype(F32)
@@ -409,15 +409,16 @@
     cat[0:inner, :] = dgate[...]
     for g in range(0, conv, 128):
         cur = du[g : g + 128, :]
-        after = jnp.where(j == last, 0.0, nxt[g : g + 128, :])
-        full = jnp.concatenate([cur, after], 1)
+        after = nxt[g : g + 128, :]
+        full = jnp.concatenate([cur, jnp.where(j == last, jnp.zeros_like(after), after)], 1)
+        cur = cur.astype(F32)
         a = ain[g : g + 128, :].astype(F32)
         t = taps[g : g + 128, :]
         total = t[:, 3:4] * cur
         p = a * cur
         dtaps[3, g : g + 128, :] += p[:, 0:128] + p[:, 128:256]
         for k in (1, 2, 3):
-            moved = pltpu.roll(full, BLK + 128 - k, 1)[:, 0:BLK]
+            moved = pltpu.roll(full, BLK + 128 - k, 1)[:, 0:BLK].astype(F32)
             total = total + t[:, 3 - k : 4 - k] * moved
             p = a * moved
             dtaps[3 - k, g : g + 128, :] += p[:, 0:128] + p[:, 128:256]
@@ -596,7 +597,7 @@
                 pltpu.VMEM((2, 16, CH), F32),
             ],
         ),
-        out_shape=[sds((inner + 128, length), F32), sds((ZR, length), BF), sds((ZR, CH), F32), sds((ZR, CH), F32)],
+        out_shape=[sds((inner + 128, length), BF), sds((ZR, length), BF), sds((ZR, CH), F32), sds((ZR, CH), F32)],
         compiler_params=_params(),
         cost_estimate=pl.CostEstimate(flops=10**9, bytes_accessed=30_000_000, transcendentals=10**6),
     )(meta, u, zt, alog, dxp, ddt, dap, dbc, zb, sbin)
@@ -716,9 +717,9 @@
     a, b = jnp.stack(got[:ahead]), jnp.stack(got[ahead:])
     a = after(a, moved, b, wide=True)
     b = after(b, a)
-    both = [(i, 3 - i) for i in range(4)]
-    by, bx, bxy = twin(b, "tensor"), twin(b, "x"), lax.ppermute(b, ("x", "tensor"), both)
-    ax, ay, axy = twin(a, "x"), twin(a, "tensor"), lax.ppermute(a, ("x", "tensor"), both)
+    by, bx = twin(b, "tensor"), twin(b, "x")
+    ax, ay = twin(a, "x"), twin(a, "tensor")
+    axy, bxy = twin(ax, "tensor"), twin(by, "x")
     near = [(0, ahead, 0, 0), (0, ahead, 1, 0), (0, ahead, 0, 1), (0, ahead, 1, 1)]
     far = [(ahead, behind, 0, 0), (ahead, behind, 0, 1), (ahead, behind, 1, 0), (ahead, behind, 1, 1)]
     return [a, ax, ay, axy, b, by, bx, bxy], near + far, moved, [ax, ay, axy, by, bx, bxy]
@@ -768,6 +769,23 @@
             for piece in g:
                 total = add(total, piece)
             self.now = [total]
+
+
+def unpack(grads, inner, heads):
+    rows = grads.shape[0]
+
+    def body(src, out, gate, mid, bc, dt):
+        out[...] = src[:, 0:inner].astype(F32)
+        gate[...] = src[:, inner : 2 * inner].astype(F32)
+        mid[...] = src[:, 2 * inner : 3 * inner].astype(F32)
+        bc[...] = src[:, 3 * inner : 3 * inner + 128].astype(F32)
+        r = lax.broadcasted_iota(jnp.int32, (ZR, 2 * heads), 0)
+        c = lax.broadcasted_iota(jnp.int32, (ZR, 2 * heads), 1)
+        pick = jnp.where(r == (c & 1) * 16 + (c >> 1), 1.0, 0.0).astype(BF)
+        dt[...] = nn(src[:, 3 * inner + 128 : 3 * inner + 128 + ZR], pick)
+
+    shapes = [(rows, inner), (rows, inner), (rows, inner), (rows, 128), (rows, 2 * heads)]
+    return pl.pallas_call(body, out_shape=[sds(s, F32) for s in shapes], compiler_params=pltpu.CompilerParams(vmem_limit_bytes=VMEM_LIMIT))(grads)
 
 
 def pad_rows(fwd, bwd):
@@ -889,13 +907,8 @@
     bc_part = gw_sum[:, 2 * inner : 2 * inner + 128]
     bc_part = bc_part + twin(bc_part, "core")
     grads = jnp.concatenate([gwo_sum, gw_sum[:, : 2 * inner], bc_part, gw_sum[:, 2 * inner + 128 :]], 1)
-    grads = corner(grads.astype(BF)).astype(F32)
-    out_sum = grads[:, :inner].T
-    gate_sum = grads[:, inner : 2 * inner]
-    inner_sum = grads[:, 2 * inner : 3 * inner]
-    bc_sum = grads[:, 3 * inner : 3 * inner + 128]
-    dt_sum = grads[:, 3 * inner + 128 :].reshape(rows, 2, 16)[:, :, :heads]
-    dt_sum = jnp.transpose(dt_sum, (0, 2, 1)).reshape(rows, 2 * heads)
+    grads = corner(grads.astype(BF))
+    out_sum, gate_sum, inner_sum, bc_sum, dt_sum = unpack(grads, inner, heads)
 
     here = jnp.where(core == y, small, pair)
     joint = small + pair
@@ -914,7 +927,7 @@
         heads_of(128).sum(0),
         here[6, 256 : 256 + heads],
         here[4, :inner],
-        out_sum,
+        out_sum.T,
     )
 
 

time: 390 us -> 378 us (0.969)
  waiting for transfers between devices: 114 us -> 105 us
    ppermute x2 -> x0, waiting for transfers between devices: 14 us -> none  [the longest x1 11.2 us: gather_weights(): lax.ppermute(a, ('x', 'tensor'), both)]
    ppermute x20 -> x22, waiting for transfers between devices: 42.2 us -> 47.1 us  [twin(): return lax.ppermute(v, axis, SWAP)]
    pallas_call x1, Pallas kernels: 30.1 us -> 26.1 us  [run_weigh(): pl.pallas_call(weigh, grid_spec=pltpu.PrefetchScalarGridSpec(num_scalar_p...]
    unnamed x88 -> x97, local copies, waits for them, and re-layouts: 12.6 us -> 16.3 us
    ppermute x20 -> x22, starting transfers between devices: 22.4 us -> 22.4 us  [twin(): return lax.ppermute(v, axis, SWAP)]
  transfers between devices with their start and end apart: 40 -> 40, of which waited for: 18 -> 17; matrix products, arithmetic and copies ran while one was open for 11% -> 12% of each run, Pallas kernels for 24% -> 23%
where the time goes in v3:
time: 378 us; the launch traced here: 376 us
  Pallas kernels  142 us (38%)
  waiting for transfers between devices  105 us (28%)
  starting transfers between devices  63.3 us (17%)
  local copies, waits for them, and re-layouts  33 us (9%)
  other arithmetic  30.8 us (8%)
    pallas_call x1, Pallas kernels, run_mix(): pl.pallas_call(mix, grid_spec=pltpu.PrefetchScalarGridSpec(num_scalar_pre...  53.7 us
    ppermute x22, waiting for transfers between devices, twin(): return lax.ppermute(v, axis, SWAP)  47.1 us
    pallas_call x1, Pallas kernels, run_enter(): pl.pallas_call(functools.partial(enter, near), grid_spec=pltpu.PrefetchSc...  29.3 us
    pallas_call x1, Pallas kernels, run_weigh(): pl.pallas_call(weigh, grid_spec=pltpu.PrefetchScalarGridSpec(num_scalar_p...  26.1 us
    all_to_all x1, waiting for transfers between devices, shards(): input_grad = lax.all_to_all(after(back, output), group, 0, 0, tiled=True)  22.6 us
    ppermute x22, starting transfers between devices, twin(): return lax.ppermute(v, axis, SWAP)  22.4 us
    unnamed x97, local copies, waits for them, and re-layouts  16.3 us
    pallas_call x1, Pallas kernels, run_carry(): pl.pallas_call(carry, grid_spec=pltpu.PrefetchScalarGridSpec(num_scalar_p...  15.4 us
  transfers between devices with their start and end apart: 40, of which 17 were waited for; matrix products, arithmetic and copies ran while one was open for 12% of the time, Pallas kernels for 23%

profile of v3, /device:TPU:9, one launch (start us, length us, event | category | flops | bytes accessed | tf_op | source)
XLA Modules:
  0.0 376.1 jit_solution(13514833478350666818)
XLA Ops:
  0.7 2.8 copy.168
  3.7 3.7 collective-permute-start
  7.4 4.2 %collective-permute-done = bf16[48,2560]{1,0:T(8,128)(2,1)S(1)} collective-permute-done((bf16[48,2560]{1,0:T(8,128)(2,1)S(1)}, bf16[48,2560]{1,0:T(8,128)(2,1)S(1)}, u32[]{:S(2)}, u32[]{:S(2)}) %collective-permute-start) | collective-permute-done | bytes 245792 | tf_op jit(solution)/shard_map/ppermute | solution.py:689
  11.6 1.3 collective-permute-start.1
  15.7 3.3 shard_map.263.refs_0_
  19.0 6.9 %collective-permute-done.1.refs_1_ = bf16[48,2560]{1,0:T(8,128)(2,1)S(1)} collective-permute-done((bf16[48,2560]{1,0:T(8,128)(2,1)S(1)}, bf16[48,2560]{1,0:T(8,128)(2,1)S(1)}, u32[]{:S(2)}, u32[]{:S(2)}) %collective-permute-start.1) | collective-permute-done | bytes 245792 | tf_op jit(solution)/shard_map/ppermute | solution.py:715
  25.9 2.6 collective-permute-done.2.refs_2_
  30.4 5.8 %all-to-all-start = ((bf16[16,64,768]{2,1,0:T(8,128)(2,1)}), bf16[16,64,768]{2,1,0:T(8,128)(2,1)S(1)}, u32[]{:S(2)}, u32[]{:S(2)}) async-start(bf16[16,64,768]{2,1,0:T(8,128)(2,1)} %shard_map.264.refs_1_), calls=%async_computation | async-start | bytes 3145728 | tf_op jit(solution)/shard_map/all_to_all | solution.py:845
  40.8 22.2 %collective-permute-done.7.refs_4_.refs_5_ = bf16[2,48,2560]{2,1,0:T(8,128)(2,1)S(1)} collective-permute-done((bf16[2,48,2560]{2,1,0:T(8,128)(2,1)}, bf16[2,48,2560]{2,1,0:T(8,128)(2,1)S(1)}, u32[]{:S(2)}, u32[]{:S(2)}) %collective-permute-start.7) | collective-permute-done | bytes 491552 | tf_op jit(solution)/shard_map/ppermute | solution.py:685
  63.0 1.5 collective-permute-start.9
  64.8 11.0 %collective-permute-done.8.refs_5_.refs_6_ = bf16[2,48,2560]{2,1,0:T(8,128)(2,1)S(1)} collective-permute-done((bf16[2,48,2560]{2,1,0:T(8,128)(2,1)}, bf16[2,48,2560]{2,1,0:T(8,128)(2,1)S(1)}, u32[]{:S(2)}, u32[]{:S(2)}) %collective-permute-start.8) | collective-permute-done | bytes 491552 | tf_op jit(solution)/shard_map/ppermute | solution.py:685
  75.8 10.5 %collective-permute-done.9.refs_6_.refs_7_ = bf16[2,48,2560]{2,1,0:T(8,128)(2,1)S(1)} collective-permute-done((bf16[2,48,2560]{2,1,0:T(8,128)(2,1)S(1)}, bf16[2,48,2560]{2,1,0:T(8,128)(2,1)S(1)}, u32[]{:S(2)}, u32[]{:S(2)}) %collective-permute-start.9) | collective-permute-done | bytes 491552 | tf_op jit(solution)/shard_map/ppermute | solution.py:685
  87.9 5.5 %all-to-all-start.1 = ((bf16[16,64,768]{2,1,0:T(8,128)(2,1)}), bf16[16,64,768]{2,1,0:T(8,128)(2,1)S(1)}, u32[]{:S(2)}, u32[]{:S(2)}) async-start(bf16[16,64,768]{2,1,0:T(8,128)(2,1)} %shard_map.268), calls=%async_computation.1 | async-start | bytes 3145728 | tf_op jit(solution)/shard_map/all_to_all | solution.py:849
  93.6 2.0 collective-permute-start.11
  95.8 3.5 collective-permute-start.10
  100.5 1.2 stack.47.meta
  101.7 4.2 %collective-permute-done.10 = f32[8,768]{1,0:T(8,128)S(1)} collective-permute-done((f32[8,768]{1,0:T(8,128)S(1)}, f32[8,768]{1,0:T(8,128)S(1)}, u32[]{:S(2)}, u32[]{:S(2)}) %collective-permute-start.10) | collective-permute-done | bytes 24608 | tf_op jit(solution)/shard_map/ppermute | solution.py:689
  108.4 29.3 %shard_map.269 = (bf16[2048,768]{1,0:T(8,128)(2,1)}, f32[768,2048]{1,0:T(8,128)}, bf16[896,2048]{1,0:T(8,128)(2,1)}, f32[896,2048]{1,0:T(8,128)}, f32[32,2048]{1...) custom-call(s32[6]{0:T(128)} %stack.47.meta, ...), custom_call_target="tpu_custom_call" | custom-call | flops 5335154688 | bytes 30000000 | tf_op jit(solution)/shard_map/pallas_call | solution.py:471
  140.6 1.9 collective-permute-done.12.dyb
  143.7 53.7 %shard_map.271 = (f32[16,64,768]{2,1,0:T(8,128)}, bf16[16,64,768]{2,1,0:T(8,128)(2,1)}, bf16[768,2048]{1,0:T(8,128)(2,1)}, f32[768,2048]{1,0:T(8,128)}, f32[32,2...) custom-call(s32[6]{0:T(128)} %stack.47.meta, ...), custom_call_target="tpu_custom_call" | custom-call | flops 40000000000 | bytes 50000000 | tf_op jit(solution)/shard_map/pallas_call | solution.py:521
  197.6 15.4 %shard_map.273 = (bf16[896,2048]{1,0:T(8,128)(2,1)}, bf16[32,2048]{1,0:T(8,128)(2,1)}, f32[32,128]{1,0:T(8,128)}, f32[32,128]{1,0:T(8,128)}) custom-call(s32[6]{0:T(128)} %stack.47.meta, f32[896,2048]{1,0:T(8,128)} %get-tuple-element.57.u, f32[32,2048]{1,0:T(8,128)} %get-tuple-element.54.refs_1_.zt, f32[32,1]{1,0:T(8,128)} %get-tuple-element.208.refs_11_.alog, ...), custom_call_target="tpu_custom_call" | custom-call | flops 1000000000 | bytes 30000000 | tf_op jit(solution)/shard_map/pallas_call | solution.py:586
  214.4 3.9 %fusion.8 = (f32[16,64]{1,0:T(8,128)S(1)}, bf16[16,64,768]{2,1,0:T(8,128)(2,1)}) fusion(bf16[16,64,768]{2,1,0:T(8,128)(2,1)S(1)} %copy-done.3, f32[16,64,768]{2,1,0:T(8,128)} %shard_map.274, bf16[16,64,768]{2,1,0:T(8,128)(2,1)S(1)} %collective-permute-done.13, f32[16,64]{1,0:T(8,128)S(1)} %fusion.24), kind=kLoop, calls=%fused_computation.11 | loop fusion | flops 6290432 | bytes 7872512 | tf_op jit(solution)/shard_map/reduce_sum | solution.py:880
  218.3 3.8 %all-to-all-start.2 = ((bf16[16,64,768]{2,1,0:T(8,128)(2,1)}), bf16[16,64,768]{2,1,0:T(8,128)(2,1)S(1)}, u32[]{:S(2)}, u32[]{:S(2)}) async-start(bf16[16,64,768]{2,1,0:T(8,128)(2,1)} %get-tuple-element.197.refs_1_), calls=%async_computation.2 | async-start | bytes 3145728 | tf_op jit(solution)/shard_map/all_to_all | solution.py:866
  222.1 26.1 %shard_map.276 = (bf16[1696,2048]{1,0:T(8,128)(2,1)}, f32[8,896]{1,0:T(8,128)}, bf16[2,2,48,1696]{3,2,1,0:T(8,128)(2,1)}, bf16[2,2,48,1696]{3,2,1,0:T(8,128)(2,1...) custom-call(s32[6]{0:T(128)} %stack.47.meta, bf16[896,2048]{1,0:T(8,128)(2,1)} %shard_map.275.du.nxt, ...), custom_call_target="tpu_custom_call" | custom-call | flops 5335154688 | bytes 30000000 | tf_op jit(solution)/shard_map/pallas_call | solution.py:613
  248.3 1.2 collective-permute-start.15
  249.5 12.7 %shard_map.278 = (f32[16,64,768]{2,1,0:T(8,128)}, bf16[16,64,768]{2,1,0:T(8,128)(2,1)}) custom-call(s32[6]{0:T(128)} %stack.47.meta, bf16[1696,2048]{1,0:T(8,128)(2,1)} %shard_map.277.cat, bf16[1696,768]{1,0:T(8,128)(2,1)} %get-tuple-element.72.wt), custom_call_target="tpu_custom_call" | custom-call | flops 1000000 | bytes 20000000 | tf_op jit(solution)/shard_map/pallas_call | solution.py:647
  262.2 1.8 collective-permute-start.14
  267.9 1.2 collective-permute-start.21
  270.3 1.7 slice_bitcast_fusion.3.refs_0_
  273.0 3.4 fusion.2
  276.8 3.7 fusion.6.refs_0_.refs_1_
  282.2 2.1 collective-permute-start.25
  288.8 1.4 convert_add_fusion.2
  292.0 2.6 convert_add_fusion.1
  294.7 2.1 collective-permute-start.18
  298.0 4.9 %all-to-all-start.3 = ((bf16[16,64,768]{2,1,0:T(8,128)(2,1)}), bf16[16,64,768]{2,1,0:T(8,128)(2,1)S(1)}, u32[]{:S(2)}, u32[]{:S(2)}) async-start(bf16[16,64,768]{2,1,0:T(8,128)(2,1)} %shard_map.279), calls=%async_computation.3 | async-start | bytes 3145728 | tf_op jit(solution)/shard_map/all_to_all | solution.py:885
  302.9 1.9 fusion.13
  306.0 4.2 %collective-permute-start.19 = (f32[8,896]{1,0:T(8,128)S(1)}, f32[8,896]{1,0:T(8,128)S(1)}, u32[]{:S(2)}, u32[]{:S(2)}) collective-permute-start(f32[8,896]{1,0:T(8,128)S(1)} %add.137), channel_id=1, source_target_pairs={{0,2},{2,0},{1,3},{3,1},{4,6},{6,4},{5,7},{7,5},{8,10},{10,8},{9,1... | collective-permute-start | bytes 86024 | tf_op jit(solution)/shard_map/ppermute | solution.py:685
  314.3 1.2 fusion.10
  316.3 22.6 %all-to-all-done.3.refs_1_ = bf16[16,64,768]{2,1,0:T(8,128)(2,1)S(1)} async-done(((bf16[16,64,768]{2,1,0:T(8,128)(2,1)}), bf16[16,64,768]{2,1,0:T(8,128)(2,1)S(1)}, u32[]{:S(2)}, u32[]{:S(2)}) %all-to-all-start.3) | async-done | bytes 1572896 | tf_op jit(solution)/shard_map/all_to_all | solution.py:885
  342.3 2.2 collective-permute-done.29
  344.5 3.6 collective-permute-done.32
  348.2 9.0 %collective-permute-done.33 = bf16[48,1696]{1,0:T(8,128)(2,1)} collective-permute-done((bf16[48,1696]{1,0:T(8,128)(2,1)}, bf16[48,1696]{1,0:T(8,128)(2,1)}, u32[]{:S(2)}, u32[]{:S(2)}) %collective-permute-start.33) | collective-permute-done | bytes 162848 | tf_op jit(solution)/shard_map/ppermute | solution.py:747
  357.2 1.3 fusion.26
  362.3 3.1 collective-permute-start.35
  368.3 1.7 collective-permute-done.35.src
  370.7 1.7 shard_map.291
  372.4 1.4 copy.137
  (235 shorter events, 55.8 us)
Async XLA Ops:
  0.6 14.4 %copy-start.41 = (s32[16]{0:T(128)S(1)}, s32[16]{0:T(128)}, u32[]{:S(2)}) copy-start(s32[16]{0:T(128)} %param.19) | copy-start | bytes 196
  3.7 7.9 %collective-permute-start = (bf16[48,2560]{1,0:T(8,128)(2,1)S(1)}, bf16[48,2560]{1,0:T(8,128)(2,1)S(1)}, u32[]{:S(2)}, u32[]{:S(2)}) collective-permute-start(bf16[48,2560]{1,0:T(8,128)(2,1)S(1)} %pad_dynamic-update-slice_fusion), channel_id=1, source_target_pairs={{0,0},{1,2},{2,1},{3,3},{4,4},{5,6},{6,5},{7,7},{8,8},{9,10},{10,9... | collective-permute-start | bytes 737288 | tf_op jit(solution)/shard_map/ppermute | solution.py:689
  11.6 14.3 %collective-permute-start.1 = (bf16[48,2560]{1,0:T(8,128)(2,1)S(1)}, bf16[48,2560]{1,0:T(8,128)(2,1)S(1)}, u32[]{:S(2)}, u32[]{:S(2)}) collective-permute-start(bf16[48,2560]{1,0:T(8,128)(2,1)S(1)} %collective-permute-done), channel_id=1, source_target_pairs={{0,8},{8,16},{16,24},{24,0},{1,9},{9,17},{17,25},{25,1},{2,10},{10... | collective-permute-start | bytes 737288 | tf_op jit(solution)/shard_map/ppermute | solution.py:715
  12.9 15.6 %collective-permute-start.2 = (bf16[48,2560]{1,0:T(8,128)(2,1)S(1)}, bf16[48,2560]{1,0:T(8,128)(2,1)S(1)}, u32[]{:S(2)}, u32[]{:S(2)}) collective-permute-start(bf16[48,2560]{1,0:T(8,128)(2,1)S(1)} %collective-permute-done), channel_id=1, source_target_pairs={{0,16},{8,24},{16,0},{24,8},{1,17},{9,25},{17,1},{25,9},{2,18},{10... | collective-permute-start | bytes 737288 | tf_op jit(solution)/shard_map/ppermute | solution.py:715
  13.8 15.8 %collective-permute-start.3 = (bf16[48,2560]{1,0:T(8,128)(2,1)S(1)}, bf16[48,2560]{1,0:T(8,128)(2,1)S(1)}, u32[]{:S(2)}, u32[]{:S(2)}) collective-permute-start(bf16[48,2560]{1,0:T(8,128)(2,1)S(1)} %collective-permute-done), channel_id=1, source_target_pairs={{0,24},{8,0},{16,8},{24,16},{1,25},{9,1},{17,9},{25,17},{2,26},{10... | collective-permute-start | bytes 737288 | tf_op jit(solution)/shard_map/ppermute | solution.py:715
  30.4 57.5 %all-to-all-start = ((bf16[16,64,768]{2,1,0:T(8,128)(2,1)}), bf16[16,64,768]{2,1,0:T(8,128)(2,1)S(1)}, u32[]{:S(2)}, u32[]{:S(2)}) async-start(bf16[16,64,768]{2,1,0:T(8,128)(2,1)} %shard_map.264.refs_1_), calls=%async_computation | async-start | bytes 3145728 | tf_op jit(solution)/shard_map/all_to_all | solution.py:845
  37.9 25.2 %collective-permute-start.7 = (bf16[2,48,2560]{2,1,0:T(8,128)(2,1)}, bf16[2,48,2560]{2,1,0:T(8,128)(2,1)S(1)}, u32[]{:S(2)}, u32[]{:S(2)}) collective-permute-start(bf16[2,48,2560]{2,1,0:T(8,128)(2,1)} %shard_map.266.refs_4_), channel_id=1, source_target_pairs={{0,1},{1,0},{2,3},{3,2},{4,5},{5,4},{6,7},{7,6},{8,9},{9,8},{10,11... | collective-permute-start | bytes 1474568 | tf_op jit(solution)/shard_map/ppermute | solution.py:685
  39.1 25.4 %collective-permute-start.4 = (bf16[2,48,2560]{2,1,0:T(8,128)(2,1)}, bf16[2,48,2560]{2,1,0:T(8,128)(2,1)S(1)}, u32[]{:S(2)}, u32[]{:S(2)}) collective-permute-start(bf16[2,48,2560]{2,1,0:T(8,128)(2,1)} %shard_map.265.refs_1_.refs_0_), channel_id=1, source_target_pairs={{0,4},{4,0},{1,5},{5,1},{2,6},{6,2},{3,7},{7,3},{8,12},{12,8},{9,1... | collective-permute-start | bytes 1474568 | tf_op jit(solution)/shard_map/ppermute | solution.py:685
  40.2 35.5 %collective-permute-start.8 = (bf16[2,48,2560]{2,1,0:T(8,128)(2,1)}, bf16[2,48,2560]{2,1,0:T(8,128)(2,1)S(1)}, u32[]{:S(2)}, u32[]{:S(2)}) collective-permute-start(bf16[2,48,2560]{2,1,0:T(8,128)(2,1)} %shard_map.266.refs_4_), channel_id=1, source_target_pairs={{0,4},{4,0},{1,5},{5,1},{2,6},{6,2},{3,7},{7,3},{8,12},{12,8},{9,1... | collective-permute-start | bytes 1474568 | tf_op jit(solution)/shard_map/ppermute | solution.py:685
  40.5 35.2 %collective-permute-start.5 = (bf16[2,48,2560]{2,1,0:T(8,128)(2,1)}, bf16[2,48,2560]{2,1,0:T(8,128)(2,1)S(1)}, u32[]{:S(2)}, u32[]{:S(2)}) collective-permute-start(bf16[2,48,2560]{2,1,0:T(8,128)(2,1)} %shard_map.265.refs_1_.refs_0_), channel_id=1, source_target_pairs={{0,1},{1,0},{2,3},{3,2},{4,5},{5,4},{6,7},{7,6},{8,9},{9,8},{10,11... | collective-permute-start | bytes 1474568 | tf_op jit(solution)/shard_map/ppermute | solution.py:685
  63.0 24.8 %copy-start.11 = (bf16[2,48,2560]{2,1,0:T(8,128)(2,1)}, bf16[2,48,2560]{2,1,0:T(8,128)(2,1)S(1)}, u32[]{:S(2)}) copy-start(bf16[2,48,2560]{2,1,0:T(8,128)(2,1)S(1)} %collective-permute-done.7.refs_4_.refs_5_) | copy-start | bytes 1474564
  63.0 23.2 %collective-permute-start.9 = (bf16[2,48,2560]{2,1,0:T(8,128)(2,1)S(1)}, bf16[2,48,2560]{2,1,0:T(8,128)(2,1)S(1)}, u32[]{:S(2)}, u32[]{:S(2)}) collective-permute-start(bf16[2,48,2560]{2,1,0:T(8,128)(2,1)S(1)} %collective-permute-done.7.refs_4_.refs_5_), channel_id=1, source_target_pairs={{0,4},{4,0},{1,5},{5,1},{2,6},{6,2},{3,7},{7,3},{8,12},{12,8},{9,1... | collective-permute-start | bytes 1474568 | tf_op jit(solution)/shard_map/ppermute | solution.py:685
  64.5 23.4 %copy-start.12 = (bf16[2,48,2560]{2,1,0:T(8,128)(2,1)}, bf16[2,48,2560]{2,1,0:T(8,128)(2,1)S(1)}, u32[]{:S(2)}) copy-start(bf16[2,48,2560]{2,1,0:T(8,128)(2,1)S(1)} %collective-permute-done.4.refs_1_) | copy-start | bytes 1474564
  64.5 21.8 %collective-permute-start.6 = (bf16[2,48,2560]{2,1,0:T(8,128)(2,1)S(1)}, bf16[2,48,2560]{2,1,0:T(8,128)(2,1)S(1)}, u32[]{:S(2)}, u32[]{:S(2)}) collective-permute-start(bf16[2,48,2560]{2,1,0:T(8,128)(2,1)S(1)} %collective-permute-done.4.refs_1_), channel_id=1, source_target_pairs={{0,1},{1,0},{2,3},{3,2},{4,5},{5,4},{6,7},{7,6},{8,9},{9,8},{10,11... | collective-permute-start | bytes 1474568 | tf_op jit(solution)/shard_map/ppermute | solution.py:685
  87.9 49.8 %all-to-all-start.1 = ((bf16[16,64,768]{2,1,0:T(8,128)(2,1)}), bf16[16,64,768]{2,1,0:T(8,128)(2,1)S(1)}, u32[]{:S(2)}, u32[]{:S(2)}) async-start(bf16[16,64,768]{2,1,0:T(8,128)(2,1)} %shard_map.268), calls=%async_computation.1 | async-start | bytes 3145728 | tf_op jit(solution)/shard_map/all_to_all | solution.py:849
  93.5 13.2 %copy-start.37 = (f32[4,128]{1,0:T(4,128)S(1)}, f32[4,128]{1,0:T(4,128)}, u32[]{:S(2)}) copy-start(f32[4,128]{1,0:T(4,128)} %param.26) | copy-start | bytes 6148
  93.6 14.9 %collective-permute-start.11 = (bf16[16,64,768]{2,1,0:T(8,128)(2,1)}, bf16[16,64,768]{2,1,0:T(8,128)(2,1)}, u32[]{:S(2)}, u32[]{:S(2)}) collective-permute-start(bf16[16,64,768]{2,1,0:T(8,128)(2,1)} %shard_map.267.xa), channel_id=1, source_target_pairs={{0,2},{2,0},{1,3},{3,1},{4,6},{6,4},{5,7},{7,5},{8,10},{10,8},{9,1... | collective-permute-start | bytes 4718600 | tf_op jit(solution)/shard_map/ppermute | solution.py:685
  95.8 10.1 %collective-permute-start.10 = (f32[8,768]{1,0:T(8,128)S(1)}, f32[8,768]{1,0:T(8,128)S(1)}, u32[]{:S(2)}, u32[]{:S(2)}) collective-permute-start(f32[8,768]{1,0:T(8,128)S(1)} %maximum_maximum_fusion), channel_id=1, source_target_pairs={{0,0},{1,2},{2,1},{3,3},{4,4},{5,6},{6,5},{7,7},{8,8},{9,10},{10,9... | collective-permute-start | bytes 73736 | tf_op jit(solution)/shard_map/ppermute | solution.py:689
  138.9 3.6 collective-permute-start.12
  197.4 16.9 %collective-permute-start.13 = (bf16[16,64,768]{2,1,0:T(8,128)(2,1)}, bf16[16,64,768]{2,1,0:T(8,128)(2,1)S(1)}, u32[]{:S(2)}, u32[]{:S(2)}) collective-permute-start(bf16[16,64,768]{2,1,0:T(8,128)(2,1)} %get-tuple-element.67), channel_id=1, source_target_pairs={{0,2},{2,0},{1,3},{3,1},{4,6},{6,4},{5,7},{7,5},{8,10},{10,8},{9,1... | collective-permute-start | bytes 4718600 | tf_op jit(solution)/shard_map/ppermute | solution.py:685
  213.0 51.0 %collective-permute-start.23 = (bf16[2,2,48,768]{3,2,1,0:T(8,128)(2,1)}, bf16[2,2,48,768]{3,2,1,0:T(8,128)(2,1)}, u32[]{:S(2)}, u32[]{:S(2)}) collective-permute-start(bf16[2,2,48,768]{3,2,1,0:T(8,128)(2,1)} %get-tuple-element.84), channel_id=1, source_target_pairs={{0,1},{1,0},{2,3},{3,2},{4,5},{5,4},{6,7},{7,6},{8,9},{9,8},{10,11... | collective-permute-start | bytes 884744 | tf_op jit(solution)/shard_map/ppermute | solution.py:685
  213.1 53.7 %collective-permute-start.20 = (bf16[2,2,48,768]{3,2,1,0:T(8,128)(2,1)}, bf16[2,2,48,768]{3,2,1,0:T(8,128)(2,1)S(1)}, u32[]{:S(2)}, u32[]{:S(2)}) collective-permute-start(bf16[2,2,48,768]{3,2,1,0:T(8,128)(2,1)} %get-tuple-element.82), channel_id=1, source_target_pairs={{0,4},{4,0},{1,5},{5,1},{2,6},{6,2},{3,7},{7,3},{8,12},{12,8},{9,1... | collective-permute-start | bytes 884744 | tf_op jit(solution)/shard_map/ppermute | solution.py:685
  218.3 78.5 %all-to-all-start.2 = ((bf16[16,64,768]{2,1,0:T(8,128)(2,1)}), bf16[16,64,768]{2,1,0:T(8,128)(2,1)S(1)}, u32[]{:S(2)}, u32[]{:S(2)}) async-start(bf16[16,64,768]{2,1,0:T(8,128)(2,1)} %get-tuple-element.197.refs_1_), calls=%async_computation.2 | async-start | bytes 3145728 | tf_op jit(solution)/shard_map/all_to_all | solution.py:866
  248.3 37.4 %collective-permute-start.15 = (f32[8,896]{1,0:T(8,128)}, f32[8,896]{1,0:T(8,128)S(1)}, u32[]{:S(2)}, u32[]{:S(2)}) collective-permute-start(f32[8,896]{1,0:T(8,128)} %get-tuple-element.78.refs_1_.refs_0_), channel_id=1, source_target_pairs={{0,4},{4,0},{1,5},{5,1},{2,6},{6,2},{3,7},{7,3},{8,12},{12,8},{9,1... | collective-permute-start | bytes 86024 | tf_op jit(solution)/shard_map/ppermute | solution.py:685
  249.5 14.5 %copy-start.18 = (bf16[2,2,48,768]{3,2,1,0:T(8,128)(2,1)S(1)}, bf16[2,2,48,768]{3,2,1,0:T(8,128)(2,1)}, u32[]{:S(2)}) copy-start(bf16[2,2,48,768]{3,2,1,0:T(8,128)(2,1)} %shard_map.283) | copy-start | bytes 884740
  262.2 10.5 %collective-permute-start.14 = (bf16[16,64,768]{2,1,0:T(8,128)(2,1)}, bf16[16,64,768]{2,1,0:T(8,128)(2,1)}, u32[]{:S(2)}, u32[]{:S(2)}) collective-permute-start(bf16[16,64,768]{2,1,0:T(8,128)(2,1)} %get-tuple-element.80), channel_id=1, source_target_pairs={{0,2},{2,0},{1,3},{3,1},{4,6},{6,4},{5,7},{7,5},{8,10},{10,8},{9,1... | collective-permute-start | bytes 4718600 | tf_op jit(solution)/shard_map/ppermute | solution.py:685
  266.5 14.0 %collective-permute-start.24 = (bf16[2,48,768]{2,1,0:T(8,128)(2,1)}, bf16[2,48,768]{2,1,0:T(8,128)(2,1)}, u32[]{:S(2)}, u32[]{:S(2)}) collective-permute-start(bf16[2,48,768]{2,1,0:T(8,128)(2,1)} %fusion.16), channel_id=1, source_target_pairs={{0,4},{4,0},{1,5},{5,1},{2,6},{6,2},{3,7},{7,3},{8,12},{12,8},{9,1... | collective-permute-start | bytes 442376 | tf_op jit(solution)/shard_map/ppermute | solution.py:685
  267.9 16.4 %collective-permute-start.21 = (bf16[2,48,768]{2,1,0:T(8,128)(2,1)S(1)}, bf16[2,48,768]{2,1,0:T(8,128)(2,1)S(1)}, u32[]{:S(2)}, u32[]{:S(2)}) collective-permute-start(bf16[2,48,768]{2,1,0:T(8,128)(2,1)S(1)} %fusion.15), channel_id=1, source_target_pairs={{0,1},{1,0},{2,3},{3,2},{4,5},{5,4},{6,7},{7,6},{8,9},{9,8},{10,11... | collective-permute-start | bytes 442376 | tf_op jit(solution)/shard_map/ppermute | solution.py:685
  269.1 18.5 %collective-permute-start.27 = (bf16[2,2,48,1696]{3,2,1,0:T(8,128)(2,1)}, bf16[2,2,48,1696]{3,2,1,0:T(8,128)(2,1)}, u32[]{:S(2)}, u32[]{:S(2)}) collective-permute-start(bf16[2,2,48,1696]{3,2,1,0:T(8,128)(2,1)} %get-tuple-element.86), channel_id=1, source_target_pairs={{0,4},{4,0},{1,5},{5,1},{2,6},{6,2},{3,7},{7,3},{8,12},{12,8},{9,1... | collective-permute-start | bytes 1953800 | tf_op jit(solution)/shard_map/ppermute | solution.py:685
  272.7 19.2 %collective-permute-start.30 = (bf16[2,2,48,1696]{3,2,1,0:T(8,128)(2,1)}, bf16[2,2,48,1696]{3,2,1,0:T(8,128)(2,1)}, u32[]{:S(2)}, u32[]{:S(2)}) collective-permute-start(bf16[2,2,48,1696]{3,2,1,0:T(8,128)(2,1)} %get-tuple-element.88), channel_id=1, source_target_pairs={{0,1},{1,0},{2,3},{3,2},{4,5},{5,4},{6,7},{7,6},{8,9},{9,8},{10,11... | collective-permute-start | bytes 1953800 | tf_op jit(solution)/shard_map/ppermute | solution.py:685
  282.2 23.7 %collective-permute-start.25 = (bf16[48,768]{1,0:T(8,128)(2,1)}, bf16[48,768]{1,0:T(8,128)(2,1)S(1)}, u32[]{:S(2)}, u32[]{:S(2)}) collective-permute-start(bf16[48,768]{1,0:T(8,128)(2,1)} %get-tuple-element.200), channel_id=1, source_target_pairs={{0,16},{8,24},{16,0},{24,8},{1,17},{9,25},{17,1},{25,9},{2,18},{10... | collective-permute-start | bytes 221192 | tf_op jit(solution)/shard_map/ppermute | solution.py:747
  284.3 25.8 %collective-permute-start.26 = (bf16[48,768]{1,0:T(8,128)(2,1)}, bf16[48,768]{1,0:T(8,128)(2,1)}, u32[]{:S(2)}, u32[]{:S(2)}) collective-permute-start(bf16[48,768]{1,0:T(8,128)(2,1)} %get-tuple-element.201), channel_id=1, source_target_pairs={{0,24},{8,0},{16,8},{24,16},{1,25},{9,1},{17,9},{25,17},{2,26},{10... | collective-permute-start | bytes 221192 | tf_op jit(solution)/shard_map/ppermute | solution.py:747
  285.6 24.5 %collective-permute-start.22 = (bf16[48,768]{1,0:T(8,128)(2,1)S(1)}, bf16[48,768]{1,0:T(8,128)(2,1)}, u32[]{:S(2)}, u32[]{:S(2)}) collective-permute-start(bf16[48,768]{1,0:T(8,128)(2,1)S(1)} %fusion.21), channel_id=1, source_target_pairs={{0,8},{8,16},{16,24},{24,0},{1,9},{9,17},{17,25},{25,1},{2,10},{10... | collective-permute-start | bytes 221192 | tf_op jit(solution)/shard_map/ppermute | solution.py:747
  287.6 3.4 collective-permute-start.16
  291.0 20.2 %collective-permute-start.28 = (bf16[2,48,1696]{2,1,0:T(8,128)(2,1)}, bf16[2,48,1696]{2,1,0:T(8,128)(2,1)}, u32[]{:S(2)}, u32[]{:S(2)}) collective-permute-start(bf16[2,48,1696]{2,1,0:T(8,128)(2,1)} %fusion.12), channel_id=1, source_target_pairs={{0,1},{1,0},{2,3},{3,2},{4,5},{5,4},{6,7},{7,6},{8,9},{9,8},{10,11... | collective-permute-start | bytes 976904 | tf_op jit(solution)/shard_map/ppermute | solution.py:685
  291.9 2.8 collective-permute-start.17
  294.7 10.0 %collective-permute-start.18 = (f32[8,896]{1,0:T(8,128)S(1)}, f32[8,896]{1,0:T(8,128)S(1)}, u32[]{:S(2)}, u32[]{:S(2)}) collective-permute-start(f32[8,896]{1,0:T(8,128)S(1)} %add.136), channel_id=1, source_target_pairs={{0,16},{8,24},{16,0},{24,8},{1,17},{9,25},{17,1},{25,9},{2,18},{10... | collective-permute-start | bytes 86024 | tf_op jit(solution)/shard_map/ppermute | solution.py:897
  298.0 40.9 %all-to-all-start.3 = ((bf16[16,64,768]{2,1,0:T(8,128)(2,1)}), bf16[16,64,768]{2,1,0:T(8,128)(2,1)S(1)}, u32[]{:S(2)}, u32[]{:S(2)}) async-start(bf16[16,64,768]{2,1,0:T(8,128)(2,1)} %shard_map.279), calls=%async_computation.3 | async-start | bytes 3145728 | tf_op jit(solution)/shard_map/all_to_all | solution.py:885
  304.7 9.5 %collective-permute-start.31 = (bf16[2,48,1696]{2,1,0:T(8,128)(2,1)}, bf16[2,48,1696]{2,1,0:T(8,128)(2,1)}, u32[]{:S(2)}, u32[]{:S(2)}) collective-permute-start(bf16[2,48,1696]{2,1,0:T(8,128)(2,1)} %fusion.13), channel_id=1, source_target_pairs={{0,4},{4,0},{1,5},{5,1},{2,6},{6,2},{3,7},{7,3},{8,12},{12,8},{9,1... | collective-permute-start | bytes 976904 | tf_op jit(solution)/shard_map/ppermute | solution.py:685
  306.0 5.2 %collective-permute-start.19 = (f32[8,896]{1,0:T(8,128)S(1)}, f32[8,896]{1,0:T(8,128)S(1)}, u32[]{:S(2)}, u32[]{:S(2)}) collective-permute-start(f32[8,896]{1,0:T(8,128)S(1)} %add.137), channel_id=1, source_target_pairs={{0,2},{2,0},{1,3},{3,1},{4,6},{6,4},{5,7},{7,5},{8,10},{10,8},{9,1... | collective-permute-start | bytes 86024 | tf_op jit(solution)/shard_map/ppermute | solution.py:685
  316.3 25.3 %copy-start.10 = (f32[2,48,1696]{2,1,0:T(8,128)S(1)}, f32[2,48,1696]{2,1,0:T(8,128)}, u32[]{:S(2)}) copy-start(f32[2,48,1696]{2,1,0:T(8,128)} %copy-done.9) | copy-start | bytes 1953796
  340.1 4.5 %collective-permute-start.29 = (bf16[48,1696]{1,0:T(8,128)(2,1)}, bf16[48,1696]{1,0:T(8,128)(2,1)S(1)}, u32[]{:S(2)}, u32[]{:S(2)}) collective-permute-start(bf16[48,1696]{1,0:T(8,128)(2,1)} %shard_map.287), channel_id=1, source_target_pairs={{0,8},{8,16},{16,24},{24,0},{1,9},{9,17},{17,25},{25,1},{2,10},{10... | collective-permute-start | bytes 488456 | tf_op jit(solution)/shard_map/ppermute | solution.py:747
  340.1 8.1 %collective-permute-start.32 = (bf16[48,1696]{1,0:T(8,128)(2,1)}, bf16[48,1696]{1,0:T(8,128)(2,1)}, u32[]{:S(2)}, u32[]{:S(2)}) collective-permute-start(bf16[48,1696]{1,0:T(8,128)(2,1)} %shard_map.289), channel_id=1, source_target_pairs={{0,16},{8,24},{16,0},{24,8},{1,17},{9,25},{17,1},{25,9},{2,18},{10... | collective-permute-start | bytes 488456 | tf_op jit(solution)/shard_map/ppermute | solution.py:747
  341.2 32.6 %copy-start.5 = (bf16[16,64,768]{2,1,0:T(8,128)(2,1)S(1)}, bf16[16,64,768]{2,1,0:T(8,128)(2,1)}, u32[]{:S(2)}) copy-start(bf16[16,64,768]{2,1,0:T(8,128)(2,1)} %copy-done.4) | copy-start | bytes 4718596
  341.2 15.9 %collective-permute-start.33 = (bf16[48,1696]{1,0:T(8,128)(2,1)}, bf16[48,1696]{1,0:T(8,128)(2,1)}, u32[]{:S(2)}, u32[]{:S(2)}) collective-permute-start(bf16[48,1696]{1,0:T(8,128)(2,1)} %shard_map.290), channel_id=1, source_target_pairs={{0,24},{8,0},{16,8},{24,16},{1,25},{9,1},{17,9},{25,17},{2,26},{10... | collective-permute-start | bytes 488456 | tf_op jit(solution)/shard_map/ppermute | solution.py:747
  342.3 32.7 %copy-start.1 = (bf16[16,64,768]{2,1,0:T(8,128)(2,1)S(1)}, bf16[16,64,768]{2,1,0:T(8,128)(2,1)}, u32[]{:S(2)}) copy-start(bf16[16,64,768]{2,1,0:T(8,128)(2,1)} %copy-done) | copy-start | bytes 4718596
  359.2 1.7 collective-permute-start.34
  362.3 7.7 %collective-permute-start.35 = (bf16[48,2464]{1,0:T(8,128)(2,1)}, bf16[48,2464]{1,0:T(8,128)(2,1)S(1)}, u32[]{:S(2)}, u32[]{:S(2)}) collective-permute-start(bf16[48,2464]{1,0:T(8,128)(2,1)} %pad_maximum_fusion.2), channel_id=1, source_target_pairs={{0,0},{1,2},{2,1},{3,3},{4,4},{5,6},{6,5},{7,7},{8,8},{9,10},{10,9... | collective-permute-start | bytes 709640 | tf_op jit(solution)/shard_map/ppermute | solution.py:689
  (36 other events, 125.7 us)
